TPU v7x, 32 devices: a whole 2x2x4 slice. The times are simulated.
32 devices in a mesh: section: 2 (over y), dp: 4 (over x, core), tensor: 4 (over z).
Axes of the slice: x: 2, y: 2, z: 4, core: 2. Of those that a mesh axis runs over, the one named last changes fastest.
Arguments:
- tokens: bfloat16 [8, 1024, 1024], P('dp', 'tensor'), may hold values from -6 to 6
- lengths: int32 [8], P('dp'), may hold values from 128 to 1024, as said below
- qkv_weight: bfloat16 [2, 3, 1024, 1024], P('section', None, None, 'tensor'), may hold values from -0.1875 to 0.1875
- out_weight: bfloat16 [2, 1024, 1024], P('section', 'tensor'), may hold values from -0.75 to 0.75
- gate_up_weight: bfloat16 [2, 2, 1024, 2816], P('section', None, None, 'tensor'), may hold values from -0.1875 to 0.1875
- down_weight: bfloat16 [2, 2816, 1024], P('section', 'tensor'), may hold values from -0.109375 to 0.109375
- norm_gains: float32 [2, 2, 1024], P('section'), may hold values from 0.5 to 1.5
- cotangent: bfloat16 [8, 1024, 1024], P('dp', 'tensor'), may hold values from -6 to 6
Outputs:
- layer_outs: bfloat16 [2, 8, 1024, 1024], P('section', 'dp', 'tensor')
- input_grads: float32 [2, 8, 1024, 1024], P('section', 'dp', 'tensor')
- qkv_grad: float32 [2, 3, 1024, 1024], P('section', None, 'dp', 'tensor')
- out_grad: float32 [2, 1024, 1024], P('section', 'tensor', 'dp')
- gate_up_grad: float32 [2, 2, 1024, 2816], P('section', None, 'dp', 'tensor')
- down_grad: float32 [2, 2816, 1024], P('section', 'tensor', 'dp')
- gain_grad: float32 [2, 2, 1024], P('section', None, ('dp', 'tensor'))
Inputs may be any that keep to these rules, and one draw needn't show every extreme that they name: Positions from lengths[s] on are padding. Some sequence has all 1024 tokens.
All inputs are finite; a program needn't handle non-finite values.
Results may differ from a plain program's by a relative error of at most 0.03.
Values may be sent and summed in bfloat16 or wider, within the bound.
A program may use at most 256 MiB of HBM per device.

v0:
```python
import jax
import jax.numpy as jnp
from jax import lax
from jax.sharding import PartitionSpec as P

D = 1024
HD = 64


NORM_EPS = 1e-06
ROPE_BASE = 10000.0
SCORE_SCALE = 0.125
MASK_VALUE = -1e30


def from_behind(value, axis, steps):
    count = lax.axis_size(axis)
    leading, last = (max(0, -steps), min(count, count - steps))
    return lax.ppermute(value, axis, [(source, source + steps) for source in range(leading, last)])


def rms_norm(values, gain):
    return values * lax.rsqrt(jnp.mean(values * values, axis=-1, keepdims=True) + NORM_EPS) * gain


def rope_tables(positions_count):
    positions = jnp.arange(positions_count, dtype=jnp.float32)
    frequency = ROPE_BASE ** (-jnp.arange(HD // 2, dtype=jnp.float32) * 2.0 / HD)
    angles = positions[:, None] * frequency[None, :]
    return (jnp.cos(angles), jnp.sin(angles))


def rotate(values, cos_table, sine_table):
    first_half = values[..., : HD // 2]
    second_half = values[..., HD // 2 :]
    cos_part = cos_table[:, None, :]
    sin_part = sine_table[:, None, :]
    return jnp.concatenate(
        [
            first_half * cos_part - second_half * sin_part,
            first_half * sin_part + second_half * cos_part,
        ],
        axis=-1,
    )


def score_block(query_rot, key_rot, length):
    seq_len = query_rot.shape[0]
    raw_scores = (
        jnp.einsum("qhd,khd->hqk", query_rot, key_rot, preferred_element_type=jnp.float32)
        * SCORE_SCALE
    )
    row_index = jnp.arange(seq_len)[:, None]
    col_index = jnp.arange(seq_len)[None, :]
    is_valid = (col_index <= row_index) & (col_index < length)
    return jnp.where(is_valid[None], raw_scores, MASK_VALUE)


def forward_layer(layer_weights, layer_in, first_values, length, blend_share, tables):
    w_qkv, w_out, w_gate_up, w_down, gain_pair = layer_weights
    cos_table, sine_table = tables
    resid_in = layer_in.astype(jnp.float32)
    normed = rms_norm(resid_in, gain_pair[0]).astype(jnp.bfloat16)
    rows_full = lax.all_gather(normed, "tensor", axis=0, tiled=True)
    seq_len = rows_full.shape[0]
    projected = jnp.einsum("sd,cde->cse", rows_full, w_qkv, preferred_element_type=jnp.float32)
    head_count = projected.shape[2] // HD
    query_rot = rotate(projected[0].reshape(seq_len, head_count, HD), cos_table, sine_table).astype(
        jnp.bfloat16
    )
    key_rot = rotate(projected[1].reshape(seq_len, head_count, HD), cos_table, sine_table).astype(
        jnp.bfloat16
    )
    own_values = projected[2].astype(jnp.bfloat16)
    used_values = (
        blend_share * own_values.astype(jnp.float32)
        + (1.0 - blend_share) * first_values.astype(jnp.float32)
    ).astype(jnp.bfloat16)
    scores = score_block(query_rot, key_rot, length)
    row_top = jnp.max(scores, axis=-1, keepdims=True)
    expd = jnp.exp(scores - row_top)
    row_total = jnp.sum(expd, axis=-1, keepdims=True)
    attn_probs = (expd / row_total).astype(jnp.bfloat16)
    log_total = (row_top + jnp.log(row_total))[..., 0]
    attended = (
        jnp.einsum(
            "hqk,khd->qhd",
            attn_probs,
            used_values.reshape(seq_len, head_count, HD),
            preferred_element_type=jnp.float32,
        )
        .reshape(seq_len, -1)
        .astype(jnp.bfloat16)
    )
    piece = attended
    hidden_res = resid_in + lax.psum_scatter(
        jnp.dot(piece, w_out, preferred_element_type=jnp.float32).astype(jnp.bfloat16),
        "tensor",
        scatter_dimension=0,
        tiled=True,
    ).astype(jnp.float32)
    mixed_in = rms_norm(hidden_res, gain_pair[1]).astype(jnp.bfloat16)
    mixed_full = lax.all_gather(mixed_in, "tensor", axis=0, tiled=True)
    gate_up = jnp.einsum("sd,cdf->csf", mixed_full, w_gate_up, preferred_element_type=jnp.float32)
    activ = (jax.nn.silu(gate_up[0]) * gate_up[1]).astype(jnp.bfloat16)
    piece = activ
    result = hidden_res + lax.psum_scatter(
        jnp.dot(piece, w_down, preferred_element_type=jnp.float32).astype(jnp.bfloat16),
        "tensor",
        scatter_dimension=0,
        tiled=True,
    ).astype(jnp.float32)
    kept = (
        resid_in,
        rows_full,
        query_rot,
        key_rot,
        used_values,
        log_total,
        attended,
        hidden_res,
        mixed_full,
        gate_up,
        activ,
    )
    return (result.astype(jnp.bfloat16), own_values, kept)


def backward_layer(
    layer_weights, layer_in, first_values, length, blend_share, tables, grad_out, grad_first
):
    w_qkv, w_out, w_gate_up, w_down, gain_pair = layer_weights
    cos_table, sine_table = tables
    unused_out, unused_values, kept = forward_layer(
        layer_weights, layer_in, first_values, length, blend_share, tables
    )
    (
        resid_in,
        rows_full,
        query_rot,
        key_rot,
        used_values,
        log_total,
        attended,
        hidden_res,
        mixed_full,
        gate_up,
        activ,
    ) = kept
    seq_len = rows_full.shape[0]
    head_count = query_rot.shape[1]
    out_full = lax.all_gather(grad_out.astype(jnp.bfloat16), "tensor", axis=0, tiled=True)
    grad_activ = jnp.einsum("sd,fd->sf", out_full, w_down, preferred_element_type=jnp.float32)
    grad_down = jnp.einsum("sf,sd->fd", activ, out_full, preferred_element_type=jnp.float32)
    unused_swiglu, swiglu_back = jax.vjp(
        lambda gate_in, up_in: jax.nn.silu(gate_in) * up_in, gate_up[0], gate_up[1]
    )
    grad_gate, grad_up = swiglu_back(grad_activ)
    grad_gate_up = jnp.stack([grad_gate, grad_up]).astype(jnp.bfloat16)
    grad_w_gate_up = jnp.einsum(
        "sd,csf->cdf", mixed_full, grad_gate_up, preferred_element_type=jnp.float32
    )
    piece = grad_gate_up
    grad_mixed = lax.psum_scatter(
        jnp.einsum("csf,cdf->sd", piece, w_gate_up, preferred_element_type=jnp.float32).astype(
            jnp.bfloat16
        ),
        "tensor",
        scatter_dimension=0,
        tiled=True,
    ).astype(jnp.float32)
    unused_norm, second_norm_back = jax.vjp(rms_norm, hidden_res, gain_pair[1])
    grad_hnorm, grad_gain_two = second_norm_back(grad_mixed)
    grad_hidden = grad_out + grad_hnorm
    attn_full = lax.all_gather(grad_hidden.astype(jnp.bfloat16), "tensor", axis=0, tiled=True)
    grad_w_out = jnp.einsum("se,sd->ed", attended, attn_full, preferred_element_type=jnp.float32)
    grad_attended = jnp.einsum("sd,ed->se", attn_full, w_out, preferred_element_type=jnp.float32)
    grad_attended = grad_attended.astype(jnp.bfloat16).reshape(seq_len, head_count, HD)
    scores = score_block(query_rot, key_rot, length)
    attn_probs = jnp.exp(scores - log_total[..., None])
    value_heads = used_values.reshape(seq_len, head_count, HD)
    grad_probs = jnp.einsum(
        "qhd,khd->hqk", grad_attended, value_heads, preferred_element_type=jnp.float32
    )
    row_delta = jnp.sum(grad_probs * attn_probs, axis=-1, keepdims=True)
    grad_scores = (attn_probs * (grad_probs - row_delta)).astype(jnp.bfloat16)
    grad_used = jnp.einsum(
        "hqk,qhd->khd",
        attn_probs.astype(jnp.bfloat16),
        grad_attended,
        preferred_element_type=jnp.float32,
    ).reshape(seq_len, -1)
    grad_query_rot = (
        jnp.einsum("hqk,khd->qhd", grad_scores, key_rot, preferred_element_type=jnp.float32)
        * SCORE_SCALE
    )
    grad_key_rot = (
        jnp.einsum("hqk,qhd->khd", grad_scores, query_rot, preferred_element_type=jnp.float32)
        * SCORE_SCALE
    )
    unused_rot, rotate_back = jax.vjp(
        lambda heads_in: rotate(heads_in, cos_table, sine_table), jnp.zeros_like(grad_query_rot)
    )
    grad_query = rotate_back(grad_query_rot)[0].reshape(seq_len, -1).astype(jnp.bfloat16)
    grad_key = rotate_back(grad_key_rot)[0].reshape(seq_len, -1).astype(jnp.bfloat16)
    grad_value = (blend_share * grad_used + grad_first.astype(jnp.float32)).astype(jnp.bfloat16)
    grad_first_out = ((1.0 - blend_share) * grad_used).astype(jnp.bfloat16)
    grad_projected = jnp.stack([grad_query, grad_key, grad_value])
    grad_w_qkv = jnp.einsum(
        "sd,cse->cde", rows_full, grad_projected, preferred_element_type=jnp.float32
    )
    piece = grad_projected
    grad_normed = lax.psum_scatter(
        jnp.einsum("cse,cde->sd", piece, w_qkv, preferred_element_type=jnp.float32).astype(
            jnp.bfloat16
        ),
        "tensor",
        scatter_dimension=0,
        tiled=True,
    ).astype(jnp.float32)
    unused_first, first_norm_back = jax.vjp(rms_norm, resid_in, gain_pair[0])
    grad_resid, grad_gain_one = first_norm_back(grad_normed)
    grad_in = grad_hidden + grad_resid
    grads = (
        grad_w_qkv,
        grad_w_out,
        grad_w_gate_up,
        grad_down,
        jnp.stack([grad_gain_one, grad_gain_two]),
    )
    return (grad_in, grad_first_out, grads)


def store_slot(buffer, new_value, mb_slot, is_valid):
    updated = lax.dynamic_update_index_in_dim(buffer, new_value, mb_slot, 0)
    return jnp.where(is_valid, updated, buffer)


def shards(
    tokens, lengths, qkv_weight, out_weight, gate_up_weight, down_weight, norm_gains, cotangent
):
    section_rank = lax.axis_index("section")
    is_first = section_rank == 0
    blend_share = jnp.where(is_first, 1.0, 0.5).astype(jnp.float32)
    mb_count = tokens.shape[0]
    row_share = tokens.shape[1]
    tensor_rank = lax.axis_index("tensor")
    seq_len = row_share * lax.axis_size("tensor")
    layer_weights = (qkv_weight[0], out_weight[0], gate_up_weight[0], down_weight[0], norm_gains[0])
    tables = rope_tables(seq_len)
    heads_width = qkv_weight.shape[3]
    recv_rows = jnp.zeros((row_share, D), jnp.bfloat16)
    recv_values = jnp.zeros((seq_len, heads_width), jnp.bfloat16)
    layer_result = jnp.zeros((mb_count, row_share, D), jnp.bfloat16)
    kept_inputs = jnp.zeros((mb_count, row_share, D), jnp.bfloat16)
    kept_values = jnp.zeros((mb_count, seq_len, heads_width), jnp.bfloat16)
    for loop_step in range(mb_count + 1):
        slot_raw = loop_step - section_rank
        is_valid = (slot_raw >= 0) & (slot_raw < mb_count)
        mb_slot = jnp.clip(slot_raw, 0, mb_count - 1)
        layer_in = jnp.where(is_first, tokens[min(loop_step, mb_count - 1)], recv_rows)
        length = lengths[mb_slot]
        result, own_values, step_kept = forward_layer(
            layer_weights, layer_in, recv_values, length, blend_share, tables
        )
        kept_inputs = store_slot(kept_inputs, layer_in, mb_slot, is_valid)
        kept_values = store_slot(kept_values, recv_values, mb_slot, is_valid)
        layer_result = store_slot(layer_result, result, mb_slot, is_valid)
        if loop_step < mb_count:
            recv_rows, recv_values = from_behind((result, own_values), "section", 1)
    row_index = tensor_rank * row_share + jnp.arange(row_share)
    recv_grad = jnp.zeros((row_share, D), jnp.bfloat16)
    recv_grad_values = jnp.zeros((seq_len, heads_width), jnp.bfloat16)
    input_grads = jnp.zeros((mb_count, row_share, D), jnp.float32)
    grad_sums = None
    gain_sums = jnp.zeros((2, D), jnp.float32)
    for loop_step in range(mb_count + 1):
        slot_raw = mb_count - loop_step - section_rank
        is_valid = (slot_raw >= 0) & (slot_raw < mb_count)
        mb_slot = jnp.clip(slot_raw, 0, mb_count - 1)
        length = lengths[mb_slot]
        row_mask = (row_index < length).astype(jnp.float32)
        cot_rows = cotangent[mb_slot].astype(jnp.float32) * row_mask[:, None]
        grad_out = jnp.where(is_first, recv_grad.astype(jnp.float32), cot_rows)
        grad_in, grad_first_out, grads = backward_layer(
            layer_weights,
            kept_inputs[mb_slot],
            kept_values[mb_slot],
            length,
            blend_share,
            tables,
            grad_out,
            recv_grad_values,
        )
        step_scale = is_valid.astype(jnp.float32)
        grads = tuple((term * step_scale for term in grads))
        gain_sums = gain_sums + grads[4]
        grad_sums = (
            grads[:4]
            if grad_sums is None
            else tuple(
                (total_term + new_term for total_term, new_term in zip(grad_sums, grads[:4]))
            )
        )
        input_grads = store_slot(input_grads, grad_in, mb_slot, is_valid)
        if loop_step < mb_count:
            recv_grad, recv_grad_values = from_behind(
                (grad_in.astype(jnp.bfloat16), grad_first_out), "section", -1
            )
    weight_shares = (
        lax.psum_scatter(
            grad_sums[0].astype(jnp.bfloat16), "dp", scatter_dimension=1, tiled=True
        ).astype(jnp.float32),
        lax.psum_scatter(
            grad_sums[1].astype(jnp.bfloat16), "dp", scatter_dimension=1, tiled=True
        ).astype(jnp.float32),
        lax.psum_scatter(
            grad_sums[2].astype(jnp.bfloat16), "dp", scatter_dimension=1, tiled=True
        ).astype(jnp.float32),
        lax.psum_scatter(
            grad_sums[3].astype(jnp.bfloat16), "dp", scatter_dimension=1, tiled=True
        ).astype(jnp.float32),
    )
    gain_share = lax.psum_scatter(gain_sums, ("dp", "tensor"), scatter_dimension=1, tiled=True)
    return (
        layer_result[None],
        input_grads[None],
        weight_shares[0][None],
        weight_shares[1][None],
        weight_shares[2][None],
        weight_shares[3][None],
        gain_share[None],
    )


def solution(mesh):
    in_specs = (
        P("dp", "tensor", None),
        P("dp"),
        P("section", None, None, "tensor"),
        P("section", "tensor", None),
        P("section", None, None, "tensor"),
        P("section", "tensor", None),
        P("section", None, None),
        P("dp", "tensor", None),
    )
    out_specs = (
        P("section", "dp", "tensor", None),
        P("section", "dp", "tensor", None),
        P("section", None, "dp", "tensor"),
        P("section", "tensor", "dp"),
        P("section", None, "dp", "tensor"),
        P("section", "tensor", "dp"),
        P("section", None, ("dp", "tensor")),
    )
    return jax.shard_map(shards, mesh=mesh, in_specs=in_specs, out_specs=out_specs, check_vma=False)
```

profile of v0, /device:TPU:0, one launch (start us, length us, event | category | flops | bytes accessed | tf_op | source)
XLA Modules:
  0.0 2017.2 jit_solution(11205156004740845487)
XLA Ops:
  15.5 44.8 %all-gather.19.cloned.1.call-done = bf16[1024,1024]{1,0:T(8,128)(2,1)} async-done(((bf16[256,1024]{1,0:T(8,128)(2,1)}), bf16[1024,1024]{1,0:T(8,128)(2,1)}) %all-gather.19.cloned.1.call-update) | async-done | bytes 2097168 | tf_op jit(solution)/shard_map/all_gather | solution.py:64
  88.7 42.7 %reduce-scatter.23.cloned.1.call-done = bf16[256,1024]{1,0:T(8,128)(2,1)} async-done(((bf16[1024,1024]{1,0:T(8,128)(2,1)}), bf16[256,1024]{1,0:T(8,128)(2,1)}) %reduce-scatter.23.cloned.1.call-update) | async-done | bytes 524304 | tf_op jit(solution)/shard_map/reduce_scatter | solution.py:96
  135.5 45.1 %all-gather.21.cloned.1.call-done = bf16[1024,1024]{1,0:T(8,128)(2,1)} async-done(((bf16[256,1024]{1,0:T(8,128)(2,1)}), bf16[1024,1024]{1,0:T(8,128)(2,1)}) %all-gather.21.cloned.1.call-update) | async-done | bytes 2097168 | tf_op jit(solution)/shard_map/all_gather | solution.py:103
  188.9 42.7 %reduce-scatter.25.cloned.1.call-done = bf16[256,1024]{1,0:T(8,128)(2,1)} async-done(((bf16[1024,1024]{1,0:T(8,128)(2,1)}), bf16[256,1024]{1,0:T(8,128)(2,1)}) %reduce-scatter.25.cloned.1.call-update) | async-done | bytes 524304 | tf_op jit(solution)/shard_map/reduce_scatter | solution.py:107
  263.1 37.2 %all-gather.23.cloned.1.call-done = bf16[1024,1024]{1,0:T(8,128)(2,1)} async-done(((bf16[256,1024]{1,0:T(8,128)(2,1)}), bf16[1024,1024]{1,0:T(8,128)(2,1)}) %all-gather.23.cloned.1.call-update) | async-done | bytes 2097168 | tf_op jit(solution)/shard_map/all_gather | solution.py:64
  330.7 42.6 %reduce-scatter.27.cloned.1.call-done = bf16[256,1024]{1,0:T(8,128)(2,1)} async-done(((bf16[1024,1024]{1,0:T(8,128)(2,1)}), bf16[256,1024]{1,0:T(8,128)(2,1)}) %reduce-scatter.27.cloned.1.call-update) | async-done | bytes 524304 | tf_op jit(solution)/shard_map/reduce_scatter | solution.py:96
  377.1 44.9 %all-gather.25.cloned.1.call-done = bf16[1024,1024]{1,0:T(8,128)(2,1)} async-done(((bf16[256,1024]{1,0:T(8,128)(2,1)}), bf16[1024,1024]{1,0:T(8,128)(2,1)}) %all-gather.25.cloned.1.call-update) | async-done | bytes 2097168 | tf_op jit(solution)/shard_map/all_gather | solution.py:103
  430.3 42.7 %reduce-scatter.29.cloned.1.call-done = bf16[256,1024]{1,0:T(8,128)(2,1)} async-done(((bf16[1024,1024]{1,0:T(8,128)(2,1)}), bf16[256,1024]{1,0:T(8,128)(2,1)}) %reduce-scatter.29.cloned.1.call-update) | async-done | bytes 524304 | tf_op jit(solution)/shard_map/reduce_scatter | solution.py:107
  518.3 26.6 %all-gather.33.cloned.1.call-done = bf16[1024,1024]{1,0:T(8,128)(2,1)} async-done(((bf16[256,1024]{1,0:T(8,128)(2,1)}), bf16[1024,1024]{1,0:T(8,128)(2,1)}) %all-gather.33.cloned.1.call-update) | async-done | bytes 2097168 | tf_op jit(solution)/shard_map/all_gather | solution.py:64
  578.2 42.7 %reduce-scatter.35.cloned.1.call-done = bf16[256,1024]{1,0:T(8,128)(2,1)} async-done(((bf16[1024,1024]{1,0:T(8,128)(2,1)}), bf16[256,1024]{1,0:T(8,128)(2,1)}) %reduce-scatter.35.cloned.1.call-update) | async-done | bytes 524304 | tf_op jit(solution)/shard_map/reduce_scatter | solution.py:96
  628.2 41.8 %all-gather.35.cloned.1.call-done = bf16[1024,1024]{1,0:T(8,128)(2,1)} async-done(((bf16[256,1024]{1,0:T(8,128)(2,1)}), bf16[1024,1024]{1,0:T(8,128)(2,1)}) %all-gather.35.cloned.1.call-update) | async-done | bytes 2097168 | tf_op jit(solution)/shard_map/all_gather | solution.py:103
  676.5 39.6 %all-gather.31.cloned.1.call-done = bf16[1024,1024]{1,0:T(8,128)(2,1)} async-done(((bf16[256,1024]{1,0:T(8,128)(2,1)}), bf16[1024,1024]{1,0:T(8,128)(2,1)}) %all-gather.31.cloned.1.call-update) | async-done | bytes 2097168 | tf_op jit(solution)/shard_map/all_gather | solution.py:152
  728.9 42.7 %reduce-scatter.37.cloned.1.call-done = bf16[256,1024]{1,0:T(8,128)(2,1)} async-done(((bf16[1024,1024]{1,0:T(8,128)(2,1)}), bf16[256,1024]{1,0:T(8,128)(2,1)}) %reduce-scatter.37.cloned.1.call-update) | async-done | bytes 524304 | tf_op jit(solution)/shard_map/reduce_scatter | solution.py:164
  780.5 43.9 %all-gather.37.cloned.1.call-done = bf16[1024,1024]{1,0:T(8,128)(2,1)} async-done(((bf16[256,1024]{1,0:T(8,128)(2,1)}), bf16[1024,1024]{1,0:T(8,128)(2,1)}) %all-gather.37.cloned.1.call-update) | async-done | bytes 2097168 | tf_op jit(solution)/shard_map/all_gather | solution.py:175
  933.1 46.0 %reduce-scatter.41.cloned.1.call-done = bf16[256,1024]{1,0:T(8,128)(2,1)} async-done(((bf16[1024,1024]{1,0:T(8,128)(2,1)}), bf16[256,1024]{1,0:T(8,128)(2,1)}) %reduce-scatter.41.cloned.1.call-update) | async-done | bytes 524304 | tf_op jit(solution)/shard_map/reduce_scatter | solution.py:96
  1004.8 26.6 %all-gather.43.cloned.1.call-done = bf16[1024,1024]{1,0:T(8,128)(2,1)} async-done(((bf16[256,1024]{1,0:T(8,128)(2,1)}), bf16[1024,1024]{1,0:T(8,128)(2,1)}) %all-gather.43.cloned.1.call-update) | async-done | bytes 2097168 | tf_op jit(solution)/shard_map/all_gather | solution.py:103
  1038.0 40.2 %all-gather.39.cloned.1.call-done = bf16[1024,1024]{1,0:T(8,128)(2,1)} async-done(((bf16[256,1024]{1,0:T(8,128)(2,1)}), bf16[1024,1024]{1,0:T(8,128)(2,1)}) %all-gather.39.cloned.1.call-update) | async-done | bytes 2097168 | tf_op jit(solution)/shard_map/all_gather | solution.py:152
  1090.8 42.7 %reduce-scatter.43.cloned.1.call-done = bf16[256,1024]{1,0:T(8,128)(2,1)} async-done(((bf16[1024,1024]{1,0:T(8,128)(2,1)}), bf16[256,1024]{1,0:T(8,128)(2,1)}) %reduce-scatter.43.cloned.1.call-update) | async-done | bytes 524304 | tf_op jit(solution)/shard_map/reduce_scatter | solution.py:164
  1145.4 40.7 %all-gather.45.cloned.1.call-done = bf16[1024,1024]{1,0:T(8,128)(2,1)} async-done(((bf16[256,1024]{1,0:T(8,128)(2,1)}), bf16[1024,1024]{1,0:T(8,128)(2,1)}) %all-gather.45.cloned.1.call-update) | async-done | bytes 2097168 | tf_op jit(solution)/shard_map/all_gather | solution.py:175
  1298.0 45.9 %reduce-scatter.47.cloned.1.call-done = bf16[256,1024]{1,0:T(8,128)(2,1)} async-done(((bf16[1024,1024]{1,0:T(8,128)(2,1)}), bf16[256,1024]{1,0:T(8,128)(2,1)}) %reduce-scatter.47.cloned.1.call-update) | async-done | bytes 524304 | tf_op jit(solution)/shard_map/reduce_scatter | solution.py:96
  1369.4 26.8 %all-gather.51.cloned.1.call-done = bf16[1024,1024]{1,0:T(8,128)(2,1)} async-done(((bf16[256,1024]{1,0:T(8,128)(2,1)}), bf16[1024,1024]{1,0:T(8,128)(2,1)}) %all-gather.51.cloned.1.call-update) | async-done | bytes 2097168 | tf_op jit(solution)/shard_map/all_gather | solution.py:103
  1402.7 40.2 %all-gather.47.cloned.1.call-done = bf16[1024,1024]{1,0:T(8,128)(2,1)} async-done(((bf16[256,1024]{1,0:T(8,128)(2,1)}), bf16[1024,1024]{1,0:T(8,128)(2,1)}) %all-gather.47.cloned.1.call-update) | async-done | bytes 2097168 | tf_op jit(solution)/shard_map/all_gather | solution.py:152
  1456.3 41.9 %reduce-scatter.49.cloned.1.call-done = bf16[256,1024]{1,0:T(8,128)(2,1)} async-done(((bf16[1024,1024]{1,0:T(8,128)(2,1)}), bf16[256,1024]{1,0:T(8,128)(2,1)}) %reduce-scatter.49.cloned.1.call-update) | async-done | bytes 524304 | tf_op jit(solution)/shard_map/reduce_scatter | solution.py:164
  1503.5 41.5 %all-gather.27.cloned.1.call-done = bf16[1024,1024]{1,0:T(8,128)(2,1)} async-done(((bf16[256,1024]{1,0:T(8,128)(2,1)}), bf16[1024,1024]{1,0:T(8,128)(2,1)}) %all-gather.27.cloned.1.call-update) | async-done | bytes 2097168 | tf_op jit(solution)/shard_map/all_gather | solution.py:64
  1552.1 39.2 %all-gather.53.cloned.1.call-done = bf16[1024,1024]{1,0:T(8,128)(2,1)} async-done(((bf16[256,1024]{1,0:T(8,128)(2,1)}), bf16[1024,1024]{1,0:T(8,128)(2,1)}) %all-gather.53.cloned.1.call-update) | async-done | bytes 2097168 | tf_op jit(solution)/shard_map/all_gather | solution.py:175
  1672.3 14.9 reduce-scatter.31.cloned.1.call-done
  1738.2 41.9 %all-gather.29.cloned.1.call-done = bf16[1024,1024]{1,0:T(8,128)(2,1)} async-done(((bf16[256,1024]{1,0:T(8,128)(2,1)}), bf16[1024,1024]{1,0:T(8,128)(2,1)}) %all-gather.29.cloned.1.call-update) | async-done | bytes 2097168 | tf_op jit(solution)/shard_map/all_gather | solution.py:103
  1810.5 37.2 %reduce-scatter.57.cloned.1.call-done = bf16[2,256,704]{1,2,0:T(8,128)(2,1)} async-done(((bf16[2,1024,704]{1,2,0:T(8,128)(2,1)}), bf16[2,256,704]{1,2,0:T(8,128)(2,1)}) %reduce-scatter.57.cloned.1.call-update) | async-done | bytes 720912 | tf_op jit(solution)/shard_map/reduce_scatter | solution.py:317
  1850.0 22.4 %reduce-scatter.55.cloned.1.call-done = bf16[256,256]{1,0:T(8,128)(2,1)} async-done(((bf16[256,1024]{1,0:T(8,128)(2,1)}), bf16[256,256]{1,0:T(8,128)(2,1)}) %reduce-scatter.55.cloned.1.call-update) | async-done | bytes 131088 | tf_op jit(solution)/shard_map/reduce_scatter | solution.py:314
  1874.1 29.1 %reduce-scatter.53.cloned.1.call-done = bf16[3,256,256]{1,2,0:T(8,128)(2,1)} async-done(((bf16[3,1024,256]{1,2,0:T(8,128)(2,1)}), bf16[3,256,256]{1,2,0:T(8,128)(2,1)}) %reduce-scatter.53.cloned.1.call-update) | async-done | bytes 393232 | tf_op jit(solution)/shard_map/reduce_scatter | solution.py:311
  1910.6 51.8 %reduce-scatter.61.cloned.1.call-done = f32[64,2]{1,0:T(8,128)} async-done(((f32[1024,2]{1,0:T(8,128)}), f32[64,2]{1,0:T(8,128)}) %reduce-scatter.61.cloned.1.call-update) | async-done | bytes 528
  1963.9 43.9 %reduce-scatter.33.cloned.1.call-done = bf16[256,1024]{1,0:T(8,128)(2,1)} async-done(((bf16[1024,1024]{1,0:T(8,128)(2,1)}), bf16[256,1024]{1,0:T(8,128)(2,1)}) %reduce-scatter.33.cloned.1.call-update) | async-done | bytes 524304 | tf_op jit(solution)/shard_map/reduce_scatter | solution.py:107
  (578 shorter events, 747.3 us)
Async XLA Ops:
  11.5 120.0 %reduce-scatter.23.cloned.1.call-start = ((), (), s32[]{:S(2)}) async-start(), calls=%async_computation.21 | async-start | bytes 2621440 | tf_op jit(solution)/shard_map/reduce_scatter | solution.py:96
  88.7 91.9 %all-gather.21.cloned.1.call-start = ((), (), s32[]{:S(2)}) async-start(), calls=%async_computation.22 | async-start | bytes 2621440 | tf_op jit(solution)/shard_map/all_gather | solution.py:103
  135.2 96.4 %reduce-scatter.25.cloned.1.call-start = ((), (), s32[]{:S(2)}) async-start(), calls=%async_computation.23 | async-start | bytes 2621440 | tf_op jit(solution)/shard_map/reduce_scatter | solution.py:107
  188.8 111.5 %all-gather.23.cloned.1.call-start = ((), (), s32[]{:S(2)}) async-start(), calls=%async_computation.24 | async-start | bytes 2621440 | tf_op jit(solution)/shard_map/all_gather | solution.py:64
  253.4 119.8 %reduce-scatter.27.cloned.1.call-start = ((), (), s32[]{:S(2)}) async-start(), calls=%async_computation.25 | async-start | bytes 2621440 | tf_op jit(solution)/shard_map/reduce_scatter | solution.py:96
  376.6 96.4 %reduce-scatter.29.cloned.1.call-start = ((), (), s32[]{:S(2)}) async-start(), calls=%async_computation.27 | async-start | bytes 2621440 | tf_op jit(solution)/shard_map/reduce_scatter | solution.py:107
  430.3 114.7 %all-gather.33.cloned.1.call-start = ((), (), s32[]{:S(2)}) async-start(), calls=%async_computation.33 | async-start | bytes 2621440 | tf_op jit(solution)/shard_map/all_gather | solution.py:64
  498.2 122.7 %reduce-scatter.35.cloned.1.call-start = ((), (), s32[]{:S(2)}) async-start(), calls=%async_computation.34 | async-start | bytes 2621440 | tf_op jit(solution)/shard_map/reduce_scatter | solution.py:96
  578.2 91.8 %all-gather.35.cloned.1.call-start = ((), (), s32[]{:S(2)}) async-start(), calls=%async_computation.35 | async-start | bytes 2621440 | tf_op jit(solution)/shard_map/all_gather | solution.py:103
  624.6 91.6 %all-gather.31.cloned.1.call-start = ((), (), s32[]{:S(2)}) async-start(), calls=%async_computation.32 | async-start | bytes 2621440 | tf_op jit(solution)/shard_map/all_gather | solution.py:152
  627.9 143.7 %reduce-scatter.37.cloned.1.call-start = ((), (), s32[]{:S(2)}) async-start(), calls=%async_computation.36 | async-start | bytes 2621440 | tf_op jit(solution)/shard_map/reduce_scatter | solution.py:164
  728.8 95.6 %all-gather.37.cloned.1.call-start = ((), (), s32[]{:S(2)}) async-start(), calls=%async_computation.37 | async-start | bytes 2621440 | tf_op jit(solution)/shard_map/all_gather | solution.py:175
  780.4 152.6 %reduce-scatter.39.cloned.1.call-start = ((), (), s32[]{:S(2)}) async-start(), calls=%async_computation.38 | async-start | bytes 2621440 | tf_op jit(solution)/shard_map/reduce_scatter | solution.py:213
  919.6 111.8 %all-gather.43.cloned.1.call-start = ((), (), s32[]{:S(2)}) async-start(), calls=%async_computation.42 | async-start | bytes 2621440 | tf_op jit(solution)/shard_map/all_gather | solution.py:103
  986.0 92.3 %all-gather.39.cloned.1.call-start = ((), (), s32[]{:S(2)}) async-start(), calls=%async_computation.39 | async-start | bytes 2621440 | tf_op jit(solution)/shard_map/all_gather | solution.py:152
  1004.5 129.0 %reduce-scatter.43.cloned.1.call-start = ((), (), s32[]{:S(2)}) async-start(), calls=%async_computation.43 | async-start | bytes 2621440 | tf_op jit(solution)/shard_map/reduce_scatter | solution.py:164
  1090.8 95.3 %all-gather.45.cloned.1.call-start = ((), (), s32[]{:S(2)}) async-start(), calls=%async_computation.44 | async-start | bytes 2621440 | tf_op jit(solution)/shard_map/all_gather | solution.py:175
  1140.6 91.8 %all-gather.49.cloned.1.call-start = ((), (), s32[]{:S(2)}) async-start(), calls=%async_computation.47 | async-start | bytes 2621440 | tf_op jit(solution)/shard_map/all_gather | solution.py:64
  1142.7 105.3 %collective-permute-start.5 = (bf16[1024,256]{1,0:T(8,128)(2,1)}, bf16[1024,256]{1,0:T(8,128)(2,1)}, u32[]{:S(2)}, u32[]{:S(2)}) collective-permute-start(bf16[1024,256]{1,0:T(8,128)(2,1)} %copy.70), channel_id=1, source_target_pairs={{16,0},{17,1},{18,2},{19,3},{20,4},{21,5},{22,6},{23,7},{24,8},{25... | collective-permute-start | bytes 1572872 | tf_op jit(solution)/shard_map/ppermute | solution.py:19
  1145.4 152.7 %reduce-scatter.45.cloned.1.call-start = ((), (), s32[]{:S(2)}) async-start(), calls=%async_computation.45 | async-start | bytes 2621440 | tf_op jit(solution)/shard_map/reduce_scatter | solution.py:213
  1284.6 111.5 %all-gather.51.cloned.1.call-start = ((), (), s32[]{:S(2)}) async-start(), calls=%async_computation.49 | async-start | bytes 2621440 | tf_op jit(solution)/shard_map/all_gather | solution.py:103
  1350.6 92.4 %all-gather.47.cloned.1.call-start = ((), (), s32[]{:S(2)}) async-start(), calls=%async_computation.46 | async-start | bytes 2621440 | tf_op jit(solution)/shard_map/all_gather | solution.py:152
  1369.1 129.1 %reduce-scatter.49.cloned.1.call-start = ((), (), s32[]{:S(2)}) async-start(), calls=%async_computation.50 | async-start | bytes 2621440 | tf_op jit(solution)/shard_map/reduce_scatter | solution.py:164
  1456.2 135.1 %all-gather.53.cloned.1.call-start = ((), (), s32[]{:S(2)}) async-start(), calls=%async_computation.51 | async-start | bytes 2621440 | tf_op jit(solution)/shard_map/all_gather | solution.py:175
  1503.4 183.7 %reduce-scatter.31.cloned.1.call-start = ((), (), s32[]{:S(2)}) async-start(), calls=%async_computation.29 | async-start | bytes 2621440 | tf_op jit(solution)/shard_map/reduce_scatter | solution.py:96
  1672.2 107.9 %all-gather.29.cloned.1.call-start = ((), (), s32[]{:S(2)}) async-start(), calls=%async_computation.30 | async-start | bytes 2621440 | tf_op jit(solution)/shard_map/all_gather | solution.py:103
  1690.5 118.1 %reduce-scatter.59.cloned.1.call-start = ((), (), s32[]{:S(2)}) async-start(), calls=%async_computation.56 | async-start | bytes 1802240 | tf_op jit(solution)/shard_map/reduce_scatter | solution.py:320
  1703.4 144.3 %reduce-scatter.57.cloned.1.call-start = ((), (), s32[]{:S(2)}) async-start(), calls=%async_computation.55 | async-start | bytes 3604480 | tf_op jit(solution)/shard_map/reduce_scatter | solution.py:317
  1717.4 155.1 %reduce-scatter.55.cloned.1.call-start = ((), (), s32[]{:S(2)}) async-start(), calls=%async_computation.54 | async-start | bytes 655360 | tf_op jit(solution)/shard_map/reduce_scatter | solution.py:314
  1727.3 176.0 %reduce-scatter.53.cloned.1.call-start = ((), (), s32[]{:S(2)}) async-start(), calls=%async_computation.53 | async-start | bytes 1966080 | tf_op jit(solution)/shard_map/reduce_scatter | solution.py:311
  1735.2 227.2 %reduce-scatter.61.cloned.1.call-start = ((), (), s32[]{:S(2)}) async-start(), calls=%async_computation.57 | async-start | bytes 557056
  1738.2 269.6 %reduce-scatter.33.cloned.1.call-start = ((), (), s32[]{:S(2)}) async-start(), calls=%async_computation.31 | async-start | bytes 2621440 | tf_op jit(solution)/shard_map/reduce_scatter | solution.py:107
  (155 other events, 3568.0 us)
Sparse Core Ops, SparseCore 0:
  11.6 48.6 all-gather.18
  88.8 42.5 reduce-scatter.22
  135.3 45.2 all-gather.20
  188.9 42.5 reduce-scatter.24
  253.5 46.7 all-gather.22
  376.7 45.2 all-gather.24
  430.4 42.5 reduce-scatter.28
  498.3 46.5 all-gather.32
  578.3 42.5 reduce-scatter.34
  624.7 45.2 all-gather.34
  671.5 44.6 all-gather.30
  729.0 42.5 reduce-scatter.36
  779.1 45.2 all-gather.36
  825.8 44.6 all-gather.40
  890.4 42.5 reduce-scatter.38
  935.9 43.1 reduce-scatter.40
  986.1 45.2 all-gather.42
  1033.5 44.6 all-gather.38
  1090.9 42.5 reduce-scatter.42
  1140.7 45.3 all-gather.44
  1187.7 44.6 all-gather.48
  1255.4 42.5 reduce-scatter.44
  1300.7 43.1 reduce-scatter.46
  1350.7 45.4 all-gather.50
  1398.3 44.6 all-gather.46
  1455.6 42.5 reduce-scatter.48
  1499.8 45.2 all-gather.26
  1546.6 44.6 all-gather.52
  1689.5 43.1 reduce-scatter.50
  1734.9 45.1 all-gather.28
  1906.6 55.7 reduce-scatter.60
  1964.9 42.8 reduce-scatter.32
  (6 shorter events, 196.9 us)
where the time goes:
time: 2030 us; the launch traced here: 2020 us
  waiting for transfers between devices  1350 us (67%)
  matrix products  367 us (18%)
  other arithmetic  197 us (10%)
  local copies, waits for them, and re-layouts  61.1 us (3%)
  starting transfers between devices  26.9 us (1%)
    reduce_scatter x6, waiting for transfers between devices, forward_layer(): lax.psum_scatter(jnp.dot(piece, w_out, preferred_element_type=jnp.float32...  235 us
    all_gather x6, waiting for transfers between devices, forward_layer(): mixed_full = lax.all_gather(mixed_in, 'tensor', axis=0, tiled=True)  227 us
    all_gather x6, waiting for transfers between devices, forward_layer(): rows_full = lax.all_gather(normed, 'tensor', axis=0, tiled=True)  154 us
    reduce_scatter x3, waiting for transfers between devices, forward_layer(): lax.psum_scatter(jnp.dot(piece, w_down, preferred_element_type=jnp.float3...  129 us
    reduce_scatter x3, waiting for transfers between devices, backward_layer(): lax.psum_scatter(jnp.einsum('csf,cdf->sd', piece, w_gate_up, preferred_el...  127 us
    all_gather x3, waiting for transfers between devices, backward_layer(): lax.all_gather(grad_hidden.astype(jnp.bfloat16), 'tensor', axis=0, tiled=...  124 us
    all_gather x3, waiting for transfers between devices, backward_layer(): lax.all_gather(grad_out.astype(jnp.bfloat16), 'tensor', axis=0, tiled=True)  120 us
    unnamed x39, waiting for transfers between devices  53.1 us
  transfers between devices with their start and end apart: 46, of which 42 were waited for; matrix products, arithmetic and copies ran while one was open for 17% of the time, Pallas kernels for 0%

commit v1 on v0

v1 whole, which is shorter than its diff:
```python
import jax
import jax.numpy as jnp
import numpy as np
from jax import lax
from jax.experimental import pallas as pl
from jax.experimental.pallas import tpu as pltpu
from jax.sharding import PartitionSpec as P

MESH = pl.DeviceIdType.MESH
ANY = pl.BlockSpec(memory_space=pl.ANY)


DEPTH = 2
CUTS = (2, 1, 4, 2)


def weight_pieces(part, _, out_rows, down_rows):
    pieces = []
    for w, total in enumerate((part, out_rows, part, down_rows)):
        cuts = CUTS[w]
        while total % (16 * cuts):
            cuts -= 1
        size = total // cuts
        pieces += [(w, i * size, size) for i in range(cuts)]
    return pieces


def gather_kernel(
    tok, cot, qkv, out, gu, down,
    seq, w_qkv, w_out, w_gu, w_down,
    loc, a2a_s, a2a_r, sib_s, sib_r, own_r, own_l, z_recv, z_fwd, x_s, x_r,
):
    mb, rows, _ = tok.shape
    n_t = lax.axis_size("tensor")
    nx = lax.axis_size("dp") // 2
    sec = lax.axis_index("section")
    dp = lax.axis_index("dp")
    z = lax.axis_index("tensor")
    x, c = dp // 2, lax.rem(dp, 2)
    dim = tok.shape[2]
    part = dim // nx
    head_cols = qkv.shape[3]
    out_rows = out.shape[1]
    here = z // mb == c
    jz = z - c * mb
    sibling = {"dp": 2 * x + 1 - c}

    barrier = pltpu.get_barrier_semaphore()
    for k in range(1, n_t):
        pl.semaphore_signal(
            barrier, inc=1, device_id={"tensor": lax.rem(z + k, n_t)}, device_id_type=MESH
        )
    for k in range(1, nx):
        pl.semaphore_signal(
            barrier, inc=1, device_id={"dp": 2 * lax.rem(x + k, nx) + c}, device_id_type=MESH
        )
    pl.semaphore_signal(barrier, inc=1, device_id=sibling, device_id_type=MESH)
    pl.semaphore_wait(barrier, n_t + nx - 1)

    pieces = weight_pieces(part, gu.shape[1], out_rows, down.shape[1])

    def shard_part(k, p):
        w, lo, size = pieces[k]
        col = pl.multiple_of(p * part, 128)
        row = pl.multiple_of(col + lo, 16)
        return (
            lambda: qkv.at[0, :, pl.ds(row, size), :],
            lambda: out.at[0, pl.ds(lo, size), pl.ds(col, part)],
            lambda: gu.at[0, :, pl.ds(row, size), :],
            lambda: down.at[0, pl.ds(lo, size), pl.ds(col, part)],
        )[w]()

    def slot_part(k, j, p):
        w, lo, size = pieces[k]
        col = pl.multiple_of(p * part, 128)
        row = pl.multiple_of(col + lo, 16)
        return (
            lambda: w_qkv.at[:, pl.ds(row, size), pl.ds(pl.multiple_of(j * head_cols, 128), head_cols)],
            lambda: w_out.at[pl.ds(pl.multiple_of(j * out_rows + lo, 16), size), pl.ds(col, part)],
            lambda: w_gu.at[j, :, pl.ds(row, size), :],
            lambda: w_down.at[j, pl.ds(lo, size), pl.ds(col, part)],
        )[w]()

    def remote(src, dst, send, recv, to):
        return pltpu.make_async_remote_copy(
            src_ref=src, dst_ref=dst, send_sem=send, recv_sem=recv,
            device_id=to, device_id_type=MESH,
        )

    right, left = {"tensor": z + 1}, {"tensor": z - 1}
    block = seq.at[pl.ds(pl.multiple_of(z * rows, 128), rows), :]

    for i in range(mb):
        zt = c * mb + i
        for which, source in ((0, tok), (1, cot)):
            @pl.when((zt != z) & (sec == which))
            def _(source=source, i=i, zt=zt):
                remote(source.at[i], block, a2a_s.at[i], a2a_r.at[z], {"tensor": zt}).start()

            @pl.when((zt == z) & (sec == which))
            def _(source=source, i=i):
                pltpu.make_async_copy(source.at[i], block, loc.at[1]).start()

    n_k = len(pieces)

    @pl.when(here)
    def _():
        for k in range(n_k):
            for p in range(nx):
                pltpu.make_async_copy(shard_part(k, p), slot_part(k, jz, p), loc.at[0]).start()

    def order(i):
        return jnp.where(c == 0, mb - 1 - i, i)

    for k in range(n_k):
        @pl.when(here)
        def _(k=k):
            @pl.when(z < n_t - 1)
            def _():
                if k >= DEPTH:
                    remote(shard_part(k - DEPTH, x), slot_part(k - DEPTH, jz, x), own_r.at[k - DEPTH], z_recv.at[k, jz], right).wait_send()
                remote(shard_part(k, x), slot_part(k, jz, x), own_r.at[k], z_recv.at[k, jz], right).start()

            @pl.when(z > 0)
            def _():
                if k >= DEPTH:
                    remote(shard_part(k - DEPTH, x), slot_part(k - DEPTH, jz, x), own_l.at[k - DEPTH], z_recv.at[k, jz], left).wait_send()
                remote(shard_part(k, x), slot_part(k, jz, x), own_l.at[k], z_recv.at[k, jz], left).start()

        for i in range(mb):
            j = order(i)
            s = c * mb + j
            piece = slot_part(k, j, x)

            @pl.when(s != z)
            def _(k=k, j=j, s=s, piece=piece):
                remote(piece, piece, z_fwd.at[k, j], z_recv.at[k, j], right).wait_recv()

                @pl.when((s < z) & (z < n_t - 1))
                def _():
                    remote(piece, piece, z_fwd.at[k, j], z_recv.at[k, j], right).start()

                @pl.when((s > z) & (z > 0))
                def _():
                    remote(piece, piece, z_fwd.at[k, j], z_recv.at[k, j], left).start()

                for d in range(1, nx):
                    remote(
                        piece, piece, x_s.at[k, j, d], x_r.at[k, j, x],
                        {"dp": 2 * lax.rem(x + d, nx) + c},
                    ).start()

        if k == min(2, n_k - 1):
            @pl.when(here)
            def _():
                for zs in range(n_t):
                    src = seq.at[pl.ds(zs * rows, rows), :]

                    @pl.when(zs != z)
                    def _(src=src, zs=zs):
                        remote(src, src, a2a_s.at[0], a2a_r.at[zs], right).wait_recv()

                pltpu.make_async_copy(block, block, loc.at[1]).wait()
                remote(seq, seq, sib_s, sib_r, sibling).start()

    for k in range(n_k):
        for j in range(mb):
            s = c * mb + j

            @pl.when(s != z)
            def _(k=k, j=j, s=s):
                for d in range(1, nx):
                    p = lax.rem(x + d, nx)
                    piece = slot_part(k, j, p)
                    remote(piece, piece, x_s.at[k, j, d], x_r.at[k, j, p], right).wait_recv()
                    own = slot_part(k, j, x)
                    remote(own, own, x_s.at[k, j, d], x_r.at[k, j, p], right).wait_send()

                @pl.when(((s < z) & (z < n_t - 1)) | ((s > z) & (z > 0)))
                def _():
                    own = slot_part(k, j, x)
                    remote(own, own, z_fwd.at[k, j], z_recv.at[k, j], right).wait_send()

    @pl.when(here)
    def _():
        for k in range(n_k):
            for p in range(nx):
                pltpu.make_async_copy(shard_part(k, p), slot_part(k, jz, p), loc.at[0]).wait()

        for k in range(max(0, n_k - DEPTH), n_k):
            @pl.when(z < n_t - 1)
            def _(k=k):
                remote(shard_part(k, x), slot_part(k, jz, x), own_r.at[k], z_recv.at[k, jz], right).wait_send()

            @pl.when(z > 0)
            def _(k=k):
                remote(shard_part(k, x), slot_part(k, jz, x), own_l.at[k], z_recv.at[k, jz], left).wait_send()

        remote(seq, seq, sib_s, sib_r, sibling).wait_send()

    @pl.when(jnp.logical_not(here))
    def _():
        remote(seq, seq, sib_s, sib_r, sibling).wait_recv()

    for i in range(mb):
        zt = c * mb + i

        @pl.when(zt != z)
        def _(i=i):
            remote(tok.at[i], block, a2a_s.at[i], a2a_r.at[z], right).wait_send()


def gather(tokens, cotangent, qkv, out, gu, down):
    mb, rows, dim = tokens.shape
    n_t = lax.axis_size("tensor")
    nx = lax.axis_size("dp") // 2
    dma = pltpu.SemaphoreType.DMA
    n_k = len(weight_pieces(dim // nx, gu.shape[1], out.shape[1], down.shape[1]))
    return pl.pallas_call(
        gather_kernel,
        out_shape=(
            jax.ShapeDtypeStruct((rows * n_t, dim), jnp.bfloat16),
            jax.ShapeDtypeStruct((3, dim, mb * qkv.shape[3]), jnp.bfloat16),
            jax.ShapeDtypeStruct((mb * out.shape[1], dim), jnp.bfloat16),
            jax.ShapeDtypeStruct((mb, 2, dim, gu.shape[3]), jnp.bfloat16),
            jax.ShapeDtypeStruct((mb, down.shape[1], dim), jnp.bfloat16),
        ),
        in_specs=[ANY] * 2 + [pl.BlockSpec(memory_space=pltpu.VMEM)] * 4,
        out_specs=(ANY,) * 5,
        scratch_shapes=[
            dma((2,)), dma((mb,)), dma((n_t,)), dma, dma,
            dma((n_k,)), dma((n_k,)), dma((n_k, mb)), dma((n_k, mb)),
            dma((n_k, mb, nx)), dma((n_k, mb, nx)),
        ],
        compiler_params=pltpu.CompilerParams(
            collective_id=0, has_side_effects=True, vmem_limit_bytes=16 << 20
        ),
        name="gather_weights",
    )(tokens, cotangent, qkv, out, gu, down)


RING_DEPTH = 3
OWN_LAG = 3


def scatter_kernel(
    g_qkv, g_out, g_gu, g_down, y, dx,
    o_qkv, o_out, o_gu, o_down, o_y, o_dx,
    xb_qkv, xb_out, xb_gu, xb_down,
    zb_qkv, zb_out, zb_gu, zb_down,
    fb_qkv, fb_out, fb_gu, fb_down,
    a2a_s, a2a_r, x_s, x_r, z_s, z_r, zo_r, f_s, f_r,
):
    mb = g_qkv.shape[0]
    n_t = lax.axis_size("tensor")
    nx = lax.axis_size("dp") // 2
    dp = lax.axis_index("dp")
    z = lax.axis_index("tensor")
    x, c = dp // 2, lax.rem(dp, 2)
    dim = g_qkv.shape[2]
    part = dim // nx
    quarter = part // 2
    rows = y.shape[0] // n_t
    here = z // mb == c
    jz = z - c * mb
    sibling = {"dp": 2 * x + 1 - c}
    right, left = {"tensor": z + 1}, {"tensor": z - 1}
    pieces = weight_pieces(part, g_gu.shape[1], g_out.shape[1], g_down.shape[1])
    n_k = len(pieces)

    barrier = pltpu.get_barrier_semaphore()
    for k in range(1, n_t):
        pl.semaphore_signal(
            barrier, inc=1, device_id={"tensor": lax.rem(z + k, n_t)}, device_id_type=MESH
        )
    for k in range(1, nx):
        pl.semaphore_signal(
            barrier, inc=1, device_id={"dp": 2 * lax.rem(x + k, nx) + c}, device_id_type=MESH
        )
    pl.semaphore_signal(barrier, inc=1, device_id=sibling, device_id_type=MESH)
    pl.semaphore_wait(barrier, n_t + nx - 1)

    def remote(src, dst, send, recv, to):
        return pltpu.make_async_remote_copy(
            src_ref=src, dst_ref=dst, send_sem=send, recv_sem=recv,
            device_id=to, device_id_type=MESH,
        )

    def grad_part(k, j, p):
        w, lo, size = pieces[k]
        col = pl.multiple_of(p * part, 128)
        row = pl.multiple_of(col + lo, 16)
        return (
            lambda: g_qkv.at[j, :, pl.ds(row, size), :],
            lambda: g_out.at[j, pl.ds(lo, size), pl.ds(col, part)],
            lambda: g_gu.at[j, :, pl.ds(row, size), :],
            lambda: g_down.at[j, pl.ds(lo, size), pl.ds(col, part)],
        )[w]()

    def buffer_part(bufs, k, j):
        w, lo, size = pieces[k]
        if w in (0, 2):
            return bufs[w].at[j, :, pl.ds(lo, size), :]
        return bufs[w].at[j, pl.ds(lo, size), :]

    def x_buf(k, j, d):
        return buffer_part([b.at[d - 1] for b in (xb_qkv, xb_out, xb_gu, xb_down)], k, j)

    def z_buf(k, j):
        return buffer_part((zb_qkv, zb_out, zb_gu, zb_down), k, j)

    @pl.when(here)
    def _():
        for t, (src, dst) in enumerate(((y, o_y), (dx, o_dx))):
            for d in range(1, n_t):
                zt = lax.rem(z + d, n_t)
                block = src.at[pl.ds(pl.multiple_of(zt * rows, 128), rows), :]
                remote(block, dst.at[jz], a2a_s.at[t, d], a2a_r.at[t, jz], {"tensor": zt}).start()

    def x_send(n):
        k, i = n // mb, n % mb
        j = jnp.where(c == 0, i, mb - 1 - i)
        for d in range(1, nx):
            to = lax.rem(x + d, nx)
            yield remote(
                grad_part(k, j, to), x_buf(k, j, d), x_s.at[k, j, d], x_r.at[k, j, d],
                {"dp": 2 * to + c},
            )

    total = n_k * mb
    for n in range(RING_DEPTH):
        for copy in x_send(n):
            copy.start()

    def final_part(k):
        w, lo, size = pieces[k]
        if w == 0:
            return o_qkv.at[:, pl.ds(lo % quarter, size), :], fb_qkv.at[:, pl.ds(lo % quarter, size), :]
        if w == 1:
            return o_out.at[pl.ds(lo, size), :], fb_out.at[pl.ds(lo, size), :]
        if w == 2:
            return o_gu.at[:, pl.ds(lo % quarter, size), :], fb_gu.at[:, pl.ds(lo % quarter, size), :]
        return o_down.at[pl.ds(lo, size), :], fb_down.at[pl.ds(lo, size), :]

    def own_piece(k):
        w, lo, size = pieces[k]
        total_sum = grad_part(k, jz, x)[...].astype(jnp.float32)
        for d in range(1, nx):
            total_sum = total_sum + x_buf(k, jz, d)[...].astype(jnp.float32)
        x_buf(k, jz, 1)[...] = total_sum.astype(jnp.bfloat16)

        @pl.when(z > 0)
        def _():
            piece = z_buf(k, jz)
            remote(piece, piece, z_s.at[k, jz], z_r.at[k, jz], right).wait_recv()
            x_buf(k, jz, 1)[...] = (
                x_buf(k, jz, 1)[...].astype(jnp.float32) + piece[...].astype(jnp.float32)
            ).astype(jnp.bfloat16)

        @pl.when(z < n_t - 1)
        def _():
            piece = z_buf(k, mb)
            remote(piece, piece, z_s.at[k, jz], zo_r.at[k], right).wait_recv()
            x_buf(k, jz, 1)[...] = (
                x_buf(k, jz, 1)[...].astype(jnp.float32) + piece[...].astype(jnp.float32)
            ).astype(jnp.bfloat16)

        summed = x_buf(k, jz, 1)
        out_ref, fin = final_part(k)
        if w in (0, 2):
            @pl.when(c == lo // quarter)
            def _():
                out_ref[...] = summed[...].astype(jnp.float32)

            @pl.when(c != lo // quarter)
            def _():
                remote(summed, fin, f_s.at[k], f_r.at[k], sibling).start()
        else:
            mine = pl.ds(pl.multiple_of(c * quarter, 128), quarter)
            theirs = pl.ds(pl.multiple_of((1 - c) * quarter, 128), quarter)
            out_ref[...] = summed[:, mine].astype(jnp.float32)
            remote(summed.at[:, theirs], fin, f_s.at[k], f_r.at[k], sibling).start()

    for k in range(n_k):
        for i in range(mb):
            n = k * mb + i
            j = jnp.where(c == 0, i, mb - 1 - i)
            s = c * mb + j
            if n + RING_DEPTH < total:
                for copy in x_send(n):
                    copy.wait_send()
                for copy in x_send(n + RING_DEPTH):
                    copy.start()
            for copy in x_send(n):
                copy.wait_recv()

            @pl.when(s != z)
            def _(k=k, j=j, s=s):
                total_sum = grad_part(k, j, x)[...].astype(jnp.float32)
                for d in range(1, nx):
                    total_sum = total_sum + x_buf(k, j, d)[...].astype(jnp.float32)
                x_buf(k, j, 1)[...] = total_sum.astype(jnp.bfloat16)

                @pl.when(((s > z) & (z > 0)) | ((s < z) & (z < n_t - 1)))
                def _():
                    piece = z_buf(k, j)
                    remote(piece, piece, z_s.at[k, j], z_r.at[k, j], right).wait_recv()
                    x_buf(k, j, 1)[...] = (
                        x_buf(k, j, 1)[...].astype(jnp.float32) + piece[...].astype(jnp.float32)
                    ).astype(jnp.bfloat16)

                @pl.when(s > z)
                def _():
                    remote(x_buf(k, j, 1), z_buf(k, j), z_s.at[k, j], z_r.at[k, j], right).start()

                @pl.when(s < z - 1)
                def _():
                    remote(x_buf(k, j, 1), z_buf(k, j), z_s.at[k, j], z_r.at[k, j], left).start()

                @pl.when(s == z - 1)
                def _():
                    remote(x_buf(k, j, 1), z_buf(k, mb), z_s.at[k, j], zo_r.at[k], left).start()

        if k >= OWN_LAG:
            @pl.when(here)
            def _(k=k):
                own_piece(k - OWN_LAG)

    @pl.when(here)
    def _():
        for k in range(max(0, n_k - OWN_LAG), n_k):
            own_piece(k)

    @pl.when(jnp.logical_not(here))
    def _():
        for k in range(n_k):
            w, lo, size = pieces[k]
            out_ref, fin = final_part(k)
            if w in (0, 2):
                @pl.when(c == lo // quarter)
                def _(k=k, out_ref=out_ref, fin=fin):
                    remote(fin, fin, f_s.at[k], f_r.at[k], sibling).wait_recv()
                    out_ref[...] = fin[...].astype(jnp.float32)
            else:
                remote(fin, fin, f_s.at[k], f_r.at[k], sibling).wait_recv()
                out_ref[...] = fin[...].astype(jnp.float32)

    for n in range(max(0, total - RING_DEPTH), total):
        for copy in x_send(n):
            copy.wait_send()

    for k in range(n_k):
        for j in range(mb):
            s = c * mb + j

            @pl.when(s != z)
            def _(k=k, j=j):
                piece = x_buf(k, j, 1)
                remote(piece, piece, z_s.at[k, j], z_r.at[k, j], right).wait_send()

    @pl.when(here)
    def _():
        for k in range(n_k):
            w, lo, size = pieces[k]
            fin = final_part(k)[1]
            if w in (0, 2):
                @pl.when(c != lo // quarter)
                def _(k=k, fin=fin):
                    remote(fin, fin, f_s.at[k], f_r.at[k], sibling).wait_send()
            else:
                remote(fin, fin, f_s.at[k], f_r.at[k], sibling).wait_send()

        for t, (src, dst) in enumerate(((y, o_y), (dx, o_dx))):
            for d in range(1, n_t):
                block = src.at[pl.ds(0, rows), :]
                remote(block, dst.at[0], a2a_s.at[t, d], a2a_r.at[t, jz], right).wait_send()
            dst[jz] = src[pl.ds(pl.multiple_of(z * rows, 128), rows), :]

    for t, dst in enumerate((o_y, o_dx)):
        for i in range(mb):
            @pl.when(c * mb + i != z)
            def _(t=t, i=i, dst=dst):
                remote(dst.at[i], dst.at[i], a2a_s.at[t, 0], a2a_r.at[t, i], right).wait_recv()


def scatter(g_qkv, g_out, g_gu, g_down, y, dx):
    mb, _, dim, cols = g_qkv.shape
    n_t = lax.axis_size("tensor")
    n_dp = lax.axis_size("dp")
    nx = n_dp // 2
    part, quarter = dim // nx, dim // n_dp
    out_rows, ff, down_rows = g_out.shape[1], g_gu.shape[3], g_down.shape[1]
    rows = y.shape[0] // n_t
    dma = pltpu.SemaphoreType.DMA
    n_k = len(weight_pieces(part, dim, out_rows, down_rows))
    bf, f32 = jnp.bfloat16, jnp.float32

    def shapes(lead, split):
        return (
            (*lead, 3, split, cols), (*lead, out_rows, split),
            (*lead, 2, split, ff), (*lead, down_rows, split),
        )

    vmem = pl.BlockSpec(memory_space=pltpu.VMEM)
    finals = shapes((), quarter)
    return pl.pallas_call(
        scatter_kernel,
        out_shape=(
            *(jax.ShapeDtypeStruct(shape, f32) for shape in finals),
            jax.ShapeDtypeStruct((mb, rows, dim), bf),
            jax.ShapeDtypeStruct((mb, rows, dim), bf),
        ),
        in_specs=[vmem] * 6,
        out_specs=(vmem,) * 6,
        scratch_shapes=[
            *(pltpu.VMEM(shape, bf) for shape in shapes((nx - 1, mb), part)),
            *(pltpu.VMEM(shape, bf) for shape in shapes((mb + 1,), part)),
            *(pltpu.VMEM(shape, bf) for shape in finals),
            dma((2, n_t)), dma((2, mb)), dma((n_k, mb, nx)), dma((n_k, mb, nx)),
            dma((n_k, mb)), dma((n_k, mb)), dma((n_k,)), dma((n_k,)), dma((n_k,)),
        ],
        compiler_params=pltpu.CompilerParams(
            collective_id=1, has_side_effects=True, vmem_limit_bytes=62 << 20
        ),
        name="scatter_grads",
    )(g_qkv, g_out, g_gu, g_down, y, dx)


NORM_EPS = 1e-6
ROPE_BASE = 10000.0
SCORE_SCALE = 0.125
MASK_VALUE = -1e30
HD = 64
PAIR = 2 * HD
BLOCK = 256
NT = (((1,), (1,)), ((), ()))


def rope_tables(positions):
    lane = np.arange(PAIR)
    frequency = ROPE_BASE ** (-(lane % (HD // 2)) * 2.0 / HD)
    angles = np.arange(positions)[:, None] * frequency[None, :]
    sign = np.where(lane % HD < HD // 2, -1.0, 1.0)
    return np.cos(angles).astype(np.float32), (np.sin(angles) * sign).astype(np.float32)


def rotate_pair(values, cos, sin):
    lane = lax.broadcasted_iota(jnp.int32, values.shape, 1)
    partner = jnp.where(
        lax.rem(lane, HD) < HD // 2,
        pltpu.roll(values, PAIR - HD // 2, 1),
        pltpu.roll(values, HD // 2, 1),
    )
    return values * cos + partner * sin


def qkv_kernel(share, x, first, gain, w, cos, sin, a_o, q_o, k_o, v_o, vu_o):
    xf = x[...].astype(jnp.float32)
    scale = lax.rsqrt(jnp.mean(xf * xf, axis=-1, keepdims=True) + NORM_EPS)
    a = (xf * scale * gain[...]).astype(jnp.bfloat16)
    a_o[...] = a
    q = jnp.dot(a, w[0], preferred_element_type=jnp.float32)
    k = jnp.dot(a, w[1], preferred_element_type=jnp.float32)
    for p in range(q.shape[1] // PAIR):
        cols = slice(p * PAIR, (p + 1) * PAIR)
        q_o[:, cols] = (rotate_pair(q[:, cols], cos[...], sin[...]) * SCORE_SCALE).astype(jnp.bfloat16)
        k_o[:, cols] = rotate_pair(k[:, cols], cos[...], sin[...]).astype(jnp.bfloat16)
    v = jnp.dot(a, w[2], preferred_element_type=jnp.float32).astype(jnp.bfloat16)
    v_o[...] = v
    vu_o[...] = (
        share[0] * v.astype(jnp.float32) + (1.0 - share[0]) * first[...].astype(jnp.float32)
    ).astype(jnp.bfloat16)


def project_qkv(x, first, gain, w, share, tables):
    seq, dim = x.shape
    width = w.shape[2]
    blk = min(BLOCK, seq)
    smem = pl.BlockSpec(memory_space=pltpu.SMEM)
    rows = lambda cols: pl.BlockSpec((blk, cols), lambda i: (i, 0))
    out = lambda cols: jax.ShapeDtypeStruct((seq, cols), jnp.bfloat16)
    return pl.pallas_call(
        qkv_kernel,
        grid=(seq // blk,),
        in_specs=[
            smem, rows(dim), rows(width),
            pl.BlockSpec((1, dim), lambda i: (0, 0)),
            pl.BlockSpec(w.shape, lambda i: (0, 0, 0)),
            rows(PAIR), rows(PAIR),
        ],
        out_specs=(rows(dim), rows(width), rows(width), rows(width), rows(width)),
        out_shape=(out(dim), out(width), out(width), out(width), out(width)),
        compiler_params=pltpu.CompilerParams(vmem_limit_bytes=32 << 20),
        cost_estimate=pl.CostEstimate(flops=6 * seq * dim * width, bytes_accessed=w.size * 2 + seq * dim * 8, transcendentals=0),
        name="project_qkv",
    )(share, x, first, gain[None], w, *tables)


def head_views(h, shape):
    lane = lax.broadcasted_iota(jnp.int32, shape, 1)
    return lane // HD == h, lane == (1 - h) * HD


def key_bias(length, shape):
    key = lax.broadcasted_iota(jnp.int32, shape, 0)
    return jnp.where(key < length, 0.0, MASK_VALUE)


def causal_block(blk):
    key = lax.broadcasted_iota(jnp.int32, (blk, blk), 0)
    query = lax.broadcasted_iota(jnp.int32, (blk, blk), 1)
    return key <= query


def attention_kernel(length, q, k, v, o, lse):
    seq = q.shape[0]
    blk = min(BLOCK, seq)
    f32, bf = jnp.float32, jnp.bfloat16
    v_t = v[...].astype(f32).T.astype(bf)
    keys = k[...].astype(f32)
    bias = key_bias(length[0], keys.shape)
    visible = causal_block(blk)
    queries = q[...].astype(f32)
    heads = []
    for h in range(2):
        inside, extra = head_views(h, keys.shape)
        heads.append((
            jnp.where(inside, keys, jnp.where(extra, bias, 0.0)).astype(bf),
            jnp.where(inside, queries, jnp.where(extra, 1.0, 0.0)).astype(bf),
            v_t[h * HD:(h + 1) * HD],
        ))
    for i in range(seq // blk):
        lo, hi = i * blk, (i + 1) * blk
        parts = []
        for h in range(2):
            kh, qh, vh = heads[h]
            qi = qh[lo:hi]
            s_diag = lax.dot_general(kh[lo:hi], qi, NT, preferred_element_type=f32)
            s_diag = jnp.where(visible, s_diag, MASK_VALUE)
            top = jnp.max(s_diag, axis=0, keepdims=True)
            if i:
                s_full = lax.dot_general(kh[:lo], qi, NT, preferred_element_type=f32)
                top = jnp.maximum(top, jnp.max(s_full, axis=0, keepdims=True))
            p_diag = jnp.exp(s_diag - top)
            total = jnp.sum(p_diag, axis=0, keepdims=True)
            acc = jnp.dot(vh[:, lo:hi], p_diag.astype(bf), preferred_element_type=f32)
            if i:
                p_full = jnp.exp(s_full - top)
                total = total + jnp.sum(p_full, axis=0, keepdims=True)
                acc = acc + jnp.dot(vh[:, :lo], p_full.astype(bf), preferred_element_type=f32)
            parts.append(acc / total)
            lse[0, h:h + 1, lo:hi] = top + jnp.log(total)
        o[lo:hi, :] = jnp.concatenate(parts, axis=0).T.astype(bf)


def attention(length, q, k, vu):
    seq, width = q.shape
    pairs = width // PAIR
    col = pl.BlockSpec((seq, PAIR), lambda p: (0, p))
    return pl.pallas_call(
        attention_kernel,
        grid=(pairs,),
        in_specs=[pl.BlockSpec(memory_space=pltpu.SMEM), col, col, col],
        out_specs=(col, pl.BlockSpec((1, 2, seq), lambda p: (p, 0, 0))),
        out_shape=(
            jax.ShapeDtypeStruct((seq, width), jnp.bfloat16),
            jax.ShapeDtypeStruct((pairs, 2, seq), jnp.float32),
        ),
        compiler_params=pltpu.CompilerParams(vmem_limit_bytes=48 << 20),
        cost_estimate=pl.CostEstimate(flops=8 * seq * seq * width, bytes_accessed=8 * seq * width, transcendentals=pairs * seq * seq),
        name="attention",
    )(length, q, k, vu)


def attention_back_kernel(length, share, q, k, v, o, do, lse, first, cos, sin, dq_o, dk_o, dv_o, dv1_o, dk_a, dv_a):
    seq = q.shape[0]
    blk = min(BLOCK, seq)
    f32, bf = jnp.float32, jnp.bfloat16
    keys = k[...].astype(f32)
    k_t = keys.T.astype(bf)
    bias = key_bias(length[0], keys.shape)
    visible = causal_block(blk)
    queries = q[...].astype(f32)
    grads = do[...].astype(f32)
    heads = []
    for h in range(2):
        inside, extra = head_views(h, keys.shape)
        heads.append((
            jnp.where(inside, keys, jnp.where(extra, bias, 0.0)).astype(bf),
            jnp.where(inside, queries, jnp.where(extra, 1.0, 0.0)).astype(bf),
            jnp.where(inside, queries, 0.0).astype(bf),
            jnp.where(inside, grads, 0.0).astype(bf),
            k_t[h * HD:(h + 1) * HD],
        ))
    vals = v[...]
    for i in range(seq // blk):
        lo, hi = i * blk, (i + 1) * blk
        product = (grads[lo:hi] * o[lo:hi, :].astype(f32)).T
        parts = []
        for h in range(2):
            kh, qh, qz, gh, kt = heads[h]
            delta = jnp.sum(product[h * HD:(h + 1) * HD], axis=0, keepdims=True)
            stat = lse[0, h:h + 1, lo:hi]

            def side(a, b, mask):
                s = lax.dot_general(kh[a:b], qh[lo:hi], NT, preferred_element_type=f32)
                p = jnp.exp(s - stat)
                if mask:
                    p = jnp.where(visible, p, 0.0)
                dp = lax.dot_general(vals[a:b], gh[lo:hi], NT, preferred_element_type=f32)
                ds = (p * (dp - delta)).astype(bf)
                dv = jnp.dot(p.astype(bf), gh[lo:hi], preferred_element_type=f32)
                dk = jnp.dot(ds, qz[lo:hi], preferred_element_type=f32)
                if mask and h == 0:
                    dv_a[a:b, :] = dv
                    dk_a[a:b, :] = dk
                else:
                    dv_a[a:b, :] += dv
                    dk_a[a:b, :] += dk
                return jnp.dot(kt[:, a:b], ds, preferred_element_type=f32)

            dq_t = side(lo, hi, True)
            if i:
                dq_t = dq_t + side(0, lo, False)
            parts.append(dq_t)
        dq = jnp.concatenate(parts, axis=0).T * SCORE_SCALE
        dq_o[lo:hi, :] = rotate_pair(dq, cos[lo:hi, :], -sin[lo:hi, :]).astype(bf)
    dk_o[...] = rotate_pair(dk_a[...], cos[...], -sin[...]).astype(bf)
    dv_o[...] = (share[0] * dv_a[...] + first[...].astype(f32)).astype(bf)
    dv1_o[...] = ((1.0 - share[0]) * dv_a[...]).astype(bf)


def attention_back(length, share, q, k, vu, o, do, lse, first, tables):
    seq, width = q.shape
    pairs = width // PAIR
    col = pl.BlockSpec((seq, PAIR), lambda p: (0, p))
    whole = pl.BlockSpec((seq, PAIR), lambda p: (0, 0))
    smem = pl.BlockSpec(memory_space=pltpu.SMEM)
    return pl.pallas_call(
        attention_back_kernel,
        grid=(pairs,),
        in_specs=[smem, smem, col, col, col, col, col, pl.BlockSpec((1, 2, seq), lambda p: (p, 0, 0)), col, whole, whole],
        out_specs=(col,) * 4,
        out_shape=(jax.ShapeDtypeStruct((seq, width), jnp.bfloat16),) * 4,
        scratch_shapes=[pltpu.VMEM((seq, PAIR), jnp.float32)] * 2,
        compiler_params=pltpu.CompilerParams(vmem_limit_bytes=48 << 20),
        cost_estimate=pl.CostEstimate(flops=20 * seq * seq * width, bytes_accessed=20 * seq * width, transcendentals=pairs * seq * seq),
        name="attention_back",
    )(length, share, q, k, vu, o, do, lse, first, *tables)


def rms_norm(values, gain):
    return values * lax.rsqrt(jnp.mean(values * values, axis=-1, keepdims=True) + NORM_EPS) * gain


def pair_sum(part):
    mine = part.astype(jnp.bfloat16)
    swap = [(d, d ^ 1) for d in range(lax.axis_size("dp"))]
    theirs = lax.ppermute(mine, "dp", swap)
    return mine.astype(jnp.float32) + theirs.astype(jnp.float32)


def to_section(values, step):
    return lax.ppermute(values, "section", [(0, 1)] if step > 0 else [(1, 0)])


def dot(a, b):
    return jnp.dot(a, b, preferred_element_type=jnp.float32)


def dot_nt(a, b):
    return lax.dot_general(a, b, NT, preferred_element_type=jnp.float32)


def dot_tn(a, b):
    return lax.dot_general(a, b, (((0,), (0,)), ((), ())), preferred_element_type=jnp.float32)


def forward_layer(weights, x, first, length, share, tables):
    w_qkv, w_out, w_gu, w_down, gains = weights
    a, q, k, v, vu = project_qkv(x, first, gains[0], w_qkv, share, tables)
    o, lse = attention(length, q, k, vu)
    h = x.astype(jnp.float32) + pair_sum(dot(o, w_out))
    b = rms_norm(h, gains[1]).astype(jnp.bfloat16)
    part = 0.0
    hidden = []
    for j in range(w_gu.shape[0]):
        gate, up = dot(b, w_gu[j, 0]), dot(b, w_gu[j, 1])
        m = (jax.nn.silu(gate) * up).astype(jnp.bfloat16)
        part = part + dot(m, w_down[j])
        hidden.append((gate, up, m))
    y = (h + pair_sum(part)).astype(jnp.bfloat16)
    return y, v, (a, q, k, vu, o, lse, h, b, hidden)


def backward_layer(weights, x, kept, length, share, tables, dy, first_grad):
    w_qkv, w_out, w_gu, w_down, gains = weights
    a, q, k, vu, o, lse, h, b, hidden = kept
    dmo = dy.astype(jnp.bfloat16)
    part = 0.0
    g_gu, g_down = [], []
    for j, (gate, up, m) in enumerate(hidden):
        dm = dot_nt(dmo, w_down[j])
        g_down.append(dot_tn(m, dmo).astype(jnp.bfloat16))
        sig = jax.nn.sigmoid(gate)
        d_gate = (dm * up * (sig * (1.0 + gate * (1.0 - sig)))).astype(jnp.bfloat16)
        d_up = (dm * gate * sig).astype(jnp.bfloat16)
        part = part + dot_nt(d_gate, w_gu[j, 0]) + dot_nt(d_up, w_gu[j, 1])
        g_gu.append(jnp.stack([dot_tn(b, d_gate), dot_tn(b, d_up)]).astype(jnp.bfloat16))
    db = pair_sum(part)
    _, norm_back = jax.vjp(rms_norm, h, gains[1])
    dh, dg2 = norm_back(db)
    dh = dy + dh
    dao = dh.astype(jnp.bfloat16)
    do = dot_nt(dao, w_out).astype(jnp.bfloat16)
    mb = w_gu.shape[0]
    cols = w_qkv.shape[2] // mb
    g_out = dot_tn(o, dao).astype(jnp.bfloat16).reshape(mb, -1, dao.shape[1])
    dq, dk, dv, dv1 = attention_back(length, share, q, k, vu, o, do, lse, first_grad, tables)
    grads = (dq, dk, dv)
    g_qkv = jnp.stack([
        jnp.stack([dot_tn(a, g[:, j * cols:(j + 1) * cols]) for g in grads]) for j in range(mb)
    ]).astype(jnp.bfloat16)
    da = pair_sum(sum(dot_nt(g, w_qkv[i]) for i, g in enumerate(grads)))
    _, norm_back = jax.vjp(rms_norm, x.astype(jnp.float32), gains[0])
    dx, dg1 = norm_back(da)
    return dh + dx, dv1, (g_qkv, g_out, jnp.stack(g_gu), jnp.stack(g_down), jnp.stack([dg1, dg2]))


def shards(tokens, lengths, qkv_weight, out_weight, gate_up_weight, down_weight, norm_gains, cotangent):
    is_first = lax.axis_index("section") == 0
    dp, z = lax.axis_index("dp"), lax.axis_index("tensor")
    mb, rows, dim = tokens.shape
    seq_len = rows * lax.axis_size("tensor")
    share = jnp.where(is_first, 1.0, 0.5).astype(jnp.float32)[None]
    all_lengths = lax.all_gather(lengths, "dp", axis=0, tiled=True)
    length = lax.dynamic_slice_in_dim(all_lengths, dp // 2 * 2 * mb + z, 1)
    tables = tuple(jnp.asarray(t) for t in rope_tables(seq_len))

    start, w_qkv, w_out, w_gu, w_down = gather(
        tokens, cotangent, qkv_weight, out_weight, gate_up_weight, down_weight
    )
    weights = (w_qkv, w_out, w_gu, w_down, norm_gains[0])
    first = jnp.zeros((seq_len, w_qkv.shape[2]), jnp.bfloat16)
    y, v, _ = forward_layer(weights, start, first, length, share, tables)
    x = jnp.where(is_first, start, to_section(y, 1))
    first = to_section(v, 1)
    y, _, kept = forward_layer(weights, x, first, length, share, tables)

    mask = jnp.arange(seq_len)[:, None] < length
    cot = jnp.where(mask, start.astype(jnp.float32), 0.0)
    dx, dv1, _ = backward_layer(
        weights, x, kept, length, share, tables, cot, jnp.zeros_like(first)
    )
    dy = jnp.where(is_first, to_section(dx.astype(jnp.bfloat16), -1).astype(jnp.float32), cot)
    first_grad = to_section(dv1, -1)
    dx, _, grads = backward_layer(weights, x, kept, length, share, tables, dy, first_grad)
    g_qkv, g_out, g_gu, g_down, g_gain = grads
    gain = lax.psum_scatter(
        jnp.where(lax.rem(dp, 2) == 0, g_gain, 0.0), ("dp", "tensor"), scatter_dimension=1, tiled=True
    )
    o_qkv, o_out, o_gu, o_down, o_y, o_dx = scatter(
        g_qkv, g_out, g_gu, g_down, y, dx.astype(jnp.bfloat16)
    )
    return (
        o_y[None], o_dx.astype(jnp.float32)[None], o_qkv[None], o_out[None], o_gu[None], o_down[None], gain[None],
    )


def solution(mesh):
    in_specs = (
        P("dp", "tensor", None),
        P("dp"),
        P("section", None, None, "tensor"),
        P("section", "tensor", None),
        P("section", None, None, "tensor"),
        P("section", "tensor", None),
        P("section", None, None),
        P("dp", "tensor", None),
    )
    out_specs = (
        P("section", "dp", "tensor", None),
        P("section", "dp", "tensor", None),
        P("section", None, "dp", "tensor"),
        P("section", "tensor", "dp"),
        P("section", None, "dp", "tensor"),
        P("section", "tensor", "dp"),
        P("section", None, ("dp", "tensor")),
    )
    return jax.shard_map(shards, mesh=mesh, in_specs=in_specs, out_specs=out_specs, check_vma=False)
```

time: 2030 us -> 785 us (0.39)
  waiting for transfers between devices: 1350 us -> 129 us
  Pallas kernels: 0 us -> 368 us
  matrix products: 367 us -> 127 us
  other arithmetic: 197 us -> 43.8 us
    all_gather x18 -> x0, waiting for transfers between devices: 625 us -> none  [the longest x6 227 us: forward_layer(): mixed_full = lax.all_gather(mixed_in, 'tensor', axis=0, tiled=True)]
    reduce_scatter x19 -> x0, waiting for transfers between devices: 618 us -> none  [the longest x6 235 us: forward_layer(): lax.psum_scatter(jnp.dot(piece, w_out, preferred_element_type=jnp.float32...]
    pallas_call x0 -> x8, Pallas kernels: none -> 368 us  [the longest x1 175 us: scatter(): pl.pallas_call(scatter_kernel, out_shape=(*(jax.ShapeDtypeStruct(shape, f...]
    dot_general x66 -> x45, matrix products: 331 us -> 127 us  [the longest x20 63.7 us: dot_nt(): return lax.dot_general(a, b, NT, preferred_element_type=jnp.float32)]
    ppermute x8 -> x12, waiting for transfers between devices: 52.3 us -> 129 us  [the longest x4 114 us: to_section(): return lax.ppermute(values, 'section', [(0, 1)] if step > 0 else [(1, 0)])]
    convert_element_type x29 -> x7, other arithmetic: 87.1 us -> 22.4 us  [the longest x2 10.7 us: forward_layer(): y = (h + pair_sum(part)).astype(jnp.bfloat16)]
    unnamed x39 -> x2, waiting for transfers between devices: 53.1 us -> 0.02 us
    sub x3 -> x0, matrix products: 35.7 us -> none  [forward_layer(): expd = jnp.exp(scores - row_top)]
  transfers between devices with their start and end apart: 46 -> 13, of which waited for: 42 -> 7; matrix products, arithmetic and copies ran while one was open for 17% -> 10% of each run, Pallas kernels for 0% -> 23%
where the time goes in v1:
time: 785 us; the launch traced here: 776 us
  Pallas kernels  368 us (47%)
  waiting for transfers between devices  129 us (16%)
  matrix products  127 us (16%)
  other arithmetic  43.8 us (6%)
  local copies, waits for them, and re-layouts  43.5 us (6%)
  starting transfers between devices  43.1 us (5%)
  between operations  15.9 us (2%)
    pallas_call x1, Pallas kernels, scatter(): pl.pallas_call(scatter_kernel, out_shape=(*(jax.ShapeDtypeStruct(shape, f...  175 us
    ppermute x4, waiting for transfers between devices, to_section(): return lax.ppermute(values, 'section', [(0, 1)] if step > 0 else [(1, 0)])  114 us
    pallas_call x1, Pallas kernels, gather(): pl.pallas_call(gather_kernel, out_shape=(jax.ShapeDtypeStruct((rows * n_t...  109 us
    dot_general x20, matrix products, dot_nt(): return lax.dot_general(a, b, NT, preferred_element_type=jnp.float32)  63.7 us
    dot_general x12, matrix products, dot(): return jnp.dot(a, b, preferred_element_type=jnp.float32)  41.6 us
    unnamed x177, local copies, waits for them, and re-layouts  41.5 us
    pallas_call x2, Pallas kernels, attention_back(): pl.pallas_call(attention_back_kernel, grid=(pairs,), in_specs=[smem, smem...  40.7 us
    ppermute x8, starting transfers between devices, pair_sum(): theirs = lax.ppermute(mine, 'dp', swap)  35 us
  transfers between devices with their start and end apart: 13, of which 7 were waited for; matrix products, arithmetic and copies ran while one was open for 10% of the time, Pallas kernels for 23%

profile of v1, /device:TPU:0, one launch (start us, length us, event | category | flops | bytes accessed | tf_op | source)
XLA Modules:
  0.0 775.9 jit_solution(12560369007611727774)
XLA Ops:
  10.0 6.3 all-reduce
  17.7 4.7 copy.32.gu
  29.8 108.8 %gather_weights.1 = (bf16[1024,1024]{1,0:T(8,128)(2,1)S(1)}, bf16[3,1024,512]{2,1,0:T(8,128)(2,1)S(1)}, bf16[512,1024]{1,0:T(8,128)(2,1)S(1)}, bf16[2,2,1024,704...) custom-call(bf16[2,256,1024]{2,1,0:T(8,128)(2,1)S(1)} %copy-done.8, bf16[2,256,1024]{2,1,0:T(8,128)(2,1)S(1)} %copy-done.9, ...), custom_call_target="tpu_custom_call" | custom-call | tf_op jit(solution)/shard_map/gather_weights/pallas_call | solution.py:219
  141.5 5.7 project_qkv.2
  154.8 16.7 %attention.2 = (bf16[1024,512]{1,0:T(8,128)(2,1)S(1)}, f32[4,2,1024]{2,1,0:T(2,128)}) custom-call(s32[1]{0:T(128)} %dynamic_slice.3.length, bf16[1024,512]{1,0:T(8,128)(2,1)S(1)} %copy-done.38, bf16[1024,512]{1,0:T(8,128)(2,1)S(1)} %copy-done.40, bf16[1024,512]{1,0:T(8,128)(2,1)S(1)} %copy-done.42), custom_call_target="tpu_custom_call" | custom-call | flops 4294967296 | bytes 4194304 | tf_op jit(solution)/shard_map/attention/pallas_call | solution.py:660
  172.7 33.0 %collective-permute-start = (bf16[1024,1024]{1,0:T(8,128)(2,1)S(1)}, bf16[1024,1024]{1,0:T(8,128)(2,1)S(1)}, u32[]{:S(2)}, u32[]{:S(2)}) collective-permute-start(bf16[1024,1024]{1,0:T(8,128)(2,1)S(1)} %convolution_convert_fusion.1), channel_id=1, source_target_pairs={{0,4},{4,0},{8,12},{12,8},{1,5},{5,1},{9,13},{13,9},{2,6},{6,2},{1... | collective-permute-start | bytes 6291464 | tf_op jit(solution)/shard_map/ppermute | solution.py:759
  205.7 3.8 collective-permute-done
  218.5 9.0 %fusion.67 = f32[1024,1024]{1,0:T(8,128)} fusion(f32[1024,704]{0,1:T(8,128)} %fusion.44, bf16[1024,1024]{1,0:T(8,128)(2,1)} %copy-done.52, bf16[2,2,1024,704]{3,2,1,0:T(8,128)(2,1)} %copy-done.12, bf16[2,704,1024]{2,1,0:T(8,128)(2,1)} %copy-done.13), kind=kOutput, calls=%fused_computation.129 | convolution fusion | flops 2957115392 | bytes 12189696 | tf_op jit(solution)/shard_map/dot_general | solution.py:768
  227.5 9.8 %add_convert_fusion.7 = bf16[1024,1024]{1,0:T(8,128)(2,1)} fusion(f32[1024,1024]{1,0:T(8,128)} %fusion.67, f32[1024,704]{0,1:T(8,128)} %fusion.29, bf16[1024,1024]{1,0:T(8,128)(2,1)} %copy-done.52, bf16[2,2,1024,704]{3,2,1,0:T(8,128)(2,1)} %copy-done.12, bf16[2,704,1024]{2,1,0:T(8,128)(2,1)} %copy-done.13), kind=kOutput, calls=%fused_computation.43 | convolution fusion | flops 2959212544 | bytes 14286848 | tf_op jit(solution)/shard_map/dot_general | solution.py:768
  237.7 4.0 collective-permute-done.1
  241.6 5.4 add_convert_fusion.6
  247.0 3.6 collective-permute-start.2
  252.3 44.1 %collective-permute-done.2 = bf16[1024,1024]{1,0:T(8,128)(2,1)S(1)} collective-permute-done((bf16[1024,1024]{1,0:T(8,128)(2,1)S(1)}, bf16[1024,1024]{1,0:T(8,128)(2,1)S(1)}, u32[]{:S(2)}, u32[]{:S(2)}) %collective-permute-start.2) | collective-permute-done | bytes 2097184 | tf_op jit(solution)/shard_map/ppermute | solution.py:764
  296.7 21.7 %collective-permute-done.3.first = bf16[1024,512]{1,0:T(8,128)(2,1)S(1)} collective-permute-done((bf16[1024,512]{1,0:T(8,128)(2,1)S(1)}, bf16[1024,512]{1,0:T(8,128)(2,1)S(1)}, u32[]{:S(2)}, u32[]{:S(2)}) %collective-permute-start.3) | collective-permute-done | bytes 1048608 | tf_op jit(solution)/shard_map/ppermute | solution.py:764
  318.4 5.3 project_qkv.3
  329.8 15.8 %attention.3 = (bf16[1024,512]{1,0:T(8,128)(2,1)S(1)}, f32[4,2,1024]{2,1,0:T(2,128)S(1)}) custom-call(s32[1]{0:T(128)} %dynamic_slice.3.length, bf16[1024,512]{1,0:T(8,128)(2,1)S(1)} %copy-done.33, bf16[1024,512]{1,0:T(8,128)(2,1)S(1)} %copy-done.35, bf16[1024,512]{1,0:T(8,128)(2,1)S(1)} %get-tuple-element.49.v), custom_call_target="tpu_custom_call" | custom-call | flops 4294967296 | bytes 4194304 | tf_op jit(solution)/shard_map/attention/pallas_call | solution.py:660
  364.6 7.2 fusion.33
  371.8 6.5 fusion.40
  378.3 4.5 fusion.25
  382.8 8.2 %add_convert_fusion.5 = bf16[1024,1024]{1,0:T(8,128)(2,1)S(1)} fusion(f32[1024,1024]{1,0:T(8,128)} %fusion.25, f32[1024,1024]{1,0:T(8,128)} %fusion.40, f32[1024,1024]{1,0:T(8,128)} %fusion.33, f32[1024,704]{0,1:T(8,128)} %copy-done.69, f32[1024,704]{0,1:T(8,128)} %copy-done.67, bf16[2,2,1024,704]{3,2,1,0:T(8,128)(2,1)S(1)} %bitcast.176), kind=kOutput, calls=%fused_computation.39 | convolution fusion | flops 1484914688 | bytes 22020096 | tf_op jit(solution)/shard_map/dot_general | solution.py:772
  391.4 3.8 collective-permute-done.5
  400.4 19.8 %attention_back.2 = (bf16[1024,512]{1,0:T(8,128)(2,1)S(1)}, bf16[1024,512]{1,0:T(8,128)(2,1)S(1)}, bf16[1024,512]{1,0:T(8,128)(2,1)S(1)}, bf16[1024,512]{1,0:T(8,128)(2,1)S(1)}) custom-call(s32[1]{0:T(128)} %dynamic_slice.3.length, f32[1]{0:T(128)} %bitcast.share, bf16[1024,512]{1,0:T(8,128)(2,1)} %copy-done.32, bf16[1024,512]{1,0:T(8,128)(2,1)} %copy-done.34, ...), custom_call_target="tpu_custom_call" | custom-call | flops 10737418240 | bytes 10485760 | tf_op jit(solution)/shard_map/attention_back/pallas_call | solution.py:739
  424.6 3.8 collective-permute-done.6
  436.3 47.8 %collective-permute-done.7 = bf16[1024,1024]{1,0:T(8,128)(2,1)} collective-permute-done((bf16[1024,1024]{1,0:T(8,128)(2,1)}, bf16[1024,1024]{1,0:T(8,128)(2,1)}, u32[]{:S(2)}, u32[]{:S(2)}) %collective-permute-start.7) | collective-permute-done | bytes 2097184 | tf_op jit(solution)/shard_map/ppermute | solution.py:764
  486.4 6.1 multiply_convert_fusion.2
  492.5 4.4 multiply_convert_fusion.3
  511.7 3.5 add_convert_fusion.3
  528.8 4.0 maximum_maximum_fusion.g_gu
  534.3 5.3 add_convert_fusion.1
  542.0 20.9 %attention_back.3 = (bf16[1024,512]{1,0:T(8,128)(2,1)S(1)}, bf16[1024,512]{1,0:T(8,128)(2,1)S(1)}, bf16[1024,512]{1,0:T(8,128)(2,1)S(1)}, bf16[1024,512]{1,0:T(8,128)(2,1)}) custom-call(s32[1]{0:T(128)} %dynamic_slice.3.length, f32[1]{0:T(128)} %bitcast.share, bf16[1024,512]{1,0:T(8,128)(2,1)} %copy-done.32, bf16[1024,512]{1,0:T(8,128)(2,1)} %copy-done.34, ...), custom_call_target="tpu_custom_call" | custom-call | flops 10737418240 | bytes 10485760 | tf_op jit(solution)/shard_map/attention_back/pallas_call | solution.py:739
  579.4 5.2 fusion.7.dx
  584.6 174.8 %scatter_grads.1 = (f32[3,256,256]{2,1,0:T(8,128)}, f32[256,256]{1,0:T(8,128)}, f32[2,256,704]{2,1,0:T(8,128)}, f32[704,256]{1,0:T(8,128)}, bf16[2,256,1024]{2,1...) custom-call(bf16[2,3,1024,256]{3,2,1,0:T(8,128)(2,1)} %pad_maximum_fusion.g_qkv, bf16[2,256,1024]{2,1,0:T(8,128)(2,1)} %bitcast.181, ...), custom_call_target="tpu_custom_call" | custom-call | tf_op jit(solution)/shard_map/scatter_grads/pallas_call | solution.py:506
  (259 shorter events, 136.5 us)
Async XLA Ops:
  7.2 756.8 %reduce-scatter.4.cloned.1.call-start = ((), (), s32[]{:S(2)}) async-start(), calls=%async_computation.1 | async-start | bytes 557056
  29.8 111.6 %copy-start.21 = (f32[1024,128]{1,0:T(8,128)S(1)}, f32[1024,128]{1,0:T(8,128)}, u32[]{:S(2)}) copy-start(f32[1024,128]{1,0:T(8,128)} %constant.64.clone.sin) | copy-start | bytes 1572868
  29.8 111.6 %copy-start.25 = (f32[1024,128]{1,0:T(8,128)S(1)}, f32[1024,128]{1,0:T(8,128)}, u32[]{:S(2)}) copy-start(f32[1024,128]{1,0:T(8,128)} %constant.63.clone.cos) | copy-start | bytes 1572868
  141.4 73.9 %copy-start.12 = (bf16[2,2,1024,704]{3,2,1,0:T(8,128)(2,1)}, bf16[2,2,1024,704]{3,2,1,0:T(8,128)(2,1)S(1)}, u32[]{:S(2)}) copy-start(bf16[2,2,1024,704]{3,2,1,0:T(8,128)(2,1)S(1)} %get-tuple-element.43) | copy-start | bytes 17301508
  154.8 16.7 %copy-start.17 = (bf16[512,1024]{1,0:T(8,128)(2,1)S(1)}, bf16[512,1024]{1,0:T(8,128)(2,1)}, u32[]{:S(2)}) copy-start(bf16[512,1024]{1,0:T(8,128)(2,1)} %copy-done.16) | copy-start | bytes 3145732
  172.7 37.8 %copy-start.46 = (bf16[1024,1024]{1,0:T(8,128)(2,1)}, bf16[1024,1024]{1,0:T(8,128)(2,1)S(1)}, u32[]{:S(2)}) copy-start(bf16[1024,1024]{1,0:T(8,128)(2,1)S(1)} %convolution_convert_fusion.1) | copy-start | bytes 6291460
  172.7 36.8 %collective-permute-start = (bf16[1024,1024]{1,0:T(8,128)(2,1)S(1)}, bf16[1024,1024]{1,0:T(8,128)(2,1)S(1)}, u32[]{:S(2)}, u32[]{:S(2)}) collective-permute-start(bf16[1024,1024]{1,0:T(8,128)(2,1)S(1)} %convolution_convert_fusion.1), channel_id=1, source_target_pairs={{0,4},{4,0},{8,12},{12,8},{1,5},{5,1},{9,13},{13,9},{2,6},{6,2},{1... | collective-permute-start | bytes 6291464 | tf_op jit(solution)/shard_map/ppermute | solution.py:759
  237.3 4.4 collective-permute-start.1
  247.0 49.4 %collective-permute-start.2 = (bf16[1024,1024]{1,0:T(8,128)(2,1)S(1)}, bf16[1024,1024]{1,0:T(8,128)(2,1)S(1)}, u32[]{:S(2)}, u32[]{:S(2)}) collective-permute-start(bf16[1024,1024]{1,0:T(8,128)(2,1)S(1)} %add_convert_fusion.6), channel_id=1, source_target_pairs={{0,16},{1,17},{2,18},{3,19},{4,20},{5,21},{6,22},{7,23},{8,24},{9,... | collective-permute-start | bytes 6291464 | tf_op jit(solution)/shard_map/ppermute | solution.py:764
  250.7 67.7 %copy-start.6 = (bf16[3,1024,512]{2,1,0:T(8,128)(2,1)S(1)}, bf16[3,1024,512]{2,1,0:T(8,128)(2,1)}, u32[]{:S(2)}) copy-start(bf16[3,1024,512]{2,1,0:T(8,128)(2,1)} %copy-done.5) | copy-start | bytes 9437188
  250.7 67.7 %copy-start.22 = (f32[1024,128]{1,0:T(8,128)S(1)}, f32[1024,128]{1,0:T(8,128)}, u32[]{:S(2)}) copy-start(f32[1024,128]{1,0:T(8,128)} %constant.64.clone.sin) | copy-start | bytes 1572868
  250.7 67.7 %copy-start.26 = (f32[1024,128]{1,0:T(8,128)S(1)}, f32[1024,128]{1,0:T(8,128)}, u32[]{:S(2)}) copy-start(f32[1024,128]{1,0:T(8,128)} %constant.63.clone.cos) | copy-start | bytes 1572868
  250.7 67.7 %collective-permute-start.3 = (bf16[1024,512]{1,0:T(8,128)(2,1)S(1)}, bf16[1024,512]{1,0:T(8,128)(2,1)S(1)}, u32[]{:S(2)}, u32[]{:S(2)}) collective-permute-start(bf16[1024,512]{1,0:T(8,128)(2,1)S(1)} %copy-done.20), channel_id=1, source_target_pairs={{0,16},{1,17},{2,18},{3,19},{4,20},{5,21},{6,22},{7,23},{8,24},{9,... | collective-permute-start | bytes 3145736 | tf_op jit(solution)/shard_map/ppermute | solution.py:764
  296.7 133.1 %copy-start = (bf16[1024,1024]{1,0:T(8,128)(2,1)}, bf16[1024,1024]{1,0:T(8,128)(2,1)S(1)}, u32[]{:S(2)}) copy-start(bf16[1024,1024]{1,0:T(8,128)(2,1)S(1)} %broadcast_select_fusion.x) | copy-start | bytes 6291460
  327.0 18.6 %copy-start.36 = (bf16[1024,512]{1,0:T(8,128)(2,1)}, bf16[1024,512]{1,0:T(8,128)(2,1)S(1)}, u32[]{:S(2)}) copy-start(bf16[1024,512]{1,0:T(8,128)(2,1)S(1)} %get-tuple-element.49.v) | copy-start | bytes 3145732
  346.9 6.1 collective-permute-start.4
  352.9 25.4 %copy-start.69 = (f32[1024,704]{0,1:T(8,128)}, f32[1024,704]{0,1:T(8,128)S(1)}, u32[]{:S(2)}) copy-start(f32[1024,704]{0,1:T(8,128)S(1)} %fusion.58) | copy-start | bytes 8650756
  354.0 42.2 %copy-start.43 = (f32[1024,1024]{1,0:T(8,128)}, f32[1024,1024]{1,0:T(8,128)S(1)}, u32[]{:S(2)}) copy-start(f32[1024,1024]{1,0:T(8,128)S(1)} %get-tuple-element.86) | copy-start | bytes 12582916
  357.8 20.5 %copy-start.67 = (f32[1024,704]{0,1:T(8,128)}, f32[1024,704]{0,1:T(8,128)S(1)}, u32[]{:S(2)}) copy-start(f32[1024,704]{0,1:T(8,128)S(1)} %fusion.27) | copy-start | bytes 8650756
  391.0 4.2 collective-permute-start.5
  424.2 4.2 collective-permute-start.6
  433.4 50.6 %collective-permute-start.7 = (bf16[1024,1024]{1,0:T(8,128)(2,1)}, bf16[1024,1024]{1,0:T(8,128)(2,1)}, u32[]{:S(2)}, u32[]{:S(2)}) collective-permute-start(bf16[1024,1024]{1,0:T(8,128)(2,1)} %fusion.4), channel_id=1, source_target_pairs={{16,0},{17,1},{18,2},{19,3},{20,4},{21,5},{22,6},{23,7},{24,8},{25... | collective-permute-start | bytes 6291464 | tf_op jit(solution)/shard_map/ppermute | solution.py:764
  434.7 51.6 %copy-start.15 = (bf16[2,704,1024]{2,1,0:T(8,128)(2,1)S(1)}, bf16[2,704,1024]{2,1,0:T(8,128)(2,1)}, u32[]{:S(2)}) copy-start(bf16[2,704,1024]{2,1,0:T(8,128)(2,1)} %copy-done.13) | copy-start | bytes 8650756
  434.7 51.6 %copy-start.68 = (f32[1024,704]{0,1:T(8,128)S(1)}, f32[1024,704]{0,1:T(8,128)}, u32[]{:S(2)}) copy-start(f32[1024,704]{0,1:T(8,128)} %copy-done.67) | copy-start | bytes 8650756
  434.7 107.3 %collective-permute-start.9 = (bf16[1024,512]{1,0:T(8,128)(2,1)}, bf16[1024,512]{1,0:T(8,128)(2,1)}, u32[]{:S(2)}, u32[]{:S(2)}) collective-permute-start(bf16[1024,512]{1,0:T(8,128)(2,1)} %copy-done.18), channel_id=1, source_target_pairs={{16,0},{17,1},{18,2},{19,3},{20,4},{21,5},{22,6},{23,7},{24,8},{25... | collective-permute-start | bytes 3145736 | tf_op jit(solution)/shard_map/ppermute | solution.py:764
  486.4 13.7 %slice-start.2 = ((s8[6291456]{0:T(1024)(128)(4,1)}), s8[4194304]{0:T(1024)(128)(4,1)S(1)}, s32[]{:S(2)}) async-start(s8[6291456]{0:T(1024)(128)(4,1)} %bitcast.177), calls=%async_computation.4 | async-start | bytes 8388608
  492.5 14.3 %copy-start.61 = (bf16[1024,704]{0,1:T(8,128)(2,1)}, bf16[1024,704]{0,1:T(8,128)(2,1)S(1)}, u32[]{:S(2)}) copy-start(bf16[1024,704]{0,1:T(8,128)(2,1)S(1)} %get-tuple-element.92) | copy-start | bytes 4325380
  515.2 17.5 %collective-permute-start.8 = (bf16[1024,1024]{1,0:T(8,128)(2,1)S(1)}, bf16[1024,1024]{1,0:T(8,128)(2,1)S(1)}, u32[]{:S(2)}, u32[]{:S(2)}) collective-permute-start(bf16[1024,1024]{1,0:T(8,128)(2,1)S(1)} %add_convert_fusion.3), channel_id=1, source_target_pairs={{0,4},{4,0},{8,12},{12,8},{1,5},{5,1},{9,13},{13,9},{2,6},{6,2},{1... | collective-permute-start | bytes 6291464 | tf_op jit(solution)/shard_map/ppermute | solution.py:759
  520.7 13.6 %collective-permute-start.10 = (bf16[1024,1024]{1,0:T(8,128)(2,1)S(1)}, bf16[1024,1024]{1,0:T(8,128)(2,1)S(1)}, u32[]{:S(2)}, u32[]{:S(2)}) collective-permute-start(bf16[1024,1024]{1,0:T(8,128)(2,1)S(1)} %add_convert_fusion.2), channel_id=1, source_target_pairs={{0,4},{4,0},{8,12},{12,8},{1,5},{5,1},{9,13},{13,9},{2,6},{6,2},{1... | collective-permute-start | bytes 6291464 | tf_op jit(solution)/shard_map/ppermute | solution.py:759
  539.6 34.7 %copy-start.48 = (f32[1024,1024]{1,0:T(8,128)}, f32[1024,1024]{1,0:T(8,128)S(1)}, u32[]{:S(2)}) copy-start(f32[1024,1024]{1,0:T(8,128)S(1)} %get-tuple-element.94) | copy-start | bytes 12582916
  542.0 20.9 %copy-start.7 = (bf16[3,1024,512]{2,1,0:T(8,128)(2,1)S(1)}, bf16[3,1024,512]{2,1,0:T(8,128)(2,1)}, u32[]{:S(2)}) copy-start(bf16[3,1024,512]{2,1,0:T(8,128)(2,1)} %copy-done.5) | copy-start | bytes 9437188
  567.9 8.6 %collective-permute-start.11 = (bf16[1024,1024]{1,0:T(8,128)(2,1)S(1)}, bf16[1024,1024]{1,0:T(8,128)(2,1)S(1)}, u32[]{:S(2)}, u32[]{:S(2)}) collective-permute-start(bf16[1024,1024]{1,0:T(8,128)(2,1)S(1)} %add_convert_fusion), channel_id=1, source_target_pairs={{0,4},{4,0},{8,12},{12,8},{1,5},{5,1},{9,13},{13,9},{2,6},{6,2},{1... | collective-permute-start | bytes 6291464 | tf_op jit(solution)/shard_map/ppermute | solution.py:759
  (64 other events, 220.6 us)
Sparse Core Ops, SparseCore 0:
  579.5 60.2 reduce-scatter.3

commit v2 on v1

v2 whole, which is shorter than its diff:
```python
import jax
import jax.numpy as jnp
import numpy as np
from jax import lax
from jax.experimental import pallas as pl
from jax.experimental.pallas import tpu as pltpu
from jax.sharding import PartitionSpec as P

MESH = pl.DeviceIdType.MESH
ANY = pl.BlockSpec(memory_space=pl.ANY)
VMEM = pl.BlockSpec(memory_space=pltpu.VMEM)
NORM_EPS = 1e-6
ROPE_BASE = 10000.0
SCORE_SCALE = 0.125
MASK_VALUE = -1e30
HD = 64
PAIR = 2 * HD
CHUNKS = 4
NT = (((1,), (1,)), ((), ()))
BF, F32 = jnp.bfloat16, jnp.float32

QKV, OUT, GU, DOWN = range(4)
COUNT = (2, 1, 4, 2)
BASE = (0, 2, 3, 7)
N_PIECES = 9


def dot(a, b):
    return jnp.dot(a, b, preferred_element_type=F32)


def dot_nt(a, b):
    return lax.dot_general(a, b, NT, preferred_element_type=F32)


def dot_tn(a, b):
    return lax.dot_general(a, b, (((0,), (0,)), ((), ())), preferred_element_type=F32)


def remote(src, dst, send, recv, to):
    return pltpu.make_async_remote_copy(
        src_ref=src, dst_ref=dst, send_sem=send, recv_sem=recv, device_id=to, device_id_type=MESH
    )


class Place:
    def __init__(self, mb):
        self.n_t = lax.axis_size("tensor")
        self.nx = lax.axis_size("dp") // 2
        self.section = lax.axis_index("section")
        dp = lax.axis_index("dp")
        self.z = lax.axis_index("tensor")
        self.x, self.c = dp // 2, lax.rem(dp, 2)
        self.here = self.z // mb == self.c
        self.jz = self.z - self.c * mb
        self.sibling = {"dp": 2 * self.x + 1 - self.c}
        self.right, self.left = {"tensor": self.z + 1}, {"tensor": self.z - 1}

    def at_x(self, d):
        return {"dp": 2 * lax.rem(self.x + d, self.nx) + self.c}

    def meet(self):
        barrier = pltpu.get_barrier_semaphore()
        partners = [{"tensor": lax.rem(self.z + k, self.n_t)} for k in range(1, self.n_t)]
        partners += [self.at_x(k) for k in range(1, self.nx)]
        partners += [self.sibling, {"section": 1 - self.section}]
        for partner in partners:
            pl.semaphore_signal(barrier, inc=1, device_id=partner, device_id_type=MESH)
        pl.semaphore_wait(barrier, len(partners))


def rope_tables(positions):
    lane = np.arange(PAIR)
    frequency = ROPE_BASE ** (-(lane % (HD // 2)) * 2.0 / HD)
    angles = np.arange(positions)[:, None] * frequency[None, :]
    sign = np.where(lane % HD < HD // 2, -1.0, 1.0)
    return np.cos(angles).astype(np.float32), (np.sin(angles) * sign).astype(np.float32)


def rotate_pair(values, cos, sin):
    lane = lax.broadcasted_iota(jnp.int32, values.shape, 1)
    partner = jnp.where(
        lax.rem(lane, HD) < HD // 2,
        pltpu.roll(values, PAIR - HD // 2, 1),
        pltpu.roll(values, HD // 2, 1),
    )
    return values * cos + partner * sin


def normalise(values):
    return values * lax.rsqrt(jnp.mean(values * values, axis=-1, keepdims=True) + NORM_EPS)


def head_views(h, shape):
    lane = lax.broadcasted_iota(jnp.int32, shape, 1)
    return lane // HD == h, lane == (1 - h) * HD


def key_bias(length, shape):
    key = lax.broadcasted_iota(jnp.int32, shape, 0).astype(F32)
    return jnp.where(key < length, 0.0, MASK_VALUE)


def causal_block(blk):
    key = lax.broadcasted_iota(jnp.int32, (blk, blk), 0)
    query = lax.broadcasted_iota(jnp.int32, (blk, blk), 1)
    return key <= query


def attend(queries, keys, vals, length, put_out, put_lse):
    seq = queries.shape[0]
    blk = seq // CHUNKS
    v_t = vals.astype(F32).T.astype(BF)
    keys, queries = keys.astype(F32), queries.astype(F32)
    bias = key_bias(length, keys.shape)
    visible = causal_block(blk)
    heads = []
    for h in range(2):
        inside, extra = head_views(h, keys.shape)
        heads.append((
            jnp.where(inside, keys, jnp.where(extra, bias, 0.0)).astype(BF),
            jnp.where(inside, queries, jnp.where(extra, 1.0, 0.0)).astype(BF),
            v_t[h * HD:(h + 1) * HD],
        ))
    for i in range(CHUNKS):
        lo, hi = i * blk, (i + 1) * blk
        parts = []
        for h in range(2):
            kh, qh, vh = heads[h]
            qi = qh[lo:hi]
            s_diag = jnp.where(visible, dot_nt(kh[lo:hi], qi), MASK_VALUE)
            top = jnp.max(s_diag, axis=0, keepdims=True)
            if i:
                s_full = dot_nt(kh[:lo], qi)
                top = jnp.maximum(top, jnp.max(s_full, axis=0, keepdims=True))
            p_diag = jnp.exp(s_diag - top)
            total = jnp.sum(p_diag, axis=0, keepdims=True)
            acc = dot(vh[:, lo:hi], p_diag.astype(BF))
            if i:
                p_full = jnp.exp(s_full - top)
                total = total + jnp.sum(p_full, axis=0, keepdims=True)
                acc = acc + dot(vh[:, :lo], p_full.astype(BF))
            parts.append(acc / total)
            put_lse(h, lo, hi, top + jnp.log(total))
        put_out(lo, hi, jnp.concatenate(parts, axis=0).T.astype(BF))


def forward_kernel(
    tok, cot, lens, qkv, out, gu, down, gains, cos, sin,
    x_o, cot_o, y_o, wq_o, wo_o, wg_o, wd_o, a_o, q_o, k_o, vu_o, o_o, lse_o, h_o, b_o, g_o, u_o, m_o, len_o,
    w_qkv, w_out, w_gu, w_down, x_v, first, a_v, q_v, k_v, v_v, vu_v, o_v, lse_v, h_v, b_v, g_v, u_v, m_v,
    acc, s1, r1, r2, len_v,
    loc, a2a_s, a2a_r, sib, own_r, own_l, z_r, z_f, x_s, x_r, hop, hsib, e1, e2, vsem, lsem, outs,
):
    mb, block_rows, dim = tok.shape
    me = Place(mb)
    x, c, z, n_t, nx, jz = me.x, me.c, me.z, me.n_t, me.nx, me.jz
    part = dim // nx
    cols, ow, half = qkv.shape[3], out.shape[1], down.shape[1] // 2
    seq = x_v.shape[0]
    rows = seq // CHUNKS
    pairs = q_v.shape[0]
    first_plane, second_plane = me.section == 0, me.section == 1
    me.meet()

    def column(p):
        return pl.ds(pl.multiple_of(p * part, 128), part)

    def shard_part(w, n, p):
        if w == QKV:
            return qkv.at[0, :, pl.ds(pl.multiple_of(p * part + n * (part // 2), 16), part // 2), :]
        if w == OUT:
            return out.at[0, :, column(p)]
        if w == GU:
            return gu.at[0, n // 2, pl.ds(pl.multiple_of(lax.rem(n, 2) * half, 16), half), column(p)]
        return down.at[0, pl.ds(n * half, half), column(p)]

    def slot_part(w, n, j, p):
        if w == QKV:
            return w_qkv.at[j, :, pl.ds(pl.multiple_of(p * part + n * (part // 2), 16), part // 2), :]
        if w == OUT:
            return w_out.at[pl.ds(pl.multiple_of(j * ow, 16), ow), column(p)]
        if w == GU:
            return w_gu.at[j, n // 2, pl.ds(pl.multiple_of(lax.rem(n, 2) * half, 16), half), column(p)]
        return w_down.at[j, pl.ds(n * half, half), column(p)]

    own_slots = (
        (qkv.at[0], w_qkv.at[jz]),
        (out.at[0], w_out.at[pl.ds(pl.multiple_of(jz * ow, 16), ow), :]),
        (gu.at[0], w_gu.at[jz]),
        (down.at[0], w_down.at[jz]),
    )

    def own_copies(w, n):
        k = BASE[w] + n
        src, dst = shard_part(w, n, x), slot_part(w, n, jz, x)
        return (
            (z < n_t - 1, remote(src, dst, own_r.at[k], z_r.at[k, jz], me.right)),
            (z > 0, remote(src, dst, own_l.at[k], z_r.at[k, jz], me.left)),
        )

    def own_start(w, n):
        @pl.when(me.here)
        def _():
            for there, copy in own_copies(w, n):
                pl.when(there)(copy.start)

    def own_wait(w, n):
        @pl.when(me.here)
        def _():
            for there, copy in own_copies(w, n):
                pl.when(there)(copy.wait_send)

    def order(i):
        return jnp.where(c == 0, mb - 1 - i, i)

    def foreign(w, n, i):
        j = order(i)
        s = c * mb + j
        k = BASE[w] + n

        @pl.when(s != z)
        def _():
            piece = slot_part(w, n, j, x)
            to_right = remote(piece, piece, z_f.at[k, j], z_r.at[k, j], me.right)
            to_left = remote(piece, piece, z_f.at[k, j], z_r.at[k, j], me.left)
            to_right.wait_recv()
            pl.when((s < z) & (z < n_t - 1))(to_right.start)
            pl.when((s > z) & (z > 0))(to_left.start)
            for d in range(1, nx):
                remote(piece, piece, x_s.at[k, j, d], x_r.at[k, j, x], me.at_x(d)).start()

    def wait_slot(w, j):
        s = c * mb + j

        @pl.when(s != z)
        def _():
            for n in range(COUNT[w]):
                k = BASE[w] + n
                for d in range(1, nx):
                    p = lax.rem(x + d, nx)
                    piece = slot_part(w, n, j, p)
                    remote(piece, piece, x_s.at[k, j, d], x_r.at[k, j, p], me.right).wait_recv()

    def gu_step(n, i):
        if i == 0:
            @pl.when(n >= 2)
            def _():
                own_wait(GU, n - 2)
            own_start(GU, n)
        foreign(GU, n, i)

    def down_steps(i):
        for n in range(COUNT[DOWN]):
            if i == 0:
                own_wait(GU, n + 2)
                own_start(DOWN, n)
            foreign(DOWN, n, i)

    block = pl.ds(pl.multiple_of(z * block_rows, 128), block_rows)
    for plane, source, target in ((first_plane, tok, x_v), (second_plane, cot, cot_o)):
        for i in range(mb):
            zt = c * mb + i

            @pl.when(plane & (zt != z))
            def _(source=source, target=target, i=i, zt=zt):
                remote(source.at[i], target.at[block, :], a2a_s.at[i], a2a_r.at[z], {"tensor": zt}).start()

            @pl.when(plane & (zt == z))
            def _(source=source, target=target, i=i):
                pltpu.make_async_copy(source.at[i], target.at[block, :], loc.at[4]).start()

    @pl.when(me.here)
    def _():
        remote(lens.at[jz], len_v, lsem.at[0], lsem.at[1], me.sibling).start()
        len_v[...] = lens[jz]
        for w, (src, dst) in enumerate(own_slots):
            pltpu.make_async_copy(src, dst, loc.at[w]).start()

    own_start(QKV, 0)
    own_start(QKV, 1)
    for w, n in ((QKV, 0), (QKV, 1), (OUT, 0)):
        if w == OUT:
            own_wait(QKV, 0)
            own_start(OUT, 0)
        for i in range(mb):
            foreign(w, n, i)
        if (w, n) == (QKV, 0):
            for plane, target in ((first_plane, x_v), (second_plane, cot_o)):
                @pl.when(plane & me.here)
                def _(target=target):
                    for zs in range(n_t):
                        there = target.at[pl.ds(zs * block_rows, block_rows), :]

                        @pl.when(zs != z)
                        def _(zs=zs, there=there):
                            remote(there, there, a2a_s.at[0], a2a_r.at[zs], me.right).wait_recv()

                    pltpu.make_async_copy(tok.at[0], target.at[block, :], loc.at[4]).wait()
                    remote(target, target, sib.at[0], sib.at[1], me.sibling).start()

    @pl.when(second_plane)
    def _():
        for i in range(mb):
            @pl.loop(0, COUNT[GU])
            def _(n):
                gu_step(n, i)
            down_steps(i)

    @pl.when(jnp.logical_not(me.here))
    def _():
        remote(len_v, len_v, lsem.at[0], lsem.at[1], me.sibling).wait_recv()
        pl.when(first_plane)(remote(x_v, x_v, sib.at[0], sib.at[1], me.sibling).wait_recv)

    length = len_v[0:1, :]

    @pl.when(me.here)
    def _():
        for w, (src, dst) in enumerate(own_slots):
            pltpu.make_async_copy(src, dst, loc.at[w]).wait()

    for j in range(mb):
        wait_slot(QKV, j)
        wait_slot(OUT, j)

    pl.when(second_plane)(remote(first, first, vsem.at[0], vsem.at[1], me.sibling).wait_recv)
    gain_one, gain_two = gains[0:1, :], gains[1:2, :]

    def chunk(r):
        return pl.ds(pl.multiple_of(r * rows, 128), rows)

    def halves(r, core):
        return x_v.at[pl.ds(pl.multiple_of(r * rows + core * (rows // 2), 16), rows // 2), :]

    @pl.loop(0, CHUNKS)
    def _(r):
        @pl.when(second_plane)
        def _():
            mine, theirs = halves(r, c), halves(r, 1 - c)
            remote(mine, mine, hop.at[0, r], hop.at[1, r], me.sibling).wait_recv()
            remote(mine, mine, hsib.at[0, r], hsib.at[1, r], me.sibling).start()
            remote(theirs, theirs, hsib.at[0, r], hsib.at[1, r], me.sibling).wait_recv()

        at = chunk(r)
        a = (normalise(x_v[at, :].astype(F32)) * gain_one).astype(BF)
        a_v[at, :] = a
        cos_r, sin_r = cos[at, :], sin[at, :]
        for j in range(mb):
            q = dot(a, w_qkv[j, 0])
            k = dot(a, w_qkv[j, 1])
            v = dot(a, w_qkv[j, 2])
            for n in range(cols // PAIR):
                p = j * (cols // PAIR) + n
                lanes = slice(n * PAIR, (n + 1) * PAIR)
                q_v[p, at, :] = (rotate_pair(q[:, lanes], cos_r, sin_r) * SCORE_SCALE).astype(BF)
                k_v[p, at, :] = rotate_pair(k[:, lanes], cos_r, sin_r).astype(BF)
                v_v[p, at, :] = v[:, lanes].astype(BF)

    @pl.when(first_plane)
    def _():
        remote(v_v, first, vsem.at[0], vsem.at[1], {"section": 1 - me.section}).start()

        @pl.loop(0, pairs)
        def _(p):
            vu_v[p] = v_v[p]

    @pl.when(second_plane)
    def _():
        @pl.loop(0, pairs)
        def _(p):
            vu_v[p] = (0.5 * v_v[p].astype(F32) + 0.5 * first[p].astype(F32)).astype(BF)

    def keep(n, src, dst):
        return pltpu.make_async_copy(src, dst, outs.at[n])

    kept_early = [
        (x_v, x_o), (a_v, a_o), (q_v, q_o), (k_v, k_o), (vu_v, vu_o), (w_qkv, wq_o), (w_out, wo_o), (len_v, len_o),
    ]
    for n, (src, dst) in enumerate(kept_early):
        keep(n, src, dst).start()

    @pl.loop(0, pairs)
    def _(p):
        pl.when(first_plane)(lambda: gu_step(p, 0))
        lanes = pl.ds(pl.multiple_of(p * PAIR, PAIR), PAIR)

        def put_out(lo, hi, value):
            o_v[lo:hi, lanes] = value

        def put_lse(h, lo, hi, value):
            lse_v[p, h:h + 1, lo:hi] = value

        attend(q_v[p], k_v[p], vu_v[p], length, put_out, put_lse)

    kept_mid = [(o_v, o_o), (lse_v, lse_o)]
    for n, (src, dst) in enumerate(kept_mid, len(kept_early)):
        keep(n, src, dst).start()

    def swap(buffer, r, sems):
        return remote(s1.at[chunk(r), :], buffer.at[chunk(r), :], sems.at[0, r], sems.at[1, r], me.sibling)

    @pl.loop(0, CHUNKS)
    def _(r):
        s1[chunk(r), :] = dot(o_v[chunk(r), :], w_out[...]).astype(BF)
        swap(r1, r, e1).start()

    pl.when(first_plane)(lambda: down_steps(0))

    def finish(r):
        at = chunk(r)
        swap(r2, r, e2).wait_recv()
        r2[at, :] = (h_v[at, :] + s1[at, :].astype(F32) + r2[at, :].astype(F32)).astype(BF)

        @pl.when(first_plane)
        def _():
            mine = pl.ds(pl.multiple_of(r * rows + c * (rows // 2), 16), rows // 2)
            remote(
                r2.at[mine, :], x_v.at[mine, :], hop.at[0, r], hop.at[1, r], {"section": 1 - me.section}
            ).start()

    n_out = len(kept_early) + len(kept_mid)

    def kept_slot(i):
        j = order(i)
        base = n_out + 5 * i
        return [
            keep(base + t, src.at[j], dst.at[j])
            for t, (src, dst) in enumerate(((g_v, g_o), (u_v, u_o), (m_v, m_o), (w_gu, wg_o), (w_down, wd_o)))
        ]

    for i in range(mb):
        j = order(i)
        wait_slot(GU, j)
        wait_slot(DOWN, j)

        @pl.loop(0, CHUNKS)
        def _(r, i=i, j=j):
            at = chunk(r)
            if i + 1 < mb:
                pl.when(first_plane)(lambda: gu_step(r, i + 1))
            if i == 0:
                swap(r1, r, e1).wait_recv()
                h = x_v[at, :].astype(F32) + s1[at, :].astype(F32) + r1[at, :].astype(F32)
                h_v[at, :] = h
                b_v[at, :] = (normalise(h) * gain_two).astype(BF)
            b = b_v[at, :]
            gate = dot_nt(b, w_gu[j, 0])
            up = dot_nt(b, w_gu[j, 1])
            m = (gate / (1.0 + jnp.exp(-gate)) * up).astype(BF)
            g_v[j, at, :] = gate.astype(BF)
            u_v[j, at, :] = up.astype(BF)
            m_v[j, at, :] = m
            grown = dot(m, w_down[j])
            if i:
                grown = acc[at, :] + grown
            if i + 1 < mb:
                acc[at, :] = grown
            else:
                swap(r1, r, e1).wait_send()
                s1[at, :] = grown.astype(BF)
                swap(r2, r, e2).start()

                @pl.when(r > 0)
                def _():
                    finish(r - 1)

        for copy in kept_slot(i):
            copy.start()
        if i + 1 < mb:
            pl.when(first_plane)(lambda: down_steps(i + 1))

    finish(CHUNKS - 1)
    n_last = n_out + 5 * mb
    kept_last = [(h_v, h_o), (b_v, b_o), (r2, y_o)]
    for n, (src, dst) in enumerate(kept_last, n_last):
        keep(n, src, dst).start()

    for w, n in ((QKV, 1), (OUT, 0), (DOWN, 0), (DOWN, 1)):
        own_wait(w, n)
    for w in range(4):
        for n in range(COUNT[w]):
            k = BASE[w] + n
            for j in range(mb):
                s = c * mb + j

                @pl.when(s != z)
                def _(w=w, n=n, k=k, j=j, s=s):
                    piece = slot_part(w, n, j, x)
                    for d in range(1, nx):
                        remote(piece, piece, x_s.at[k, j, d], x_r.at[k, j, x], me.right).wait_send()
                    forwarded = ((s < z) & (z < n_t - 1)) | ((s > z) & (z > 0))
                    pl.when(forwarded)(remote(piece, piece, z_f.at[k, j], z_r.at[k, j], me.right).wait_send)

    for i in range(mb):
        @pl.when(c * mb + i != z)
        def _(i=i):
            remote(tok.at[i], tok.at[i], a2a_s.at[i], a2a_r.at[z], me.right).wait_send()

    @pl.when(me.here)
    def _():
        remote(lens.at[jz], len_v, lsem.at[0], lsem.at[1], me.sibling).wait_send()
        pl.when(first_plane)(remote(x_v, x_v, sib.at[0], sib.at[1], me.sibling).wait_send)
        pl.when(second_plane)(remote(cot_o, cot_o, sib.at[0], sib.at[1], me.sibling).wait_send)

    @pl.when(second_plane & jnp.logical_not(me.here))
    def _():
        remote(cot_o, cot_o, sib.at[0], sib.at[1], me.sibling).wait_recv()

    pl.when(first_plane)(remote(v_v, first, vsem.at[0], vsem.at[1], me.sibling).wait_send)
    for r in range(CHUNKS):
        swap(r2, r, e2).wait_send()
        mine = halves(r, c)
        pl.when(first_plane)(remote(mine, mine, hop.at[0, r], hop.at[1, r], me.sibling).wait_send)
        pl.when(second_plane)(remote(mine, mine, hsib.at[0, r], hsib.at[1, r], me.sibling).wait_send)
    for n, (src, dst) in enumerate(kept_early + kept_mid):
        keep(n, src, dst).wait()
    for i in range(mb):
        for copy in kept_slot(i):
            copy.wait()
    for n, (src, dst) in enumerate(kept_last, n_last):
        keep(n, src, dst).wait()


def forward(tokens, cotangent, lens, qkv, out, gu, down, gains, tables):
    mb, block_rows, dim = tokens.shape
    n_t = lax.axis_size("tensor")
    nx = lax.axis_size("dp") // 2
    seq = block_rows * n_t
    cols, ow, ff = qkv.shape[3], out.shape[1], down.shape[1]
    pairs = mb * cols // PAIR
    assert pairs == COUNT[GU] == CHUNKS
    dma = pltpu.SemaphoreType.DMA
    wide, heads = (seq, dim), (pairs, seq, PAIR)
    hidden, stat = (mb, seq, ff), (pairs, 2, seq)
    weights = [(mb, 3, dim, cols), (mb * ow, dim), (mb, 2, ff, dim), (mb, ff, dim)]
    shape = lambda s, t=BF: jax.ShapeDtypeStruct(s, t)
    return pl.pallas_call(
        forward_kernel,
        out_shape=(
            shape(wide), shape(wide), shape(wide), *(shape(w) for w in weights),
            shape(wide), shape(heads), shape(heads), shape(heads), shape((seq, pairs * PAIR)), shape(stat, F32),
            shape(wide, F32), shape(wide), shape(hidden), shape(hidden), shape(hidden), shape((8, 128), F32),
        ),
        in_specs=[ANY, ANY, VMEM, ANY, ANY, ANY, ANY, VMEM, VMEM, VMEM],
        out_specs=(ANY,) * 19,
        scratch_shapes=[
            *(pltpu.VMEM(w, BF) for w in weights),
            pltpu.VMEM(wide, BF), pltpu.VMEM(heads, BF), pltpu.VMEM(wide, BF),
            *[pltpu.VMEM(heads, BF)] * 4,
            pltpu.VMEM((seq, pairs * PAIR), BF), pltpu.VMEM(stat, F32),
            pltpu.VMEM(wide, F32), pltpu.VMEM(wide, BF),
            *[pltpu.VMEM(hidden, BF)] * 3,
            pltpu.VMEM(wide, F32),
            *[pltpu.VMEM(wide, BF)] * 3,
            pltpu.VMEM((8, 128), F32),
            dma((5,)), dma((mb,)), dma((n_t,)), dma((2,)), dma((N_PIECES,)), dma((N_PIECES,)),
            dma((N_PIECES, mb)), dma((N_PIECES, mb)), dma((N_PIECES, mb, nx)), dma((N_PIECES, mb, nx)),
            dma((2, CHUNKS)), dma((2, CHUNKS)), dma((2, CHUNKS)), dma((2, CHUNKS)), dma((2,)), dma((2,)),
            dma((13 + 5 * mb,)),
        ],
        compiler_params=pltpu.CompilerParams(
            collective_id=0, has_side_effects=True, vmem_limit_bytes=63 << 20
        ),
        name="forward_layer",
    )(tokens, cotangent, lens, qkv, out, gu, down, gains, *tables)


RING_DEPTH = 3
OWN_LAG = 3


def scatter_kernel(
    g_qkv, g_out, g_gu, g_down, y, dx,
    o_qkv, o_out, o_gu, o_down, o_y, o_dx,
    xb_qkv, xb_out, xb_gu, xb_down,
    zb_qkv, zb_out, zb_gu, zb_down,
    fb_qkv, fb_out, fb_gu, fb_down,
    a2a_s, a2a_r, x_s, x_r, z_s, z_r, zo_r, f_s, f_r,
):
    mb = g_qkv.shape[0]
    n_t = lax.axis_size("tensor")
    nx = lax.axis_size("dp") // 2
    dp = lax.axis_index("dp")
    z = lax.axis_index("tensor")
    x, c = dp // 2, lax.rem(dp, 2)
    dim = g_qkv.shape[2]
    part = dim // nx
    quarter = part // 2
    rows = y.shape[0] // n_t
    here = z // mb == c
    jz = z - c * mb
    sibling = {"dp": 2 * x + 1 - c}
    right, left = {"tensor": z + 1}, {"tensor": z - 1}
    half = g_down.shape[1] // 2
    pieces = [(w, n) for w in range(4) for n in range(COUNT[w])]
    n_k = N_PIECES

    barrier = pltpu.get_barrier_semaphore()
    for k in range(1, n_t):
        pl.semaphore_signal(
            barrier, inc=1, device_id={"tensor": lax.rem(z + k, n_t)}, device_id_type=MESH
        )
    for k in range(1, nx):
        pl.semaphore_signal(
            barrier, inc=1, device_id={"dp": 2 * lax.rem(x + k, nx) + c}, device_id_type=MESH
        )
    pl.semaphore_signal(barrier, inc=1, device_id=sibling, device_id_type=MESH)
    pl.semaphore_wait(barrier, n_t + nx - 1)

    def remote(src, dst, send, recv, to):
        return pltpu.make_async_remote_copy(
            src_ref=src, dst_ref=dst, send_sem=send, recv_sem=recv,
            device_id=to, device_id_type=MESH,
        )

    def grad_part(k, j, p):
        w, n = pieces[k]
        col = pl.ds(pl.multiple_of(p * part, 128), part)
        if w == QKV:
            return g_qkv.at[j, :, pl.ds(pl.multiple_of(p * part + n * quarter, 16), quarter), :]
        if w == OUT:
            return g_out.at[j, :, col]
        if w == GU:
            return g_gu.at[j, n // 2, pl.ds(n % 2 * half, half), col]
        return g_down.at[j, pl.ds(n * half, half), col]

    def buffer_part(bufs, k, j):
        w, n = pieces[k]
        if w == QKV:
            return bufs[w].at[j, :, pl.ds(n * quarter, quarter), :]
        if w == OUT:
            return bufs[w].at[j]
        if w == GU:
            return bufs[w].at[j, n // 2, pl.ds(n % 2 * half, half), :]
        return bufs[w].at[j, pl.ds(n * half, half), :]

    def x_buf(k, j, d):
        return buffer_part([b.at[d - 1] for b in (xb_qkv, xb_out, xb_gu, xb_down)], k, j)

    def z_buf(k, j):
        return buffer_part((zb_qkv, zb_out, zb_gu, zb_down), k, j)

    @pl.when(here)
    def _():
        for t, (src, dst) in enumerate(((y, o_y), (dx, o_dx))):
            for d in range(1, n_t):
                zt = lax.rem(z + d, n_t)
                block = src.at[pl.ds(pl.multiple_of(zt * rows, 128), rows), :]
                remote(block, dst.at[jz], a2a_s.at[t, d], a2a_r.at[t, jz], {"tensor": zt}).start()

    def x_send(n):
        k, i = n // mb, n % mb
        j = jnp.where(c == 0, i, mb - 1 - i)
        for d in range(1, nx):
            to = lax.rem(x + d, nx)
            yield remote(
                grad_part(k, j, to), x_buf(k, j, d), x_s.at[k, j, d], x_r.at[k, j, d],
                {"dp": 2 * to + c},
            )

    total = n_k * mb
    for t in range(RING_DEPTH):
        for copy in x_send(t):
            copy.start()

    def final_part(k):
        w, n = pieces[k]
        if w == QKV:
            return o_qkv, fb_qkv
        if w == OUT:
            return o_out, fb_out
        here_rows = pl.ds(n % 2 * half, half)
        if w == GU:
            return o_gu.at[n // 2, here_rows, :], fb_gu.at[n // 2, here_rows, :]
        return o_down.at[here_rows, :], fb_down.at[here_rows, :]

    def own_piece(k):
        w, n = pieces[k]
        total_sum = grad_part(k, jz, x)[...].astype(jnp.float32)
        for d in range(1, nx):
            total_sum = total_sum + x_buf(k, jz, d)[...].astype(jnp.float32)
        x_buf(k, jz, 1)[...] = total_sum.astype(jnp.bfloat16)

        @pl.when(z > 0)
        def _():
            piece = z_buf(k, jz)
            remote(piece, piece, z_s.at[k, jz], z_r.at[k, jz], right).wait_recv()
            x_buf(k, jz, 1)[...] = (
                x_buf(k, jz, 1)[...].astype(jnp.float32) + piece[...].astype(jnp.float32)
            ).astype(jnp.bfloat16)

        @pl.when(z < n_t - 1)
        def _():
            piece = z_buf(k, mb)
            remote(piece, piece, z_s.at[k, jz], zo_r.at[k], right).wait_recv()
            x_buf(k, jz, 1)[...] = (
                x_buf(k, jz, 1)[...].astype(jnp.float32) + piece[...].astype(jnp.float32)
            ).astype(jnp.bfloat16)

        summed = x_buf(k, jz, 1)
        out_ref, fin = final_part(k)
        if w == QKV:
            @pl.when(c == n)
            def _():
                out_ref[...] = summed[...].astype(jnp.float32)

            @pl.when(c != n)
            def _():
                remote(summed, fin, f_s.at[k], f_r.at[k], sibling).start()
        else:
            mine = pl.ds(pl.multiple_of(c * quarter, 128), quarter)
            theirs = pl.ds(pl.multiple_of((1 - c) * quarter, 128), quarter)
            out_ref[...] = summed[:, mine].astype(jnp.float32)
            remote(summed.at[:, theirs], fin, f_s.at[k], f_r.at[k], sibling).start()

    for k in range(n_k):
        for i in range(mb):
            n = k * mb + i
            j = jnp.where(c == 0, i, mb - 1 - i)
            s = c * mb + j
            if n + RING_DEPTH < total:
                for copy in x_send(n):
                    copy.wait_send()
                for copy in x_send(n + RING_DEPTH):
                    copy.start()
            for copy in x_send(n):
                copy.wait_recv()

            @pl.when(s != z)
            def _(k=k, j=j, s=s):
                total_sum = grad_part(k, j, x)[...].astype(jnp.float32)
                for d in range(1, nx):
                    total_sum = total_sum + x_buf(k, j, d)[...].astype(jnp.float32)
                x_buf(k, j, 1)[...] = total_sum.astype(jnp.bfloat16)

                @pl.when(((s > z) & (z > 0)) | ((s < z) & (z < n_t - 1)))
                def _():
                    piece = z_buf(k, j)
                    remote(piece, piece, z_s.at[k, j], z_r.at[k, j], right).wait_recv()
                    x_buf(k, j, 1)[...] = (
                        x_buf(k, j, 1)[...].astype(jnp.float32) + piece[...].astype(jnp.float32)
                    ).astype(jnp.bfloat16)

                @pl.when(s > z)
                def _():
                    remote(x_buf(k, j, 1), z_buf(k, j), z_s.at[k, j], z_r.at[k, j], right).start()

                @pl.when(s < z - 1)
                def _():
                    remote(x_buf(k, j, 1), z_buf(k, j), z_s.at[k, j], z_r.at[k, j], left).start()

                @pl.when(s == z - 1)
                def _():
                    remote(x_buf(k, j, 1), z_buf(k, mb), z_s.at[k, j], zo_r.at[k], left).start()

        if k >= OWN_LAG:
            @pl.when(here)
            def _(k=k):
                own_piece(k - OWN_LAG)

    @pl.when(here)
    def _():
        for k in range(max(0, n_k - OWN_LAG), n_k):
            own_piece(k)

    @pl.when(jnp.logical_not(here))
    def _():
        for k in range(n_k):
            w, n = pieces[k]
            out_ref, fin = final_part(k)
            if w == QKV:
                @pl.when(c == n)
                def _(k=k, out_ref=out_ref, fin=fin):
                    remote(fin, fin, f_s.at[k], f_r.at[k], sibling).wait_recv()
                    out_ref[...] = fin[...].astype(jnp.float32)
            else:
                remote(fin, fin, f_s.at[k], f_r.at[k], sibling).wait_recv()
                out_ref[...] = fin[...].astype(jnp.float32)

    for n in range(max(0, total - RING_DEPTH), total):
        for copy in x_send(n):
            copy.wait_send()

    for k in range(n_k):
        for j in range(mb):
            s = c * mb + j

            @pl.when(s != z)
            def _(k=k, j=j):
                piece = x_buf(k, j, 1)
                remote(piece, piece, z_s.at[k, j], z_r.at[k, j], right).wait_send()

    @pl.when(here)
    def _():
        for k in range(n_k):
            w, n = pieces[k]
            fin = final_part(k)[1]
            if w == QKV:
                @pl.when(c != n)
                def _(k=k, fin=fin):
                    remote(fin, fin, f_s.at[k], f_r.at[k], sibling).wait_send()
            else:
                remote(fin, fin, f_s.at[k], f_r.at[k], sibling).wait_send()

        for t, (src, dst) in enumerate(((y, o_y), (dx, o_dx))):
            for d in range(1, n_t):
                block = src.at[pl.ds(0, rows), :]
                remote(block, dst.at[0], a2a_s.at[t, d], a2a_r.at[t, jz], right).wait_send()
            dst[jz] = src[pl.ds(pl.multiple_of(z * rows, 128), rows), :]

    for t, dst in enumerate((o_y, o_dx)):
        for i in range(mb):
            @pl.when(c * mb + i != z)
            def _(t=t, i=i, dst=dst):
                remote(dst.at[i], dst.at[i], a2a_s.at[t, 0], a2a_r.at[t, i], right).wait_recv()


def scatter(g_qkv, g_out, g_gu, g_down, y, dx):
    mb, _, dim, cols = g_qkv.shape
    n_t = lax.axis_size("tensor")
    n_dp = lax.axis_size("dp")
    nx = n_dp // 2
    part, quarter = dim // nx, dim // n_dp
    out_rows, down_rows = g_out.shape[1], g_down.shape[1]
    rows = y.shape[0] // n_t
    dma = pltpu.SemaphoreType.DMA
    n_k = N_PIECES
    bf, f32 = jnp.bfloat16, jnp.float32

    def shapes(lead, split):
        return (
            (*lead, 3, split, cols), (*lead, out_rows, split),
            (*lead, 2, down_rows, split), (*lead, down_rows, split),
        )

    vmem = pl.BlockSpec(memory_space=pltpu.VMEM)
    finals = shapes((), quarter)
    return pl.pallas_call(
        scatter_kernel,
        out_shape=(
            *(jax.ShapeDtypeStruct(shape, f32) for shape in finals),
            jax.ShapeDtypeStruct((mb, rows, dim), bf),
            jax.ShapeDtypeStruct((mb, rows, dim), bf),
        ),
        in_specs=[vmem] * 6,
        out_specs=(vmem,) * 6,
        scratch_shapes=[
            *(pltpu.VMEM(shape, bf) for shape in shapes((nx - 1, mb), part)),
            *(pltpu.VMEM(shape, bf) for shape in shapes((mb + 1,), part)),
            *(pltpu.VMEM(shape, bf) for shape in finals),
            dma((2, n_t)), dma((2, mb)), dma((n_k, mb, nx)), dma((n_k, mb, nx)),
            dma((n_k, mb)), dma((n_k, mb)), dma((n_k,)), dma((n_k,)), dma((n_k,)),
        ],
        compiler_params=pltpu.CompilerParams(
            collective_id=1, has_side_effects=True, vmem_limit_bytes=62 << 20
        ),
        name="scatter_grads",
    )(g_qkv, g_out, g_gu, g_down, y, dx)


def attention_back_kernel(length, share, q, k, v, o, do, lse, first, cos, sin, dq_o, dk_o, dv_o, dv1_o, dk_a, dv_a):
    seq = q.shape[1]
    blk = seq // CHUNKS
    f32, bf = jnp.float32, jnp.bfloat16
    keys = k[0].astype(f32)
    k_t = keys.T.astype(bf)
    bias = key_bias(length[0:1, :], keys.shape)
    visible = causal_block(blk)
    queries = q[0].astype(f32)
    grads = do[...].astype(f32)
    heads = []
    for h in range(2):
        inside, extra = head_views(h, keys.shape)
        heads.append((
            jnp.where(inside, keys, jnp.where(extra, bias, 0.0)).astype(bf),
            jnp.where(inside, queries, jnp.where(extra, 1.0, 0.0)).astype(bf),
            jnp.where(inside, queries, 0.0).astype(bf),
            jnp.where(inside, grads, 0.0).astype(bf),
            k_t[h * HD:(h + 1) * HD],
        ))
    vals = v[0]
    for i in range(seq // blk):
        lo, hi = i * blk, (i + 1) * blk
        product = (grads[lo:hi] * o[lo:hi, :].astype(f32)).T
        parts = []
        for h in range(2):
            kh, qh, qz, gh, kt = heads[h]
            delta = jnp.sum(product[h * HD:(h + 1) * HD], axis=0, keepdims=True)
            stat = lse[0, h:h + 1, lo:hi]

            def side(a, b, mask):
                s = lax.dot_general(kh[a:b], qh[lo:hi], NT, preferred_element_type=f32)
                p = jnp.exp(s - stat)
                if mask:
                    p = jnp.where(visible, p, 0.0)
                dp = lax.dot_general(vals[a:b], gh[lo:hi], NT, preferred_element_type=f32)
                ds = (p * (dp - delta)).astype(bf)
                dv = jnp.dot(p.astype(bf), gh[lo:hi], preferred_element_type=f32)
                dk = jnp.dot(ds, qz[lo:hi], preferred_element_type=f32)
                if mask and h == 0:
                    dv_a[a:b, :] = dv
                    dk_a[a:b, :] = dk
                else:
                    dv_a[a:b, :] += dv
                    dk_a[a:b, :] += dk
                return jnp.dot(kt[:, a:b], ds, preferred_element_type=f32)

            dq_t = side(lo, hi, True)
            if i:
                dq_t = dq_t + side(0, lo, False)
            parts.append(dq_t)
        dq = jnp.concatenate(parts, axis=0).T * SCORE_SCALE
        dq_o[lo:hi, :] = rotate_pair(dq, cos[lo:hi, :], -sin[lo:hi, :]).astype(bf)
    dk_o[...] = rotate_pair(dk_a[...], cos[...], -sin[...]).astype(bf)
    dv_o[...] = (share[0] * dv_a[...] + first[0].astype(f32)).astype(bf)
    dv1_o[0] = ((1.0 - share[0]) * dv_a[...]).astype(bf)


def attention_back(length, share, q, k, vu, o, do, lse, first, tables):
    pairs, seq, _ = q.shape
    width = pairs * PAIR
    head = pl.BlockSpec((1, seq, PAIR), lambda p: (p, 0, 0))
    col = pl.BlockSpec((seq, PAIR), lambda p: (0, p))
    whole = pl.BlockSpec((seq, PAIR), lambda p: (0, 0))
    smem = pl.BlockSpec(memory_space=pltpu.SMEM)
    return pl.pallas_call(
        attention_back_kernel,
        grid=(pairs,),
        in_specs=[VMEM, smem, head, head, head, col, col, pl.BlockSpec((1, 2, seq), lambda p: (p, 0, 0)), head, whole, whole],
        out_specs=(col, col, col, head),
        out_shape=(*(jax.ShapeDtypeStruct((seq, width), BF),) * 3, jax.ShapeDtypeStruct((pairs, seq, PAIR), BF)),
        scratch_shapes=[pltpu.VMEM((seq, PAIR), jnp.float32)] * 2,
        compiler_params=pltpu.CompilerParams(vmem_limit_bytes=48 << 20),
        cost_estimate=pl.CostEstimate(flops=20 * seq * seq * width, bytes_accessed=20 * seq * width, transcendentals=pairs * seq * seq),
        name="attention_back",
    )(length, share, q, k, vu, o, do, lse, first, *tables)


def rms_norm(values, gain):
    return values * lax.rsqrt(jnp.mean(values * values, axis=-1, keepdims=True) + NORM_EPS) * gain


def pair_sum(part):
    mine = part.astype(jnp.bfloat16)
    swap = [(d, d ^ 1) for d in range(lax.axis_size("dp"))]
    theirs = lax.ppermute(mine, "dp", swap)
    return mine.astype(jnp.float32) + theirs.astype(jnp.float32)


def to_section(values, step):
    return lax.ppermute(values, "section", [(0, 1)] if step > 0 else [(1, 0)])


def backward_layer(weights, x, kept, length, share, tables, dy, first_grad):
    w_qkv, w_out, w_gu, w_down, gains = weights
    a, q, k, vu, o, lse, h, b, gates, ups, ms = kept
    mb = w_gu.shape[0]
    dmo = dy.astype(jnp.bfloat16)
    part = 0.0
    g_gu, g_down = [], []
    for j in range(mb):
        gate, up, m = gates[j].astype(F32), ups[j].astype(F32), ms[j]
        dm = dot_nt(dmo, w_down[j])
        g_down.append(dot_tn(m, dmo).astype(jnp.bfloat16))
        sig = jax.nn.sigmoid(gate)
        d_gate = (dm * up * (sig * (1.0 + gate * (1.0 - sig)))).astype(jnp.bfloat16)
        d_up = (dm * gate * sig).astype(jnp.bfloat16)
        part = part + dot(d_gate, w_gu[j, 0]) + dot(d_up, w_gu[j, 1])
        g_gu.append(jnp.stack([dot_tn(d_gate, b), dot_tn(d_up, b)]).astype(jnp.bfloat16))
    db = pair_sum(part)
    _, norm_back = jax.vjp(rms_norm, h, gains[1])
    dh, dg2 = norm_back(db)
    dh = dy + dh
    dao = dh.astype(jnp.bfloat16)
    do = dot_nt(dao, w_out).astype(jnp.bfloat16)
    cols = w_qkv.shape[3]
    g_out = dot_tn(o, dao).astype(jnp.bfloat16).reshape(mb, -1, dao.shape[1])
    dq, dk, dv, dv1 = attention_back(length, share, q, k, vu, o, do, lse, first_grad, tables)
    grads = (dq, dk, dv)
    g_qkv = jnp.stack([
        jnp.stack([dot_tn(a, g[:, j * cols:(j + 1) * cols]) for g in grads]) for j in range(mb)
    ]).astype(jnp.bfloat16)
    da = pair_sum(sum(dot_nt(g[:, j * cols:(j + 1) * cols], w_qkv[j, i]) for i, g in enumerate(grads) for j in range(mb)))
    _, norm_back = jax.vjp(rms_norm, x.astype(jnp.float32), gains[0])
    dx, dg1 = norm_back(da)
    return dh + dx, dv1, (g_qkv, g_out, jnp.stack(g_gu), jnp.stack(g_down), jnp.stack([dg1, dg2]))


def shards(tokens, lengths, qkv_weight, out_weight, gate_up_weight, down_weight, norm_gains, cotangent):
    is_first = lax.axis_index("section") == 0
    dp = lax.axis_index("dp")
    mb, rows, dim = tokens.shape
    seq_len = rows * lax.axis_size("tensor")
    share = jnp.where(is_first, 1.0, 0.5).astype(F32)[None]
    tables = tuple(jnp.asarray(t) for t in rope_tables(seq_len))
    lens = jnp.broadcast_to(lengths.astype(F32)[:, None, None], (mb, 8, 128))
    (
        x, start, y, w_qkv, w_out, w_gu, w_down, a, q, k, vu, o, lse, h, b, gates, ups, ms, length,
    ) = forward(
        tokens, cotangent, lens, qkv_weight, out_weight, jnp.swapaxes(gate_up_weight, 2, 3), down_weight,
        norm_gains[0], tables,
    )
    weights = (w_qkv, w_out, w_gu, w_down, norm_gains[0])
    kept = (a, q, k, vu, o, lse, h, b, gates, ups, ms)
    mask = jnp.arange(seq_len)[:, None].astype(F32) < length[0, 0]
    cot = jnp.where(mask, start.astype(F32), 0.0)
    dx, dv1, _ = backward_layer(weights, x, kept, length, share, tables, cot, jnp.zeros_like(q))
    dy = jnp.where(is_first, to_section(dx.astype(BF), -1).astype(F32), cot)
    first_grad = to_section(dv1, -1)
    dx, _, grads = backward_layer(weights, x, kept, length, share, tables, dy, first_grad)
    g_qkv, g_out, g_gu, g_down, g_gain = grads
    gain = lax.psum_scatter(
        jnp.where(lax.rem(dp, 2) == 0, g_gain, 0.0), ("dp", "tensor"), scatter_dimension=1, tiled=True
    )
    o_qkv, o_out, o_gu, o_down, o_y, o_dx = scatter(g_qkv, g_out, g_gu, g_down, y, dx.astype(BF))
    return (
        o_y[None], o_dx.astype(F32)[None], o_qkv[None], o_out[None], jnp.swapaxes(o_gu, 1, 2)[None], o_down[None],
        gain[None],
    )


def solution(mesh):
    in_specs = (
        P("dp", "tensor", None),
        P("dp"),
        P("section", None, None, "tensor"),
        P("section", "tensor", None),
        P("section", None, None, "tensor"),
        P("section", "tensor", None),
        P("section", None, None),
        P("dp", "tensor", None),
    )
    out_specs = (
        P("section", "dp", "tensor", None),
        P("section", "dp", "tensor", None),
        P("section", None, "dp", "tensor"),
        P("section", "tensor", "dp"),
        P("section", None, "dp", "tensor"),
        P("section", "tensor", "dp"),
        P("section", None, ("dp", "tensor")),
    )
    return jax.shard_map(shards, mesh=mesh, in_specs=in_specs, out_specs=out_specs, check_vma=False)
```

time: 785 us -> 642 us (0.82)
  starting transfers between devices: 43.1 us -> 3.79 us
  matrix products: 127 us -> 89.1 us
  waiting for transfers between devices: 129 us -> 95 us
  local copies, waits for them, and re-layouts: 43.5 us -> 13.9 us
  Pallas kernels: 368 us -> 379 us
    dot_general x45 -> x39, matrix products: 127 us -> 89.1 us  [the longest x18 50.1 us: dot_nt(): return lax.dot_general(a, b, NT, preferred_element_type=F32)]
    ppermute x8 -> x4, starting transfers between devices: 35 us -> 0.92 us  [pair_sum(): theirs = lax.ppermute(mine, 'dp', swap)]
    unnamed x177 -> x95, local copies, waits for them, and re-layouts: 41.5 us -> 11 us
    ppermute x4 -> x2, waiting for transfers between devices: 114 us -> 86.5 us  [to_section(): return lax.ppermute(values, 'section', [(0, 1)] if step > 0 else [(1, 0)])]
    pallas_call x7 -> x3, Pallas kernels: 193 us -> 213 us  [the longest x1 174 us: forward(): pl.pallas_call(forward_kernel, out_shape=(shape(wide), shape(wide), shape...]
    convert_element_type x6 -> x3, other arithmetic: 20.1 us -> 8.64 us  [the longest x1 5.22 us: shards(): dx.astype(BF)]
    pallas_call x1, Pallas kernels: 175 us -> 166 us  [scatter(): pl.pallas_call(scatter_kernel, out_shape=(*(jax.ShapeDtypeStruct(shape, f...]
  transfers between devices with their start and end apart: 13 -> 7, of which waited for: 7 -> 3; matrix products, arithmetic and copies ran while one was open for 10% -> 10% of each run, Pallas kernels for 23% -> 26%
where the time goes in v2:
time: 642 us; the launch traced here: 635 us
  Pallas kernels  379 us (59%)
  waiting for transfers between devices  95 us (15%)
  matrix products  89.1 us (14%)
  other arithmetic  39.4 us (6%)
  between operations  15 us (2%)
  local copies, waits for them, and re-layouts  13.9 us (2%)
    pallas_call x1, Pallas kernels, forward(): pl.pallas_call(forward_kernel, out_shape=(shape(wide), shape(wide), shape...  174 us
    pallas_call x1, Pallas kernels, scatter(): pl.pallas_call(scatter_kernel, out_shape=(*(jax.ShapeDtypeStruct(shape, f...  166 us
    ppermute x2, waiting for transfers between devices, to_section(): return lax.ppermute(values, 'section', [(0, 1)] if step > 0 else [(1, 0)])  86.5 us
    dot_general x18, matrix products, dot_nt(): return lax.dot_general(a, b, NT, preferred_element_type=F32)  50.1 us
    pallas_call x2, Pallas kernels, attention_back(): pl.pallas_call(attention_back_kernel, grid=(pairs,), in_specs=[VMEM, smem...  38.5 us
    dot_general x13, matrix products, dot_tn(): lax.dot_general(a, b, (((0,), (0,)), ((), ())), preferred_element_type=F32)  21.1 us
    dot_general x8, matrix products, dot(): return jnp.dot(a, b, preferred_element_type=F32)  17.9 us
  transfers between devices with their start and end apart: 7, of which 3 were waited for; matrix products, arithmetic and copies ran while one was open for 10% of the time, Pallas kernels for 26%

profile of v2, /device:TPU:0, one launch (start us, length us, event | category | flops | bytes accessed | tf_op | source)
XLA Modules:
  0.0 635.1 jit_solution(6575379181457341154)
XLA Ops:
  8.5 174.1 %forward_layer.1 = (bf16[1024,1024]{1,0:T(8,128)(2,1)}, bf16[1024,1024]{1,0:T(8,128)(2,1)}, bf16[1024,1024]{1,0:T(8,128)(2,1)}, bf16[2,3,1024,256]{3,2,1,0:T(8,1...) custom-call(bf16[2,256,1024]{2,1,0:T(8,128)(2,1)} %tok.1, ...), custom_call_target="tpu_custom_call" | custom-call | tf_op jit(solution)/shard_map/forward_layer/pallas_call | solution.py:537
  184.5 4.0 fusion.77
  192.9 2.5 fusion.45
  195.4 2.5 fusion.43
  197.9 3.7 add_convert_fusion.3
  201.7 4.5 collective-permute-done
  206.2 4.8 multiply_reduce_fusion.3
  211.0 3.4 fusion
  214.5 2.3 fusion.57.do
  217.9 18.9 %attention_back.2 = (bf16[1024,512]{1,0:T(8,128)(2,1)S(1)}, bf16[1024,512]{1,0:T(8,128)(2,1)S(1)}, bf16[1024,512]{1,0:T(8,128)(2,1)S(1)}, bf16[4,1024,128]{2,1,0:T(8,128)(2,1)S(1)}) custom-call(f32[8,128]{1,0:T(8,128)S(1)} %copy-done.3, f32[1]{0:T(128)} %bitcast.2.share, bf16[4,1024,128]{2,1,0:T(8,128)(2,1)} %get-tuple-element.41.q, ...), custom_call_target="tpu_custom_call" | custom-call | flops 10737418240 | bytes 10485760 | tf_op jit(solution)/shard_map/attention_back/pallas_call | solution.py:926
  239.6 2.7 fusion.128
  242.3 2.8 fusion.132
  245.1 2.8 fusion.124
  247.9 6.5 %add_convert_fusion.2 = bf16[1024,1024]{1,0:T(8,128)(2,1)S(1)} fusion(f32[1024,1024]{1,0:T(8,128)} %fusion.124, f32[1024,1024]{1,0:T(8,128)} %fusion.128, f32[1024,1024]{1,0:T(8,128)} %fusion.132, f32[1024,1024]{1,0:T(8,128)S(1)} %fusion.140, f32[1024,1024]{1,0:T(8,128)S(1)} %fusion.136, bf16[1024,512]{1,0:T(8,128)(2,1)S(1)} %get-tuple-element.56, ...), kind=kOutput, calls=%fused_computation.38 | convolution fusion | flops 543162368 | bytes 24117248 | tf_op jit(solution)/shard_map/dot_general | solution.py:33
  254.6 4.0 collective-permute-done.1
  260.0 2.8 fusion.2
  265.6 86.5 %collective-permute-done.2 = bf16[1024,1024]{1,0:T(8,128)(2,1)} collective-permute-done((bf16[1024,1024]{1,0:T(8,128)(2,1)}, bf16[1024,1024]{1,0:T(8,128)(2,1)}, u32[]{:S(2)}, u32[]{:S(2)}) %collective-permute-start.2) | collective-permute-done | bytes 2097184 | tf_op jit(solution)/shard_map/ppermute | solution.py:951
  352.1 2.9 fusion.14
  361.4 5.6 fusion.40
  374.4 3.3 fusion.63
  385.4 3.4 maximum_maximum_fusion.g_gu
  390.6 3.5 fusion.3
  394.1 2.3 convolution_convert_fusion.7.do
  397.4 19.6 %attention_back.3 = (bf16[1024,512]{1,0:T(8,128)(2,1)S(1)}, bf16[1024,512]{1,0:T(8,128)(2,1)S(1)}, bf16[1024,512]{1,0:T(8,128)(2,1)S(1)}, bf16[4,1024,128]{2,1,0:T(8,128)(2,1)}) custom-call(f32[8,128]{1,0:T(8,128)S(1)} %copy-done.3, f32[1]{0:T(128)} %bitcast.2.share, bf16[4,1024,128]{2,1,0:T(8,128)(2,1)} %get-tuple-element.41.q, ...), custom_call_target="tpu_custom_call" | custom-call | flops 10737418240 | bytes 10485760 | tf_op jit(solution)/shard_map/attention_back/pallas_call | solution.py:926
  421.6 2.7 fusion.126
  425.1 2.8 fusion.122
  427.9 5.0 add_convert_fusion
  433.5 3.2 fusion.103
  442.2 2.2 convolution_convert_fusion.6
  447.5 5.2 fusion.5.dx
  452.8 166.3 %scatter_grads.1 = (f32[3,256,256]{2,1,0:T(8,128)}, f32[256,256]{1,0:T(8,128)}, f32[2,704,256]{2,1,0:T(8,128)}, f32[704,256]{1,0:T(8,128)}, bf16[2,256,1024]{2,1...) custom-call(bf16[2,3,1024,256]{3,2,1,0:T(8,128)(2,1)} %pad_maximum_fusion.g_qkv, bf16[2,256,1024]{2,1,0:T(8,128)(2,1)} %bitcast.188, ...), custom_call_target="tpu_custom_call" | custom-call | tf_op jit(solution)/shard_map/scatter_grads/pallas_call | solution.py:838
  619.1 2.9 bitcast_convert_fusion
  (148 shorter events, 60.6 us)
Async XLA Ops:
  7.2 614.9 %reduce-scatter.4.cloned.1.call-start = ((), (), s32[]{:S(2)}) async-start(), calls=%async_computation.1 | async-start | bytes 557056
  184.5 4.0 copy-start.9
  184.5 4.0 copy-start.26
  184.5 5.9 slice-start
  197.9 3.8 copy-start.20
  201.6 4.6 collective-permute-start
  206.2 4.8 copy-start.4
  211.0 3.5 copy-start.32
  214.5 3.4 copy-start
  214.5 3.4 copy-start.1
  214.5 3.4 copy-start.2
  214.5 3.4 copy-start.3
  247.9 10.7 %copy-start.6 = (bf16[1024,1024]{1,0:T(8,128)(2,1)S(1)}, bf16[1024,1024]{1,0:T(8,128)(2,1)}, u32[]{:S(2)}) copy-start(bf16[1024,1024]{1,0:T(8,128)(2,1)} %get-tuple-element.57) | copy-start | bytes 6291460
  254.4 4.2 collective-permute-start.1
  262.7 89.3 %collective-permute-start.2 = (bf16[1024,1024]{1,0:T(8,128)(2,1)}, bf16[1024,1024]{1,0:T(8,128)(2,1)}, u32[]{:S(2)}, u32[]{:S(2)}) collective-permute-start(bf16[1024,1024]{1,0:T(8,128)(2,1)} %fusion.2), channel_id=1, source_target_pairs={{16,0},{17,1},{18,2},{19,3},{20,4},{21,5},{22,6},{23,7},{24,8},{25... | collective-permute-start | bytes 6291464 | tf_op jit(solution)/shard_map/ppermute | solution.py:951
  264.0 91.0 %copy-start.25 = (bf16[2,1024,704]{2,1,0:T(8,128)(2,1)S(1)}, bf16[2,1024,704]{2,1,0:T(8,128)(2,1)}, u32[]{:S(2)}) copy-start(bf16[2,1024,704]{2,1,0:T(8,128)(2,1)} %get-tuple-element.63) | copy-start | bytes 8650756
  264.0 132.4 %collective-permute-start.4 = (bf16[4,1024,128]{2,1,0:T(8,128)(2,1)S(1)}, bf16[4,1024,128]{2,1,0:T(8,128)(2,1)S(1)}, u32[]{:S(2)}, u32[]{:S(2)}) collective-permute-start(bf16[4,1024,128]{2,1,0:T(8,128)(2,1)S(1)} %get-tuple-element.58), channel_id=1, source_target_pairs={{16,0},{17,1},{18,2},{19,3},{20,4},{21,5},{22,6},{23,7},{24,8},{25... | collective-permute-start | bytes 3145736 | tf_op jit(solution)/shard_map/ppermute | solution.py:951
  358.5 2.8 copy-start.24
  358.5 8.4 %slice-start.2 = ((s8[5767168]{0:T(1024)(128)(4,1)}), s8[4194304]{0:T(1024)(128)(4,1)S(1)}, s32[]{:S(2)}) async-start(s8[5767168]{0:T(1024)(128)(4,1)} %bitcast.194), calls=%async_computation.4 | async-start | bytes 8388608
  361.4 5.6 slice-start.3
  374.3 14.4 %collective-permute-start.3 = (bf16[1024,1024]{1,0:T(8,128)(2,1)S(1)}, bf16[1024,1024]{1,0:T(8,128)(2,1)S(1)}, u32[]{:S(2)}, u32[]{:S(2)}) collective-permute-start(bf16[1024,1024]{1,0:T(8,128)(2,1)S(1)} %add_convert_fusion.1), channel_id=1, source_target_pairs={{0,4},{4,0},{8,12},{12,8},{1,5},{5,1},{9,13},{13,9},{2,6},{6,2},{1... | collective-permute-start | bytes 6291464 | tf_op jit(solution)/shard_map/ppermute | solution.py:946
  385.4 3.7 copy-start.5
  390.6 3.5 copy-start.33
  394.1 48.1 %copy-start.11 = (f32[1024,1024]{1,0:T(8,128)}, f32[1024,1024]{1,0:T(8,128)S(1)}, u32[]{:S(2)}) copy-start(f32[1024,1024]{1,0:T(8,128)S(1)} %fusion.3) | copy-start | bytes 12582916
  432.9 11.6 %copy-start.8 = (bf16[1024,1024]{1,0:T(8,128)(2,1)}, bf16[1024,1024]{1,0:T(8,128)(2,1)S(1)}, u32[]{:S(2)}) copy-start(bf16[1024,1024]{1,0:T(8,128)(2,1)S(1)} %add_convert_fusion) | copy-start | bytes 6291460
  432.9 3.7 copy-start.29
  432.9 11.5 %collective-permute-start.5 = (bf16[1024,1024]{1,0:T(8,128)(2,1)S(1)}, bf16[1024,1024]{1,0:T(8,128)(2,1)S(1)}, u32[]{:S(2)}, u32[]{:S(2)}) collective-permute-start(bf16[1024,1024]{1,0:T(8,128)(2,1)S(1)} %add_convert_fusion), channel_id=1, source_target_pairs={{0,4},{4,0},{8,12},{12,8},{1,5},{5,1},{9,13},{13,9},{2,6},{6,2},{1... | collective-permute-start | bytes 6291464 | tf_op jit(solution)/shard_map/ppermute | solution.py:946
  619.1 4.4 copy-start.16
  619.1 5.3 copy-start.17
  619.1 6.2 copy-start.19
  619.1 6.9 %copy-start.15 = (f32[2,704,256]{2,1,0:T(8,128)S(1)}, f32[2,704,256]{2,1,0:T(8,128)}, u32[]{:S(2)}) copy-start(f32[2,704,256]{2,1,0:T(8,128)} %get-tuple-element.69) | copy-start | bytes 4325380
  623.5 3.7 copy-start.18
  (19 other events, 37.3 us)
Sparse Core Ops, SparseCore 0:
  447.7 56.6 reduce-scatter.3

commit v3 on v2

--- a/solution.py
+++ b/solution.py
@@ -565,454 +565,595 @@
     )(tokens, cotangent, lens, qkv, out, gu, down, gains, *tables)
 
 
-RING_DEPTH = 3
-OWN_LAG = 3
-
-
-def scatter_kernel(
-    g_qkv, g_out, g_gu, g_down, y, dx,
-    o_qkv, o_out, o_gu, o_down, o_y, o_dx,
-    xb_qkv, xb_out, xb_gu, xb_down,
-    zb_qkv, zb_out, zb_gu, zb_down,
-    fb_qkv, fb_out, fb_gu, fb_down,
-    a2a_s, a2a_r, x_s, x_r, z_s, z_r, zo_r, f_s, f_r,
+LAG = 2
+AHEAD = 3
+FF, OUTS, HEADS = range(3)
+FF_PIECES = 6
+PIECES = [(FF, n) for n in range(FF_PIECES)] + [(OUTS, 0), (HEADS, 0), (HEADS, 1)]
+KEY = (0, FF_PIECES, FF_PIECES + 1)
+
+
+def attend_back(queries, keys, vals, outs, grads, stats, length, add_dv, add_dk, put_dq):
+    seq = queries.shape[0]
+    blk = seq // CHUNKS
+    keys, queries, grads = keys.astype(F32), queries.astype(F32), grads.astype(F32)
+    k_t = keys.T.astype(BF)
+    bias = key_bias(length, keys.shape)
+    visible = causal_block(blk)
+    heads = []
+    for h in range(2):
+        inside, extra = head_views(h, keys.shape)
+        heads.append((
+            jnp.where(inside, keys, jnp.where(extra, bias, 0.0)).astype(BF),
+            jnp.where(inside, queries, jnp.where(extra, 1.0, 0.0)).astype(BF),
+            jnp.where(inside, queries, 0.0).astype(BF),
+            jnp.where(inside, grads, 0.0).astype(BF),
+            k_t[h * HD:(h + 1) * HD],
+        ))
+    for i in range(CHUNKS):
+        lo, hi = i * blk, (i + 1) * blk
+        product = (grads[lo:hi] * outs[lo:hi].astype(F32)).T
+        parts = []
+        for h in range(2):
+            kh, qh, qz, gh, kt = heads[h]
+            delta = jnp.sum(product[h * HD:(h + 1) * HD], axis=0, keepdims=True)
+            stat = stats(h, lo, hi)
+
+            def side(a, b, diagonal):
+                p = jnp.exp(dot_nt(kh[a:b], qh[lo:hi]) - stat)
+                if diagonal:
+                    p = jnp.where(visible, p, 0.0)
+                dp = dot_nt(vals[a:b], gh[lo:hi])
+                ds = (p * (dp - delta)).astype(BF)
+                fresh = diagonal and h == 0
+                add_dv(a, b, dot(p.astype(BF), gh[lo:hi]), fresh)
+                add_dk(a, b, dot(ds, qz[lo:hi]), fresh)
+                return dot(kt[:, a:b], ds)
+
+            dq_t = side(lo, hi, True)
+            if i:
+                dq_t = dq_t + side(0, lo, False)
+            parts.append(dq_t)
+        put_dq(lo, hi, jnp.concatenate(parts, axis=0).T * SCORE_SCALE)
+
+
+def norm_back(values, gain, grad):
+    scale = lax.rsqrt(jnp.mean(values * values, axis=-1, keepdims=True) + NORM_EPS)
+    unit = values * scale
+    inner = grad * gain
+    back = scale * (inner - unit * jnp.mean(inner * unit, axis=-1, keepdims=True))
+    return back, jnp.sum(grad * unit, axis=0, keepdims=True)
+
+
+def backward_kernel(
+    y_i, cot_i, len_i, wq_i, wo_i, wg_i, wd_i, x_i, a_i, q_i, k_i, vu_i, o_i, lse_i, h_i, b_i, g_i, u_i, m_i,
+    gains, cos, sin,
+    o_y, o_dx, o_qkv, o_out, o_gu, o_down, o_gain, lx_ff, lx_out, lx_qkv, lz_ff, lz_out, lz_qkv,
+    w_qkv, w_out, w_ff, x_v, a_v, q_v, k_v, vu_v, o_v, lse_v, h_v, b_v, g_v, u_v, m_v,
+    dmo, dao, do_v, first, s1, r1, r2, dk_a, dv_a, st_ff, st_out, st_qkv, fb_ff, fb_out, fb_qkv, g_z, g_x,
+    ld, loc, a2a_s, a2a_r, hop, hsib, e1, e2, vsem, x_s, x_r, z_s, z_r, zo_r, f_s, f_r, stage, gz_s, gz_r, gx_s, gx_r,
 ):
-    mb = g_qkv.shape[0]
-    n_t = lax.axis_size("tensor")
-    nx = lax.axis_size("dp") // 2
-    dp = lax.axis_index("dp")
-    z = lax.axis_index("tensor")
-    x, c = dp // 2, lax.rem(dp, 2)
-    dim = g_qkv.shape[2]
+    mb, block_rows, dim = o_y.shape
+    me = Place(mb)
+    x, c, z, n_t, nx, jz = me.x, me.c, me.z, me.n_t, me.nx, me.jz
     part = dim // nx
     quarter = part // 2
-    rows = y.shape[0] // n_t
-    here = z // mb == c
-    jz = z - c * mb
-    sibling = {"dp": 2 * x + 1 - c}
-    right, left = {"tensor": z + 1}, {"tensor": z - 1}
-    half = g_down.shape[1] // 2
-    pieces = [(w, n) for w in range(4) for n in range(COUNT[w])]
-    n_k = N_PIECES
-
-    barrier = pltpu.get_barrier_semaphore()
-    for k in range(1, n_t):
-        pl.semaphore_signal(
-            barrier, inc=1, device_id={"tensor": lax.rem(z + k, n_t)}, device_id_type=MESH
-        )
-    for k in range(1, nx):
-        pl.semaphore_signal(
-            barrier, inc=1, device_id={"dp": 2 * lax.rem(x + k, nx) + c}, device_id_type=MESH
-        )
-    pl.semaphore_signal(barrier, inc=1, device_id=sibling, device_id_type=MESH)
-    pl.semaphore_wait(barrier, n_t + nx - 1)
-
-    def remote(src, dst, send, recv, to):
-        return pltpu.make_async_remote_copy(
-            src_ref=src, dst_ref=dst, send_sem=send, recv_sem=recv,
-            device_id=to, device_id_type=MESH,
-        )
-
-    def grad_part(k, j, p):
-        w, n = pieces[k]
-        col = pl.ds(pl.multiple_of(p * part, 128), part)
-        if w == QKV:
-            return g_qkv.at[j, :, pl.ds(pl.multiple_of(p * part + n * quarter, 16), quarter), :]
-        if w == OUT:
-            return g_out.at[j, :, col]
-        if w == GU:
-            return g_gu.at[j, n // 2, pl.ds(n % 2 * half, half), col]
-        return g_down.at[j, pl.ds(n * half, half), col]
-
-    def buffer_part(bufs, k, j):
-        w, n = pieces[k]
-        if w == QKV:
-            return bufs[w].at[j, :, pl.ds(n * quarter, quarter), :]
-        if w == OUT:
-            return bufs[w].at[j]
-        if w == GU:
-            return bufs[w].at[j, n // 2, pl.ds(n % 2 * half, half), :]
-        return bufs[w].at[j, pl.ds(n * half, half), :]
-
-    def x_buf(k, j, d):
-        return buffer_part([b.at[d - 1] for b in (xb_qkv, xb_out, xb_gu, xb_down)], k, j)
-
-    def z_buf(k, j):
-        return buffer_part((zb_qkv, zb_out, zb_gu, zb_down), k, j)
-
-    @pl.when(here)
-    def _():
-        for t, (src, dst) in enumerate(((y, o_y), (dx, o_dx))):
+    cols, ow, half = w_qkv.shape[3], w_out.shape[0] // mb, w_ff.shape[2] // 2
+    seq = x_v.shape[0]
+    rows = seq // CHUNKS
+    pairs = q_v.shape[0]
+    slot_pairs = cols // PAIR
+    first_plane, second_plane = me.section == 0, me.section == 1
+    other_plane = {"section": 1 - me.section}
+    me.meet()
+
+    loads = [
+        (wd_i, w_ff.at[:, 0]), (wg_i, w_ff.at[:, 1:3]), (g_i, g_v), (u_i, u_v), (h_i, h_v), (wo_i, w_out),
+        (m_i, m_v), (b_i, b_v), (q_i, q_v), (k_i, k_v), (vu_i, vu_v), (o_i, o_v), (lse_i, lse_v),
+        (wq_i, w_qkv), (x_i, x_v), (a_i, a_v),
+    ]
+    pl.when(second_plane)(pltpu.make_async_copy(cot_i, dmo, ld.at[len(loads)]).start)
+    for n, (src, dst) in enumerate(loads):
+        pltpu.make_async_copy(src, dst, ld.at[n]).start()
+
+    def loaded(lo, hi):
+        for n in range(lo, hi):
+            pltpu.make_async_copy(*loads[n], ld.at[n]).wait()
+
+    def block(n):
+        return pl.ds(pl.multiple_of(n * block_rows, 128), block_rows)
+
+    def give_back(t, src, dst):
+        @pl.when(me.here)
+        def _():
             for d in range(1, n_t):
-                zt = lax.rem(z + d, n_t)
-                block = src.at[pl.ds(pl.multiple_of(zt * rows, 128), rows), :]
-                remote(block, dst.at[jz], a2a_s.at[t, d], a2a_r.at[t, jz], {"tensor": zt}).start()
-
-    def x_send(n):
-        k, i = n // mb, n % mb
-        j = jnp.where(c == 0, i, mb - 1 - i)
+                to = lax.rem(z + d, n_t)
+                remote(src.at[block(to), :], dst.at[jz], a2a_s.at[t, d], a2a_r.at[t, jz], {"tensor": to}).start()
+            pltpu.make_async_copy(src.at[block(z), :], dst.at[jz], loc.at[t]).start()
+
+    give_back(0, y_i, o_y)
+
+    def chunk(r):
+        return pl.ds(pl.multiple_of(r * rows, 128), rows)
+
+    def half_rows(r, core):
+        return dmo.at[pl.ds(pl.multiple_of(r * rows + core * (rows // 2), 16), rows // 2), :]
+
+    def swap(buffer, r, sems):
+        return remote(s1.at[chunk(r), :], buffer.at[chunk(r), :], sems.at[0, r], sems.at[1, r], me.sibling)
+
+    gain_one, gain_two = gains[0:1, :], gains[1:2, :]
+    length = len_i[0:1, :]
+    o_gain[...] = jnp.zeros_like(o_gain)
+    loaded(0, 6)
+    pl.when(second_plane)(pltpu.make_async_copy(cot_i, dmo, ld.at[len(loads)]).wait)
+
+    def finish_mixed(r):
+        at = chunk(r)
+        swap(r1, r, e1).wait_recv()
+        db = s1[at, :].astype(F32) + r1[at, :].astype(F32)
+        back, gain = norm_back(h_v[at, :], gain_two, db)
+        o_gain[1:2, :] += gain
+        dh = dmo[at, :].astype(F32) + back
+        h_v[at, :] = dh
+        low = dh.astype(BF)
+        dao[at, :] = low
+        do_v[at, :] = dot_nt(low, w_out[...]).astype(BF)
+
+    @pl.loop(0, CHUNKS)
+    def _(r):
+        at = chunk(r)
+
+        @pl.when(first_plane)
+        def _():
+            mine, theirs = half_rows(r, c), half_rows(r, 1 - c)
+            remote(mine, mine, hop.at[0, r], hop.at[1, r], me.sibling).wait_recv()
+            remote(mine, mine, hsib.at[0, r], hsib.at[1, r], me.sibling).start()
+            remote(theirs, theirs, hsib.at[0, r], hsib.at[1, r], me.sibling).wait_recv()
+
+        @pl.when(second_plane)
+        def _():
+            position = (r * rows + lax.broadcasted_iota(jnp.int32, (rows, dim), 0)).astype(F32)
+            dmo[at, :] = jnp.where(position < len_i[0:1, 0:1], dmo[at, :].astype(F32), 0.0).astype(BF)
+
+        dy = dmo[at, :]
+        total = None
+        for j in range(mb):
+            dm = dot_nt(dy, w_ff[j, 0])
+            gate, up = g_v[j, at, :].astype(F32), u_v[j, at, :].astype(F32)
+            sig = 1.0 / (1.0 + jnp.exp(-gate))
+            d_gate = (dm * up * (sig * (1.0 + gate * (1.0 - sig)))).astype(BF)
+            d_up = (dm * (gate * sig)).astype(BF)
+            g_v[j, at, :] = d_gate
+            u_v[j, at, :] = d_up
+            term = dot(d_gate, w_ff[j, 1]) + dot(d_up, w_ff[j, 2])
+            total = term if total is None else total + term
+        s1[at, :] = total.astype(BF)
+        swap(r1, r, e1).start()
+
+        @pl.when(r > 0)
+        def _():
+            finish_mixed(r - 1)
+
+    def ff_grads(t):
+        left = (m_v, g_v, u_v)[t]
+        right = (dmo, b_v, b_v)[t]
+
+        @pl.loop(0, mb)
+        def _(j):
+            @pl.loop(0, 2)
+            def _(n):
+                lanes = pl.ds(pl.multiple_of(n * (dim // 2), 128), dim // 2)
+                w_ff[j, t, :, lanes] = dot_tn(left[j], right[:, lanes]).astype(BF)
+
+    def column(p):
+        return pl.ds(pl.multiple_of(p * part, 128), part)
+
+    def order(i):
+        return jnp.where(c == 0, i, mb - 1 - i)
+
+    def key(kind, n):
+        return KEY[kind] + n
+
+    def half_of(n):
+        return pl.ds(pl.multiple_of(lax.rem(n, 2) * half, 16), half)
+
+    def grad_part(kind, n, j, p):
+        if kind == FF:
+            return w_ff.at[j, n // 2, half_of(n), column(p)]
+        if kind == OUTS:
+            return w_out.at[pl.ds(pl.multiple_of(j * ow, 16), ow), column(p)]
+        return w_qkv.at[j, :, pl.ds(pl.multiple_of(p * part + n * quarter, 16), quarter), :]
+
+    def landing(bufs, kind, n, slot):
+        if kind == FF:
+            return bufs[FF].at[slot, n // 2, half_of(n), :]
+        if kind == OUTS:
+            return bufs[OUTS].at[slot]
+        return bufs[HEADS].at[slot, :, pl.ds(n * quarter, quarter), :]
+
+    def land_x(kind, n, j, d):
+        return landing([b.at[d - 1] for b in (lx_ff, lx_out, lx_qkv)], kind, n, j)
+
+    def land_z(kind, n, slot):
+        return landing((lz_ff, lz_out, lz_qkv), kind, n, slot)
+
+    def staged(kind, slot):
+        return (st_ff, st_out, st_qkv)[kind].at[slot]
+
+    def x_copies(kind, n, j):
+        k = key(kind, n)
         for d in range(1, nx):
             to = lax.rem(x + d, nx)
-            yield remote(
-                grad_part(k, j, to), x_buf(k, j, d), x_s.at[k, j, d], x_r.at[k, j, d],
-                {"dp": 2 * to + c},
+            yield d, remote(
+                grad_part(kind, n, j, to), land_x(kind, n, j, d), x_s.at[k, j, d], x_r.at[k, j, d], me.at_x(d)
             )
 
-    total = n_k * mb
-    for t in range(RING_DEPTH):
-        for copy in x_send(t):
+    def x_start(kind, n, i):
+        for _, copy in x_copies(kind, n, order(i)):
             copy.start()
 
-    def final_part(k):
-        w, n = pieces[k]
-        if w == QKV:
-            return o_qkv, fb_qkv
-        if w == OUT:
-            return o_out, fb_out
-        here_rows = pl.ds(n % 2 * half, half)
-        if w == GU:
-            return o_gu.at[n // 2, here_rows, :], fb_gu.at[n // 2, here_rows, :]
-        return o_down.at[here_rows, :], fb_down.at[here_rows, :]
-
-    def own_piece(k):
-        w, n = pieces[k]
-        total_sum = grad_part(k, jz, x)[...].astype(jnp.float32)
+    def reduce_step(kind, n, i):
+        k, j = key(kind, n), order(i)
+        s = c * mb + j
+        mine = grad_part(kind, n, j, x)
+        outer = ((s > z) & (z > 0)) | ((s < z) & (z < n_t - 1))
+        fetch = [pltpu.make_async_copy(land_x(kind, n, j, d), staged(kind, d - 1), stage.at[d - 1]) for d in range(1, nx)]
+        from_z = land_z(kind, n, j)
+        fetch_z = pltpu.make_async_copy(from_z, staged(kind, nx - 1), stage.at[nx - 1])
+        for d, copy in x_copies(kind, n, j):
+            copy.wait_recv()
+            fetch[d - 1].start()
+
+        @pl.when(outer)
+        def _():
+            remote(from_z, from_z, z_s.at[k, j], z_r.at[k, j], me.right).wait_recv()
+            fetch_z.start()
+
+        for copy in fetch:
+            copy.wait()
+        total = mine[...].astype(F32)
         for d in range(1, nx):
-            total_sum = total_sum + x_buf(k, jz, d)[...].astype(jnp.float32)
-        x_buf(k, jz, 1)[...] = total_sum.astype(jnp.bfloat16)
-
-        @pl.when(z > 0)
-        def _():
-            piece = z_buf(k, jz)
-            remote(piece, piece, z_s.at[k, jz], z_r.at[k, jz], right).wait_recv()
-            x_buf(k, jz, 1)[...] = (
-                x_buf(k, jz, 1)[...].astype(jnp.float32) + piece[...].astype(jnp.float32)
-            ).astype(jnp.bfloat16)
-
-        @pl.when(z < n_t - 1)
-        def _():
-            piece = z_buf(k, mb)
-            remote(piece, piece, z_s.at[k, jz], zo_r.at[k], right).wait_recv()
-            x_buf(k, jz, 1)[...] = (
-                x_buf(k, jz, 1)[...].astype(jnp.float32) + piece[...].astype(jnp.float32)
-            ).astype(jnp.bfloat16)
-
-        summed = x_buf(k, jz, 1)
-        out_ref, fin = final_part(k)
-        if w == QKV:
-            @pl.when(c == n)
+            total = total + staged(kind, d - 1)[...].astype(F32)
+        mine[...] = total.astype(BF)
+
+        @pl.when(outer)
+        def _():
+            fetch_z.wait()
+            mine[...] = (mine[...].astype(F32) + staged(kind, nx - 1)[...].astype(F32)).astype(BF)
+
+        pl.when(s > z)(remote(mine, land_z(kind, n, j), z_s.at[k, j], z_r.at[k, j], me.right).start)
+        pl.when(s < z - 1)(remote(mine, land_z(kind, n, j), z_s.at[k, j], z_r.at[k, j], me.left).start)
+        pl.when(s == z - 1)(remote(mine, land_z(kind, n, mb), z_s.at[k, j], zo_r.at[k], me.left).start)
+
+    def final_part(kind, n):
+        if kind == FF:
+            return (o_down.at[half_of(n), :], o_gu.at[jnp.maximum(n // 2 - 1, 0), half_of(n), :]), fb_ff.at[n // 2, half_of(n), :]
+        if kind == OUTS:
+            return (o_out,), fb_out
+        return (o_qkv,), fb_qkv
+
+    def put_final(kind, n, value):
+        targets = final_part(kind, n)[0]
+        if kind == FF:
+            @pl.when(n < 2)
             def _():
-                out_ref[...] = summed[...].astype(jnp.float32)
-
-            @pl.when(c != n)
+                targets[0][...] = value
+
+            @pl.when(n >= 2)
             def _():
-                remote(summed, fin, f_s.at[k], f_r.at[k], sibling).start()
+                targets[1][...] = value
         else:
-            mine = pl.ds(pl.multiple_of(c * quarter, 128), quarter)
-            theirs = pl.ds(pl.multiple_of((1 - c) * quarter, 128), quarter)
-            out_ref[...] = summed[:, mine].astype(jnp.float32)
-            remote(summed.at[:, theirs], fin, f_s.at[k], f_r.at[k], sibling).start()
-
-    for k in range(n_k):
+            targets[0][...] = value
+
+    def own_piece(kind, n):
+        k = key(kind, n)
+        mine = grad_part(kind, n, jz, x)
+        fin = final_part(kind, n)[1]
+
+        @pl.when(me.here)
+        def _():
+            sides = ((z > 0, land_z(kind, n, jz), z_r.at[k, jz], 0), (z < n_t - 1, land_z(kind, n, mb), zo_r.at[k], nx - 1))
+            for there, src, sem, slot in sides:
+                @pl.when(there)
+                def _(src=src, sem=sem, slot=slot):
+                    remote(src, src, f_s.at[k], sem, me.right).wait_recv()
+                    pltpu.make_async_copy(src, staged(kind, slot), stage.at[slot]).start()
+            for there, src, sem, slot in sides:
+                @pl.when(there)
+                def _(src=src, slot=slot):
+                    pltpu.make_async_copy(src, staged(kind, slot), stage.at[slot]).wait()
+                    mine[...] = (mine[...].astype(F32) + staged(kind, slot)[...].astype(F32)).astype(BF)
+            if kind == HEADS:
+                @pl.when(c == n)
+                def _():
+                    put_final(kind, n, mine[...].astype(F32))
+
+                pl.when(c != n)(remote(mine, fin, f_s.at[k], f_r.at[k], me.sibling).start)
+            else:
+                for core in range(2):
+                    @pl.when(c == core)
+                    def _(core=core):
+                        put_final(kind, n, mine[:, core * quarter:(core + 1) * quarter].astype(F32))
+                        theirs = mine.at[:, (1 - core) * quarter:(2 - core) * quarter]
+                        remote(theirs, fin, f_s.at[k], f_r.at[k], me.sibling).start()
+
+    def ahead(index):
+        if index + AHEAD < len(PIECES) * mb:
+            piece, i = divmod(index + AHEAD, mb)
+            x_start(*PIECES[piece], i)
+
+    def begin_reduce():
+        for index in range(AHEAD):
+            x_start(FF, index // mb, index % mb)
+
+    def ff_round(n):
         for i in range(mb):
-            n = k * mb + i
-            j = jnp.where(c == 0, i, mb - 1 - i)
-            s = c * mb + j
-            if n + RING_DEPTH < total:
-                for copy in x_send(n):
-                    copy.wait_send()
-                for copy in x_send(n + RING_DEPTH):
-                    copy.start()
-            for copy in x_send(n):
-                copy.wait_recv()
-
-            @pl.when(s != z)
-            def _(k=k, j=j, s=s):
-                total_sum = grad_part(k, j, x)[...].astype(jnp.float32)
-                for d in range(1, nx):
-                    total_sum = total_sum + x_buf(k, j, d)[...].astype(jnp.float32)
-                x_buf(k, j, 1)[...] = total_sum.astype(jnp.bfloat16)
-
-                @pl.when(((s > z) & (z > 0)) | ((s < z) & (z < n_t - 1)))
-                def _():
-                    piece = z_buf(k, j)
-                    remote(piece, piece, z_s.at[k, j], z_r.at[k, j], right).wait_recv()
-                    x_buf(k, j, 1)[...] = (
-                        x_buf(k, j, 1)[...].astype(jnp.float32) + piece[...].astype(jnp.float32)
-                    ).astype(jnp.bfloat16)
-
-                @pl.when(s > z)
-                def _():
-                    remote(x_buf(k, j, 1), z_buf(k, j), z_s.at[k, j], z_r.at[k, j], right).start()
-
-                @pl.when(s < z - 1)
-                def _():
-                    remote(x_buf(k, j, 1), z_buf(k, j), z_s.at[k, j], z_r.at[k, j], left).start()
-
-                @pl.when(s == z - 1)
-                def _():
-                    remote(x_buf(k, j, 1), z_buf(k, mb), z_s.at[k, j], zo_r.at[k], left).start()
-
-        if k >= OWN_LAG:
-            @pl.when(here)
-            def _(k=k):
-                own_piece(k - OWN_LAG)
-
-    @pl.when(here)
-    def _():
-        for k in range(max(0, n_k - OWN_LAG), n_k):
-            own_piece(k)
-
-    @pl.when(jnp.logical_not(here))
-    def _():
-        for k in range(n_k):
-            w, n = pieces[k]
-            out_ref, fin = final_part(k)
-            if w == QKV:
-                @pl.when(c == n)
-                def _(k=k, out_ref=out_ref, fin=fin):
-                    remote(fin, fin, f_s.at[k], f_r.at[k], sibling).wait_recv()
-                    out_ref[...] = fin[...].astype(jnp.float32)
+            n_next, i_next = n + (i + AHEAD) // mb, (i + AHEAD) % mb
+
+            @pl.when(n_next < FF_PIECES)
+            def _(n_next=n_next, i_next=i_next):
+                x_start(FF, n_next, i_next)
+            reduce_step(FF, n, i)
+
+        @pl.when(n >= LAG)
+        def _():
+            own_piece(FF, n - LAG)
+
+    loaded(6, 8)
+    pl.when(first_plane)(lambda: ff_grads(0))
+    finish_mixed(CHUNKS - 1)
+
+    @pl.when(first_plane)
+    def _():
+        begin_reduce()
+        ff_grads(1)
+        ff_grads(2)
+
+    loaded(8, len(loads))
+
+    def send_dv(p):
+        return remote(vu_v.at[p], first.at[p], vsem.at[0, p], vsem.at[1, p], other_plane)
+
+    @pl.loop(0, pairs)
+    def _(p):
+        pl.when(first_plane)(lambda: ff_round(p))
+        lanes = pl.ds(pl.multiple_of(p * PAIR, PAIR), PAIR)
+
+        def add_to(acc):
+            def add(a, b, value, fresh):
+                if fresh:
+                    acc[a:b, :] = value
+                else:
+                    acc[a:b, :] += value
+            return add
+
+        def put_dq(lo, hi, dq):
+            q_v[p, lo:hi, :] = rotate_pair(dq, cos[lo:hi, :], -sin[lo:hi, :]).astype(BF)
+
+        attend_back(
+            q_v[p], k_v[p], vu_v[p], o_v[:, lanes], do_v[:, lanes], lambda h, lo, hi: lse_v[p, h:h + 1, lo:hi],
+            length, add_to(dv_a), add_to(dk_a), put_dq,
+        )
+        k_v[p] = rotate_pair(dk_a[...], cos[...], -sin[...]).astype(BF)
+
+        @pl.when(first_plane)
+        def _():
+            send_dv(p).wait_recv()
+            vu_v[p] = (dv_a[...] + first[p].astype(F32)).astype(BF)
+
+        @pl.when(second_plane)
+        def _():
+            vu_v[p] = (0.5 * dv_a[...]).astype(BF)
+            send_dv(p).start()
+
+    def slot_rows(t, j, at):
+        source = (q_v, k_v, vu_v)[t]
+        return jnp.concatenate([source[j * slot_pairs + n, at, :] for n in range(slot_pairs)], axis=1)
+
+    def finish_input(r):
+        at = chunk(r)
+        swap(r2, r, e2).wait_recv()
+        da = s1[at, :].astype(F32) + r2[at, :].astype(F32)
+        back, gain = norm_back(x_v[at, :].astype(F32), gain_one, da)
+        o_gain[0:1, :] += gain
+        r2[at, :] = (h_v[at, :] + back).astype(BF)
+
+        @pl.when(second_plane)
+        def _():
+            mine = pl.ds(pl.multiple_of(r * rows + c * (rows // 2), 16), rows // 2)
+            remote(r2.at[mine, :], dmo.at[mine, :], hop.at[0, r], hop.at[1, r], other_plane).start()
+
+    @pl.loop(0, CHUNKS)
+    def _(r):
+        at = chunk(r)
+        total = None
+        for j in range(mb):
+            for t in range(3):
+                term = dot_nt(slot_rows(t, j, at), w_qkv[j, t])
+                total = term if total is None else total + term
+        swap(r1, r, e1).wait_send()
+        s1[at, :] = total.astype(BF)
+        swap(r2, r, e2).start()
+
+        @pl.when(r > 0)
+        def _():
+            finish_input(r - 1)
+
+    finish_input(CHUNKS - 1)
+    give_back(1, r2, o_dx)
+    for d in range(1, n_t):
+        remote(o_gain, g_z.at[d], gz_s.at[d], gz_r.at[d], {"tensor": lax.rem(z + d, n_t)}).start()
+
+    @pl.when(second_plane)
+    def _():
+        for t in range(3):
+            ff_grads(t)
+        begin_reduce()
+
+    @pl.loop(0, 2)
+    def _(n):
+        lanes = pl.ds(pl.multiple_of(n * (dim // 2), 128), dim // 2)
+        w_out[:, lanes] = dot_tn(o_v[...], dao[:, lanes]).astype(BF)
+
+    everything = pl.ds(0, seq)
+
+    @pl.loop(0, mb)
+    def _(j):
+        for t in range(3):
+            w_qkv[j, t] = dot_tn(a_v[...], slot_rows(t, j, everything)).astype(BF)
+
+    @pl.when(second_plane)
+    def _():
+        @pl.loop(0, pairs)
+        def _(p):
+            ff_round(p)
+
+    for piece in range(pairs, len(PIECES)):
+        kind, n = PIECES[piece]
+        for i in range(mb):
+            ahead(piece * mb + i)
+            reduce_step(kind, n, i)
+        own_piece(*PIECES[piece - LAG])
+    for piece in range(len(PIECES) - LAG, len(PIECES)):
+        own_piece(*PIECES[piece])
+
+    for d in range(1, n_t):
+        remote(o_gain, g_z.at[d], gz_s.at[d], gz_r.at[d], me.right).wait()
+    g_z[0] = o_gain[...]
+    for d in range(1, n_t):
+        g_z[0] += g_z[d]
+    for d in range(1, nx):
+        remote(g_z.at[0], g_x.at[d], gx_s.at[d], gx_r.at[d], me.at_x(d)).start()
+    for d in range(1, nx):
+        remote(g_z.at[0], g_x.at[d], gx_s.at[d], gx_r.at[d], me.at_x(d)).wait()
+    o_gain[...] = g_z[0]
+    for d in range(1, nx):
+        o_gain[...] += g_x[d]
+
+    @pl.when(jnp.logical_not(me.here))
+    def _():
+        for kind, n in PIECES:
+            k, fin = key(kind, n), final_part(kind, n)[1]
+
+            def take(kind=kind, n=n, k=k, fin=fin):
+                remote(fin, fin, f_s.at[k], f_r.at[k], me.sibling).wait_recv()
+                put_final(kind, n, fin[...].astype(F32))
+
+            if kind == HEADS:
+                pl.when(c == n)(take)
             else:
-                remote(fin, fin, f_s.at[k], f_r.at[k], sibling).wait_recv()
-                out_ref[...] = fin[...].astype(jnp.float32)
-
-    for n in range(max(0, total - RING_DEPTH), total):
-        for copy in x_send(n):
-            copy.wait_send()
-
-    for k in range(n_k):
+                take()
+
+    for kind, n in PIECES:
+        k = key(kind, n)
         for j in range(mb):
-            s = c * mb + j
-
-            @pl.when(s != z)
-            def _(k=k, j=j):
-                piece = x_buf(k, j, 1)
-                remote(piece, piece, z_s.at[k, j], z_r.at[k, j], right).wait_send()
-
-    @pl.when(here)
-    def _():
-        for k in range(n_k):
-            w, n = pieces[k]
-            fin = final_part(k)[1]
-            if w == QKV:
-                @pl.when(c != n)
-                def _(k=k, fin=fin):
-                    remote(fin, fin, f_s.at[k], f_r.at[k], sibling).wait_send()
+            for _, copy in x_copies(kind, n, j):
+                copy.wait_send()
+            mine = grad_part(kind, n, j, x)
+            pl.when(c * mb + j != z)(remote(mine, mine, z_s.at[k, j], z_r.at[k, j], me.right).wait_send)
+
+    @pl.when(me.here)
+    def _():
+        for kind, n in PIECES:
+            k, fin = key(kind, n), final_part(kind, n)[1]
+            sent = remote(fin, fin, f_s.at[k], f_r.at[k], me.sibling)
+            if kind == HEADS:
+                pl.when(c != n)(sent.wait_send)
             else:
-                remote(fin, fin, f_s.at[k], f_r.at[k], sibling).wait_send()
-
-        for t, (src, dst) in enumerate(((y, o_y), (dx, o_dx))):
+                sent.wait_send()
+        for t, (src, dst) in enumerate(((y_i, o_y), (r2, o_dx))):
             for d in range(1, n_t):
-                block = src.at[pl.ds(0, rows), :]
-                remote(block, dst.at[0], a2a_s.at[t, d], a2a_r.at[t, jz], right).wait_send()
-            dst[jz] = src[pl.ds(pl.multiple_of(z * rows, 128), rows), :]
+                there = src.at[block(0), :]
+                remote(there, dst.at[0], a2a_s.at[t, d], a2a_r.at[t, jz], me.right).wait_send()
+            pltpu.make_async_copy(src.at[block(z), :], dst.at[jz], loc.at[t]).wait()
 
     for t, dst in enumerate((o_y, o_dx)):
         for i in range(mb):
             @pl.when(c * mb + i != z)
             def _(t=t, i=i, dst=dst):
-                remote(dst.at[i], dst.at[i], a2a_s.at[t, 0], a2a_r.at[t, i], right).wait_recv()
-
-
-def scatter(g_qkv, g_out, g_gu, g_down, y, dx):
-    mb, _, dim, cols = g_qkv.shape
+                remote(dst.at[i], dst.at[i], a2a_s.at[t, 0], a2a_r.at[t, i], me.right).wait_recv()
+
+    for p in range(pairs):
+        pl.when(second_plane)(send_dv(p).wait_send)
+    for r in range(CHUNKS):
+        swap(r2, r, e2).wait_send()
+        mine = half_rows(r, c)
+        pl.when(second_plane)(remote(mine, mine, hop.at[0, r], hop.at[1, r], me.sibling).wait_send)
+        pl.when(first_plane)(remote(mine, mine, hsib.at[0, r], hsib.at[1, r], me.sibling).wait_send)
+
+
+def backward(y, cot, length, weights, kept, gains, tables, mb):
+    w_qkv, w_out, w_gu, w_down = weights
     n_t = lax.axis_size("tensor")
     n_dp = lax.axis_size("dp")
     nx = n_dp // 2
+    seq, dim = y.shape
     part, quarter = dim // nx, dim // n_dp
-    out_rows, down_rows = g_out.shape[1], g_down.shape[1]
-    rows = y.shape[0] // n_t
+    cols, ow, ff = w_qkv.shape[3], w_out.shape[0] // mb, w_down.shape[1]
+    pairs = mb * cols // PAIR
     dma = pltpu.SemaphoreType.DMA
-    n_k = N_PIECES
-    bf, f32 = jnp.bfloat16, jnp.float32
-
-    def shapes(lead, split):
-        return (
-            (*lead, 3, split, cols), (*lead, out_rows, split),
-            (*lead, 2, down_rows, split), (*lead, down_rows, split),
-        )
-
-    vmem = pl.BlockSpec(memory_space=pltpu.VMEM)
-    finals = shapes((), quarter)
+    wide, heads, hidden = (seq, dim), (pairs, seq, PAIR), (mb, seq, ff)
+    block = (mb, seq // n_t, dim)
+    shape = lambda s, t=BF: jax.ShapeDtypeStruct(s, t)
+    n_k = len(PIECES)
+    ins = (y, cot, length, *weights, *kept, gains, *tables)
+    vmem_in = {2, len(ins) - 3, len(ins) - 2, len(ins) - 1}
+
+    def parts(lead, split):
+        return (*lead, 3, ff, split), (*lead, ow, split), (*lead, 3, split, cols)
+
     return pl.pallas_call(
-        scatter_kernel,
+        backward_kernel,
         out_shape=(
-            *(jax.ShapeDtypeStruct(shape, f32) for shape in finals),
-            jax.ShapeDtypeStruct((mb, rows, dim), bf),
-            jax.ShapeDtypeStruct((mb, rows, dim), bf),
+            shape(block), shape(block),
+            shape((3, quarter, cols), F32), shape((ow, quarter), F32), shape((2, ff, quarter), F32),
+            shape((ff, quarter), F32), shape((2, dim), F32),
+            *(shape(s) for s in parts((nx - 1, mb), part)),
+            *(shape(s) for s in parts((mb + 1,), part)),
         ),
-        in_specs=[vmem] * 6,
-        out_specs=(vmem,) * 6,
+        in_specs=[VMEM if n in vmem_in else ANY for n in range(len(ins))],
+        out_specs=(ANY, ANY, *(VMEM,) * 5, *(ANY,) * 6),
         scratch_shapes=[
-            *(pltpu.VMEM(shape, bf) for shape in shapes((nx - 1, mb), part)),
-            *(pltpu.VMEM(shape, bf) for shape in shapes((mb + 1,), part)),
-            *(pltpu.VMEM(shape, bf) for shape in finals),
-            dma((2, n_t)), dma((2, mb)), dma((n_k, mb, nx)), dma((n_k, mb, nx)),
-            dma((n_k, mb)), dma((n_k, mb)), dma((n_k,)), dma((n_k,)), dma((n_k,)),
+            pltpu.VMEM(w_qkv.shape, BF), pltpu.VMEM(w_out.shape, BF), pltpu.VMEM((mb, 3, ff, dim), BF),
+            pltpu.VMEM(wide, BF), pltpu.VMEM(wide, BF), *[pltpu.VMEM(heads, BF)] * 3,
+            pltpu.VMEM((seq, pairs * PAIR), BF), pltpu.VMEM((pairs, 2, seq), F32),
+            pltpu.VMEM(wide, F32), pltpu.VMEM(wide, BF), *[pltpu.VMEM(hidden, BF)] * 3,
+            pltpu.VMEM(wide, BF), pltpu.VMEM(wide, BF), pltpu.VMEM((seq, pairs * PAIR), BF), pltpu.VMEM(heads, BF),
+            *[pltpu.VMEM(wide, BF)] * 3, *[pltpu.VMEM((seq, PAIR), F32)] * 2,
+            pltpu.VMEM((nx, ff // 2, part), BF), pltpu.VMEM((nx, ow, part), BF), pltpu.VMEM((nx, 3, quarter, cols), BF),
+            *(pltpu.VMEM(s, BF) for s in parts((), quarter)),
+            pltpu.VMEM((n_t, 2, dim), F32), pltpu.VMEM((nx, 2, dim), F32),
+            dma((17,)), dma((2,)), dma((2, n_t)), dma((2, mb)),
+            dma((2, CHUNKS)), dma((2, CHUNKS)), dma((2, CHUNKS)), dma((2, CHUNKS)), dma((2, pairs)),
+            dma((n_k, mb, nx)), dma((n_k, mb, nx)), dma((n_k, mb)), dma((n_k, mb)), dma((n_k,)), dma((n_k,)), dma((n_k,)),
+            dma((nx,)), dma((n_t,)), dma((n_t,)), dma((nx,)), dma((nx,)),
         ],
         compiler_params=pltpu.CompilerParams(
-            collective_id=1, has_side_effects=True, vmem_limit_bytes=62 << 20
+            collective_id=1, has_side_effects=True, vmem_limit_bytes=63 << 20
         ),
-        name="scatter_grads",
-    )(g_qkv, g_out, g_gu, g_down, y, dx)
-
-
-def attention_back_kernel(length, share, q, k, v, o, do, lse, first, cos, sin, dq_o, dk_o, dv_o, dv1_o, dk_a, dv_a):
-    seq = q.shape[1]
-    blk = seq // CHUNKS
-    f32, bf = jnp.float32, jnp.bfloat16
-    keys = k[0].astype(f32)
-    k_t = keys.T.astype(bf)
-    bias = key_bias(length[0:1, :], keys.shape)
-    visible = causal_block(blk)
-    queries = q[0].astype(f32)
-    grads = do[...].astype(f32)
-    heads = []
-    for h in range(2):
-        inside, extra = head_views(h, keys.shape)
-        heads.append((
-            jnp.where(inside, keys, jnp.where(extra, bias, 0.0)).astype(bf),
-            jnp.where(inside, queries, jnp.where(extra, 1.0, 0.0)).astype(bf),
-            jnp.where(inside, queries, 0.0).astype(bf),
-            jnp.where(inside, grads, 0.0).astype(bf),
-            k_t[h * HD:(h + 1) * HD],
-        ))
-    vals = v[0]
-    for i in range(seq // blk):
-        lo, hi = i * blk, (i + 1) * blk
-        product = (grads[lo:hi] * o[lo:hi, :].astype(f32)).T
-        parts = []
-        for h in range(2):
-            kh, qh, qz, gh, kt = heads[h]
-            delta = jnp.sum(product[h * HD:(h + 1) * HD], axis=0, keepdims=True)
-            stat = lse[0, h:h + 1, lo:hi]
-
-            def side(a, b, mask):
-                s = lax.dot_general(kh[a:b], qh[lo:hi], NT, preferred_element_type=f32)
-                p = jnp.exp(s - stat)
-                if mask:
-                    p = jnp.where(visible, p, 0.0)
-                dp = lax.dot_general(vals[a:b], gh[lo:hi], NT, preferred_element_type=f32)
-                ds = (p * (dp - delta)).astype(bf)
-                dv = jnp.dot(p.astype(bf), gh[lo:hi], preferred_element_type=f32)
-                dk = jnp.dot(ds, qz[lo:hi], preferred_element_type=f32)
-                if mask and h == 0:
-                    dv_a[a:b, :] = dv
-                    dk_a[a:b, :] = dk
-                else:
-                    dv_a[a:b, :] += dv
-                    dk_a[a:b, :] += dk
-                return jnp.dot(kt[:, a:b], ds, preferred_element_type=f32)
-
-            dq_t = side(lo, hi, True)
-            if i:
-                dq_t = dq_t + side(0, lo, False)
-            parts.append(dq_t)
-        dq = jnp.concatenate(parts, axis=0).T * SCORE_SCALE
-        dq_o[lo:hi, :] = rotate_pair(dq, cos[lo:hi, :], -sin[lo:hi, :]).astype(bf)
-    dk_o[...] = rotate_pair(dk_a[...], cos[...], -sin[...]).astype(bf)
-    dv_o[...] = (share[0] * dv_a[...] + first[0].astype(f32)).astype(bf)
-    dv1_o[0] = ((1.0 - share[0]) * dv_a[...]).astype(bf)
-
-
-def attention_back(length, share, q, k, vu, o, do, lse, first, tables):
-    pairs, seq, _ = q.shape
-    width = pairs * PAIR
-    head = pl.BlockSpec((1, seq, PAIR), lambda p: (p, 0, 0))
-    col = pl.BlockSpec((seq, PAIR), lambda p: (0, p))
-    whole = pl.BlockSpec((seq, PAIR), lambda p: (0, 0))
-    smem = pl.BlockSpec(memory_space=pltpu.SMEM)
-    return pl.pallas_call(
-        attention_back_kernel,
-        grid=(pairs,),
-        in_specs=[VMEM, smem, head, head, head, col, col, pl.BlockSpec((1, 2, seq), lambda p: (p, 0, 0)), head, whole, whole],
-        out_specs=(col, col, col, head),
-        out_shape=(*(jax.ShapeDtypeStruct((seq, width), BF),) * 3, jax.ShapeDtypeStruct((pairs, seq, PAIR), BF)),
-        scratch_shapes=[pltpu.VMEM((seq, PAIR), jnp.float32)] * 2,
-        compiler_params=pltpu.CompilerParams(vmem_limit_bytes=48 << 20),
-        cost_estimate=pl.CostEstimate(flops=20 * seq * seq * width, bytes_accessed=20 * seq * width, transcendentals=pairs * seq * seq),
-        name="attention_back",
-    )(length, share, q, k, vu, o, do, lse, first, *tables)
-
-
-def rms_norm(values, gain):
-    return values * lax.rsqrt(jnp.mean(values * values, axis=-1, keepdims=True) + NORM_EPS) * gain
-
-
-def pair_sum(part):
-    mine = part.astype(jnp.bfloat16)
-    swap = [(d, d ^ 1) for d in range(lax.axis_size("dp"))]
-    theirs = lax.ppermute(mine, "dp", swap)
-    return mine.astype(jnp.float32) + theirs.astype(jnp.float32)
-
-
-def to_section(values, step):
-    return lax.ppermute(values, "section", [(0, 1)] if step > 0 else [(1, 0)])
-
-
-def backward_layer(weights, x, kept, length, share, tables, dy, first_grad):
-    w_qkv, w_out, w_gu, w_down, gains = weights
-    a, q, k, vu, o, lse, h, b, gates, ups, ms = kept
-    mb = w_gu.shape[0]
-    dmo = dy.astype(jnp.bfloat16)
-    part = 0.0
-    g_gu, g_down = [], []
-    for j in range(mb):
-        gate, up, m = gates[j].astype(F32), ups[j].astype(F32), ms[j]
-        dm = dot_nt(dmo, w_down[j])
-        g_down.append(dot_tn(m, dmo).astype(jnp.bfloat16))
-        sig = jax.nn.sigmoid(gate)
-        d_gate = (dm * up * (sig * (1.0 + gate * (1.0 - sig)))).astype(jnp.bfloat16)
-        d_up = (dm * gate * sig).astype(jnp.bfloat16)
-        part = part + dot(d_gate, w_gu[j, 0]) + dot(d_up, w_gu[j, 1])
-        g_gu.append(jnp.stack([dot_tn(d_gate, b), dot_tn(d_up, b)]).astype(jnp.bfloat16))
-    db = pair_sum(part)
-    _, norm_back = jax.vjp(rms_norm, h, gains[1])
-    dh, dg2 = norm_back(db)
-    dh = dy + dh
-    dao = dh.astype(jnp.bfloat16)
-    do = dot_nt(dao, w_out).astype(jnp.bfloat16)
-    cols = w_qkv.shape[3]
-    g_out = dot_tn(o, dao).astype(jnp.bfloat16).reshape(mb, -1, dao.shape[1])
-    dq, dk, dv, dv1 = attention_back(length, share, q, k, vu, o, do, lse, first_grad, tables)
-    grads = (dq, dk, dv)
-    g_qkv = jnp.stack([
-        jnp.stack([dot_tn(a, g[:, j * cols:(j + 1) * cols]) for g in grads]) for j in range(mb)
-    ]).astype(jnp.bfloat16)
-    da = pair_sum(sum(dot_nt(g[:, j * cols:(j + 1) * cols], w_qkv[j, i]) for i, g in enumerate(grads) for j in range(mb)))
-    _, norm_back = jax.vjp(rms_norm, x.astype(jnp.float32), gains[0])
-    dx, dg1 = norm_back(da)
-    return dh + dx, dv1, (g_qkv, g_out, jnp.stack(g_gu), jnp.stack(g_down), jnp.stack([dg1, dg2]))
+        name="backward_layer",
+    )(*ins)
 
 
 def shards(tokens, lengths, qkv_weight, out_weight, gate_up_weight, down_weight, norm_gains, cotangent):
-    is_first = lax.axis_index("section") == 0
-    dp = lax.axis_index("dp")
+    dp, z = lax.axis_index("dp"), lax.axis_index("tensor")
     mb, rows, dim = tokens.shape
-    seq_len = rows * lax.axis_size("tensor")
-    share = jnp.where(is_first, 1.0, 0.5).astype(F32)[None]
-    tables = tuple(jnp.asarray(t) for t in rope_tables(seq_len))
+    n_t = lax.axis_size("tensor")
+    tables = tuple(jnp.asarray(t) for t in rope_tables(rows * n_t))
     lens = jnp.broadcast_to(lengths.astype(F32)[:, None, None], (mb, 8, 128))
     (
-        x, start, y, w_qkv, w_out, w_gu, w_down, a, q, k, vu, o, lse, h, b, gates, ups, ms, length,
+        x, cot, y, w_qkv, w_out, w_gu, w_down, a, q, k, vu, o, lse, h, b, gates, ups, ms, length,
     ) = forward(
         tokens, cotangent, lens, qkv_weight, out_weight, jnp.swapaxes(gate_up_weight, 2, 3), down_weight,
         norm_gains[0], tables,
     )
-    weights = (w_qkv, w_out, w_gu, w_down, norm_gains[0])
-    kept = (a, q, k, vu, o, lse, h, b, gates, ups, ms)
-    mask = jnp.arange(seq_len)[:, None].astype(F32) < length[0, 0]
-    cot = jnp.where(mask, start.astype(F32), 0.0)
-    dx, dv1, _ = backward_layer(weights, x, kept, length, share, tables, cot, jnp.zeros_like(q))
-    dy = jnp.where(is_first, to_section(dx.astype(BF), -1).astype(F32), cot)
-    first_grad = to_section(dv1, -1)
-    dx, _, grads = backward_layer(weights, x, kept, length, share, tables, dy, first_grad)
-    g_qkv, g_out, g_gu, g_down, g_gain = grads
-    gain = lax.psum_scatter(
-        jnp.where(lax.rem(dp, 2) == 0, g_gain, 0.0), ("dp", "tensor"), scatter_dimension=1, tiled=True
-    )
-    o_qkv, o_out, o_gu, o_down, o_y, o_dx = scatter(g_qkv, g_out, g_gu, g_down, y, dx.astype(BF))
+    o_y, o_dx, o_qkv, o_out, o_gu, o_down, gain = backward(
+        y, cot, length, (w_qkv, w_out, w_gu, w_down), (x, a, q, k, vu, o, lse, h, b, gates, ups, ms),
+        norm_gains[0], tables, mb,
+    )[:7]
+    share = dim // (lax.axis_size("dp") * n_t)
+    gain = lax.dynamic_slice_in_dim(gain, (dp * n_t + z) * share, share, 1)
     return (
         o_y[None], o_dx.astype(F32)[None], o_qkv[None], o_out[None], jnp.swapaxes(o_gu, 1, 2)[None], o_down[None],
         gain[None],

time: 642 us -> 492 us (0.77)
  Pallas kernels: 379 us -> 480 us
  waiting for transfers between devices: 95 us -> 0 us
  matrix products: 89.1 us -> 0 us
  other arithmetic: 39.4 us -> 3.58 us
  between operations: 15 us -> 0.67 us
  local copies, waits for them, and re-layouts: 13.9 us -> 6.53 us
    pallas_call x3 -> x1, Pallas kernels: 205 us -> 306 us  [backward(): pl.pallas_call(backward_kernel, out_shape=(shape(block), shape(block), sh...]
    ppermute x6 -> x0, waiting for transfers between devices: 95 us -> none  [the longest x2 86.5 us: to_section(): return lax.ppermute(values, 'section', [(0, 1)] if step > 0 else [(1, 0)])]
    dot_general x39 -> x0, matrix products: 89.1 us -> none  [the longest x18 50.1 us: dot_nt(): return lax.dot_general(a, b, NT, preferred_element_type=F32)]
    convert_element_type x3 -> x0, other arithmetic: 10.9 us -> none  [the longest x1 5.22 us: shards(): dx.astype(BF)]
    reduce_sum x4 -> x0, other arithmetic: 9.64 us -> none  [the longest x2 6.14 us: rms_norm(): jnp.mean(values * values, axis=-1, keepdims=True) + NORM_EPS]
    another operation x4 -> x0, other arithmetic: 7.6 us -> none  [the longest x1 3.39 us: backward_layer(): jnp.stack(g_gu)]
    add x2 -> x0, other arithmetic: 6.94 us -> none  [backward_layer(): dh = dy + dh]
    unnamed x95 -> x15, local copies, waits for them, and re-layouts: 11 us -> 4.53 us
  transfers between devices with their start and end apart: 7 -> 0, of which waited for: 3 -> 0; matrix products, arithmetic and copies ran while one was open for 10% -> 0% of each run, Pallas kernels for 26% -> 0%
where the time goes in v3:
time: 492 us; the launch traced here: 490 us
  Pallas kernels  480 us (98%)
  local copies, waits for them, and re-layouts  6.53 us (1%)
    pallas_call x1, Pallas kernels, backward(): pl.pallas_call(backward_kernel, out_shape=(shape(block), shape(block), sh...  306 us
    pallas_call x1, Pallas kernels, forward(): pl.pallas_call(forward_kernel, out_shape=(shape(wide), shape(wide), shape...  174 us

profile of v3, /device:TPU:0, one launch (start us, length us, event | category | flops | bytes accessed | tf_op | source)
XLA Modules:
  0.0 490.4 jit_solution(9189802385649738536)
XLA Ops:
  0.6 0.7 convert_element_type.4
  1.3 0.7 broadcast_in_dim.30.lens
  2.0 174.1 %forward_layer.1 = (bf16[1024,1024]{1,0:T(8,128)(2,1)}, bf16[1024,1024]{1,0:T(8,128)(2,1)}, bf16[1024,1024]{1,0:T(8,128)(2,1)}, bf16[2,3,1024,256]{3,2,1,0:T(8,1...) custom-call(bf16[2,256,1024]{2,1,0:T(8,128)(2,1)} %tok.1, ...), custom_call_target="tpu_custom_call" | custom-call | tf_op jit(solution)/shard_map/forward_layer/pallas_call | solution.py:537
  176.0 305.5 %backward_layer.1 = (bf16[2,256,1024]{2,1,0:T(8,128)(2,1)}, bf16[2,256,1024]{2,1,0:T(8,128)(2,1)}, f32[3,256,256]{2,1,0:T(8,128)}, f32[256,256]{1,0:T(8,128)}, f...) custom-call(bf16[1024,1024]{1,0:T(8,128)(2,1)} %get-tuple-element.33, ...), custom_call_target="tpu_custom_call" | custom-call | tf_op jit(solution)/shard_map/backward_layer/pallas_call | solution.py:1106
  481.6 0.0 copy-start.1
  481.6 0.0 copy-start.2
  481.6 2.9 bitcast_convert_fusion
  484.5 0.0 copy-start.4
  484.5 1.3 dynamic-slice_bitcast_fusion
  485.8 0.0 copy-done.1
  485.8 0.0 copy-start
  485.8 1.0 copy.22
  486.8 0.0 copy-done.2
  486.8 0.9 copy.23
  487.7 0.0 copy-done.4
  487.7 0.0 copy-start.3
  487.7 0.7 copy.24
  488.4 0.0 copy-done
  488.4 1.1 copy.25
  489.5 0.0 copy-done.3
  489.5 0.9 copy.26
Async XLA Ops:
  481.6 4.3 copy-start.1
  481.6 5.2 %copy-start.2 = (f32[3,256,256]{2,1,0:T(8,128)S(1)}, f32[3,256,256]{2,1,0:T(8,128)}, u32[]{:S(2)}) copy-start(f32[3,256,256]{2,1,0:T(8,128)} %get-tuple-element.54) | copy-start | bytes 2359300
  484.5 3.2 copy-start.4
  485.8 2.6 copy-start
  487.7 1.8 copy-start.3

commit v4 on v3

v4 whole, which is shorter than its diff:
```python
import jax
import jax.numpy as jnp
import numpy as np
from jax import lax
from jax.experimental import pallas as pl
from jax.experimental.pallas import tpu as pltpu
from jax.sharding import PartitionSpec as P

MESH = pl.DeviceIdType.MESH
ANY = pl.BlockSpec(memory_space=pl.ANY)
VMEM = pl.BlockSpec(memory_space=pltpu.VMEM)
NORM_EPS = 1e-6
ROPE_BASE = 10000.0
SCORE_SCALE = 0.125
MASK_VALUE = -1e30
HD = 64
PAIR = 2 * HD
CHUNKS = 4
NT = (((1,), (1,)), ((), ()))
BF, F32 = jnp.bfloat16, jnp.float32

QKV, OUT, GU, DOWN = range(4)
COUNT = (2, 1, 4, 2)
BASE = (0, 2, 3, 7)
N_PIECES = 9


def dot(a, b):
    return jnp.dot(a, b, preferred_element_type=F32)


def dot_nt(a, b):
    return lax.dot_general(a, b, NT, preferred_element_type=F32)


def dot_tn(a, b):
    return lax.dot_general(a, b, (((0,), (0,)), ((), ())), preferred_element_type=F32)


def remote(src, dst, send, recv, to):
    return pltpu.make_async_remote_copy(
        src_ref=src, dst_ref=dst, send_sem=send, recv_sem=recv, device_id=to, device_id_type=MESH
    )


class Place:
    def __init__(self, mb):
        self.n_t = lax.axis_size("tensor")
        self.nx = lax.axis_size("dp") // 2
        self.section = lax.axis_index("section")
        dp = lax.axis_index("dp")
        self.z = lax.axis_index("tensor")
        self.x, self.c = dp // 2, lax.rem(dp, 2)
        self.here = self.z // mb == self.c
        self.jz = self.z - self.c * mb
        self.sibling = {"dp": 2 * self.x + 1 - self.c}
        self.right, self.left = {"tensor": self.z + 1}, {"tensor": self.z - 1}

    def at_x(self, d):
        return {"dp": 2 * lax.rem(self.x + d, self.nx) + self.c}

    def meet(self):
        barrier = pltpu.get_barrier_semaphore()
        partners = [{"tensor": lax.rem(self.z + k, self.n_t)} for k in range(1, self.n_t)]
        partners += [self.at_x(k) for k in range(1, self.nx)]
        partners += [self.sibling, {"section": 1 - self.section}]
        for partner in partners:
            pl.semaphore_signal(barrier, inc=1, device_id=partner, device_id_type=MESH)
        pl.semaphore_wait(barrier, len(partners))


def rope_tables(positions):
    lane = np.arange(PAIR)
    frequency = ROPE_BASE ** (-(lane % (HD // 2)) * 2.0 / HD)
    angles = np.arange(positions)[:, None] * frequency[None, :]
    sign = np.where(lane % HD < HD // 2, -1.0, 1.0)
    return np.cos(angles).astype(np.float32), (np.sin(angles) * sign).astype(np.float32)


def rotate_pair(values, cos, sin):
    lane = lax.broadcasted_iota(jnp.int32, values.shape, 1)
    partner = jnp.where(
        lax.rem(lane, HD) < HD // 2,
        pltpu.roll(values, PAIR - HD // 2, 1),
        pltpu.roll(values, HD // 2, 1),
    )
    return values * cos + partner * sin


def normalise(values):
    return values * lax.rsqrt(jnp.mean(values * values, axis=-1, keepdims=True) + NORM_EPS)


def head_views(h, shape):
    lane = lax.broadcasted_iota(jnp.int32, shape, 1)
    return lane // HD == h, lane == (1 - h) * HD


def causal_block(blk):
    key = lax.broadcasted_iota(jnp.int32, (blk, blk), 0)
    query = lax.broadcasted_iota(jnp.int32, (blk, blk), 1)
    return key <= query


def head_keys(keys, length, first_row):
    position = (first_row + lax.broadcasted_iota(jnp.int32, keys.shape, 0)).astype(F32)
    bias = jnp.where(position < length, 0.0, MASK_VALUE)
    views = []
    for h in range(2):
        inside, extra = head_views(h, keys.shape)
        views.append(jnp.where(inside, keys, jnp.where(extra, bias, 0.0)).astype(BF))
    return views


def head_queries(h, queries, mark):
    inside, extra = head_views(h, queries.shape)
    return jnp.where(inside, queries, jnp.where(extra, mark, 0.0)).astype(BF)


def attend_block(i, blk, queries, keys, vals_t, put_out, put_lse):
    lo, hi = i * blk, (i + 1) * blk
    visible = causal_block(blk)
    queries = queries.astype(F32)
    parts = []
    for h in range(2):
        qi = head_queries(h, queries, 1.0)
        vh = slice(h * HD, (h + 1) * HD)
        s_diag = jnp.where(visible, dot_nt(keys(h, lo, hi), qi), MASK_VALUE)
        top = jnp.max(s_diag, axis=0, keepdims=True)
        if i:
            s_full = dot_nt(keys(h, 0, lo), qi)
            top = jnp.maximum(top, jnp.max(s_full, axis=0, keepdims=True))
        p_diag = jnp.exp(s_diag - top)
        total = jnp.sum(p_diag, axis=0, keepdims=True)
        acc = dot(vals_t(vh, lo, hi), p_diag.astype(BF))
        if i:
            p_full = jnp.exp(s_full - top)
            total = total + jnp.sum(p_full, axis=0, keepdims=True)
            acc = acc + dot(vals_t(vh, 0, lo), p_full.astype(BF))
        parts.append(acc / total)
        put_lse(h, lo, hi, top + jnp.log(total))
    put_out(lo, hi, jnp.concatenate(parts, axis=0).T.astype(BF))


def forward_part(
    me, tok, cot, lens, qkv, out, gu, down, gains, cos, sin, tok_o,
    w_qkv, w_out, w_ff, x_v, first, q_v, ka_v, kb_v, vt_v, v_v, vu_v, o_v, lse_v, h_v, b_v, g_v, u_v, m_v,
    s1, r1, r2, dmo, len_v,
    loc, a2a_s, a2a_r, c2a_s, c2a_r, y_s, y_r, sib, own_r, own_l, z_r, z_f, x_s, x_r, hop, hsib, e1, e2, vsem, lsem,
):
    mb, block_rows, dim = tok.shape
    x, c, z, n_t, nx, jz = me.x, me.c, me.z, me.n_t, me.nx, me.jz
    part = dim // nx
    cols, ow, half = qkv.shape[3], out.shape[1], down.shape[1] // 2
    seq = x_v.shape[0]
    rows = seq // CHUNKS
    pairs = q_v.shape[0]
    first_plane, second_plane = me.section == 0, me.section == 1

    def column(p):
        return pl.ds(pl.multiple_of(p * part, 128), part)

    def shard_part(w, n, p):
        if w == QKV:
            return qkv.at[0, :, pl.ds(pl.multiple_of(p * part + n * (part // 2), 16), part // 2), :]
        if w == OUT:
            return out.at[0, :, column(p)]
        if w == GU:
            return gu.at[0, n // 2, pl.ds(pl.multiple_of(lax.rem(n, 2) * half, 16), half), column(p)]
        return down.at[0, pl.ds(n * half, half), column(p)]

    def slot_part(w, n, j, p):
        if w == QKV:
            return w_qkv.at[j, :, pl.ds(pl.multiple_of(p * part + n * (part // 2), 16), part // 2), :]
        if w == OUT:
            return w_out.at[pl.ds(pl.multiple_of(j * ow, 16), ow), column(p)]
        if w == GU:
            return w_ff.at[j, 1 + n // 2, pl.ds(pl.multiple_of(lax.rem(n, 2) * half, 16), half), column(p)]
        return w_ff.at[j, 0, pl.ds(n * half, half), column(p)]

    own_slots = (
        (qkv.at[0], w_qkv.at[jz]),
        (out.at[0], w_out.at[pl.ds(pl.multiple_of(jz * ow, 16), ow), :]),
        (gu.at[0], w_ff.at[jz, 1:3]),
        (down.at[0], w_ff.at[jz, 0]),
    )

    def own_copies(w, n):
        k = BASE[w] + n
        src, dst = shard_part(w, n, x), slot_part(w, n, jz, x)
        return (
            (z < n_t - 1, remote(src, dst, own_r.at[k], z_r.at[k, jz], me.right)),
            (z > 0, remote(src, dst, own_l.at[k], z_r.at[k, jz], me.left)),
        )

    def own_start(w, n):
        @pl.when(me.here)
        def _():
            for there, copy in own_copies(w, n):
                pl.when(there)(copy.start)

    def own_wait(w, n):
        @pl.when(me.here)
        def _():
            for there, copy in own_copies(w, n):
                pl.when(there)(copy.wait_send)

    def order(i):
        return jnp.where(c == 0, mb - 1 - i, i)

    def foreign(w, n, i):
        j = order(i)
        s = c * mb + j
        k = BASE[w] + n

        @pl.when(s != z)
        def _():
            piece = slot_part(w, n, j, x)
            to_right = remote(piece, piece, z_f.at[k, j], z_r.at[k, j], me.right)
            to_left = remote(piece, piece, z_f.at[k, j], z_r.at[k, j], me.left)
            to_right.wait_recv()
            pl.when((s < z) & (z < n_t - 1))(to_right.start)
            pl.when((s > z) & (z > 0))(to_left.start)
            for d in range(1, nx):
                remote(piece, piece, x_s.at[k, j, d], x_r.at[k, j, x], me.at_x(d)).start()

    def wait_slot(w, j):
        s = c * mb + j

        @pl.when(s != z)
        def _():
            for n in range(COUNT[w]):
                k = BASE[w] + n
                for d in range(1, nx):
                    p = lax.rem(x + d, nx)
                    piece = slot_part(w, n, j, p)
                    remote(piece, piece, x_s.at[k, j, d], x_r.at[k, j, p], me.right).wait_recv()

    def gu_step(n, i):
        if i == 0:
            @pl.when(n >= 2)
            def _():
                own_wait(GU, n - 2)
            own_start(GU, n)
        foreign(GU, n, i)

    def down_steps(i):
        for n in range(COUNT[DOWN]):
            if i == 0:
                own_wait(GU, n + 2)
                own_start(DOWN, n)
            foreign(DOWN, n, i)

    def block_at(n):
        return pl.ds(pl.multiple_of(n * block_rows, 128), block_rows)

    block = block_at(z)
    other_plane = {"section": 1 - me.section}

    def spread(source, target, send, recv):
        for i in range(mb):
            zt = c * mb + i

            @pl.when(zt != z)
            def _(i=i, zt=zt):
                remote(source.at[i], target.at[block, :], send.at[i], recv.at[z], {"tensor": zt}).start()

    def arrived(target, zs, recv):
        there = target.at[block_at(zs), :]
        return remote(there, there, recv.at[zs], recv.at[zs], me.right)

    def to_first(zs):
        return remote(tok_o.at[block_at(zs), :], x_v.at[block_at(zs), :], y_s.at[zs], y_r.at[zs], other_plane)

    pl.when(second_plane)(lambda: spread(tok, tok_o, a2a_s, a2a_r))
    for i in range(mb):
        @pl.when(first_plane & (c * mb + i == z))
        def _(i=i):
            pltpu.make_async_copy(tok.at[i], x_v.at[block, :], loc.at[4]).start()

    @pl.when(me.here)
    def _():
        remote(lens.at[jz], len_v, lsem.at[0], lsem.at[1], me.sibling).start()
        len_v[...] = lens[jz]
        for w, (src, dst) in enumerate(own_slots):
            pltpu.make_async_copy(src, dst, loc.at[w]).start()

    own_start(QKV, 0)
    own_start(QKV, 1)
    for w, n in ((QKV, 0), (QKV, 1), (OUT, 0)):
        if w == OUT:
            own_wait(QKV, 0)
            own_start(OUT, 0)
        for i in range(mb):
            foreign(w, n, i)
        if (w, n) == (QKV, 1):
            @pl.when(second_plane & me.here)
            def _():
                for zs in range(n_t):
                    @pl.when(zs != z)
                    def _(zs=zs):
                        arrived(tok_o, zs, a2a_r).wait_recv()
                        to_first(zs).start()

    def ff_steps(i):
        @pl.loop(0, COUNT[GU])
        def _(n):
            gu_step(n, i)
        down_steps(i)

    for i in range(mb - 1):
        ff_steps(i)
    @pl.when(second_plane)
    def _():
        ff_steps(mb - 1)
        spread(cot, dmo, c2a_s, c2a_r)
        for i in range(mb):
            @pl.when(c * mb + i == z)
            def _(i=i):
                pltpu.make_async_copy(cot.at[i], dmo.at[block, :], loc.at[4]).start()

    @pl.when(first_plane & me.here)
    def _():
        for zs in range(n_t):
            @pl.when(zs != z)
            def _(zs=zs):
                to_first(zs).wait_recv()
        pltpu.make_async_copy(tok.at[0], x_v.at[block, :], loc.at[4]).wait()
        remote(x_v, x_v, sib.at[0], sib.at[1], me.sibling).start()

    @pl.when(jnp.logical_not(me.here))
    def _():
        remote(len_v, len_v, lsem.at[0], lsem.at[1], me.sibling).wait_recv()
        pl.when(first_plane)(remote(x_v, x_v, sib.at[0], sib.at[1], me.sibling).wait_recv)

    length = len_v[0:1, :]

    @pl.when(me.here)
    def _():
        for w, (src, dst) in enumerate(own_slots):
            pltpu.make_async_copy(src, dst, loc.at[w]).wait()

    for j in range(mb):
        wait_slot(QKV, j)
        wait_slot(OUT, j)

    gain_one, gain_two = gains[0:1, :], gains[1:2, :]

    def chunk(r):
        return pl.ds(pl.multiple_of(r * rows, 128), rows)

    def halves(r, core):
        return x_v.at[pl.ds(pl.multiple_of(r * rows + core * (rows // 2), 16), rows // 2), :]

    def send_v(r):
        return remote(v_v.at[:, chunk(r), :], first.at[:, chunk(r), :], vsem.at[0, r], vsem.at[1, r], other_plane)

    def swap(buffer, r, sems):
        return remote(s1.at[chunk(r), :], buffer.at[chunk(r), :], sems.at[0, r], sems.at[1, r], me.sibling)

    def project(r):
        at = chunk(r)
        a = (normalise(x_v[at, :].astype(F32)) * gain_one).astype(BF)
        cos_r, sin_r = cos[at, :], sin[at, :]
        for j in range(mb):
            q = dot(a, w_qkv[j, 0])
            k = dot(a, w_qkv[j, 1])
            v = dot(a, w_qkv[j, 2])
            for n in range(cols // PAIR):
                p = j * (cols // PAIR) + n
                lanes = slice(n * PAIR, (n + 1) * PAIR)
                q_v[p, at, :] = (rotate_pair(q[:, lanes], cos_r, sin_r) * SCORE_SCALE).astype(BF)
                keys = rotate_pair(k[:, lanes], cos_r, sin_r).astype(BF).astype(F32)
                ka_v[p, at, :], kb_v[p, at, :] = head_keys(keys, length, r * rows)
                v_v[p, at, :] = v[:, lanes].astype(BF)

        @pl.when(first_plane)
        def _():
            send_v(r).start()
            for p in range(pairs):
                vals = v_v[p, at, :]
                vu_v[p, at, :] = vals
                vt_v[p, :, at] = vals.astype(F32).T.astype(BF)

        @pl.when(second_plane)
        def _():
            send_v(r).wait_recv()
            for p in range(pairs):
                vals = (0.5 * v_v[p, at, :].astype(F32) + 0.5 * first[p, at, :].astype(F32)).astype(BF)
                vu_v[p, at, :] = vals
                vt_v[p, :, at] = vals.astype(F32).T.astype(BF)

    def attention(r):
        for i in range(CHUNKS):
            @pl.when(r == i)
            def _(i=i):
                @pl.loop(0, pairs, unroll=2)
                def _(p):
                    lanes = pl.ds(pl.multiple_of(p * PAIR, PAIR), PAIR)

                    def put_out(lo, hi, value):
                        o_v[lo:hi, lanes] = value

                    def put_lse(h, lo, hi, value):
                        lse_v[p, h:h + 1, lo:hi] = value

                    attend_block(
                        i, rows, q_v[p, i * rows:(i + 1) * rows, :],
                        lambda h, lo, hi: (ka_v, kb_v)[h][p, lo:hi, :],
                        lambda vh, lo, hi: vt_v[p, vh, lo:hi],
                        put_out, put_lse,
                    )

    def mix(r):
        at = chunk(r)
        swap(r1, r, e1).wait_recv()
        h = x_v[at, :].astype(F32) + s1[at, :].astype(F32) + r1[at, :].astype(F32)
        h_v[at, :] = h
        b = (normalise(h) * gain_two).astype(BF)
        b_v[at, :] = b
        grown = None
        for j in range(mb):
            gate = dot_nt(b, w_ff[j, 1])
            up = dot_nt(b, w_ff[j, 2])
            m = (gate / (1.0 + jnp.exp(-gate)) * up).astype(BF)
            g_v[j, at, :] = gate.astype(BF)
            u_v[j, at, :] = up.astype(BF)
            m_v[j, at, :] = m
            term = dot(m, w_ff[j, 0])
            grown = term if grown is None else grown + term
        swap(r1, r, e1).wait_send()
        s1[at, :] = grown.astype(BF)
        swap(r2, r, e2).start()

    def finish(r):
        at = chunk(r)
        swap(r2, r, e2).wait_recv()
        r2[at, :] = (h_v[at, :] + s1[at, :].astype(F32) + r2[at, :].astype(F32)).astype(BF)

        @pl.when(first_plane)
        def _():
            mine = pl.ds(pl.multiple_of(r * rows + c * (rows // 2), 16), rows // 2)
            remote(
                r2.at[mine, :], x_v.at[mine, :], hop.at[0, r], hop.at[1, r], other_plane
            ).start()

    def mix_all(r):
        mix(r)

        @pl.when(r > 0)
        def _():
            finish(r - 1)

    @pl.when(second_plane)
    def _():
        for j in range(mb):
            wait_slot(GU, j)
            wait_slot(DOWN, j)

    @pl.loop(0, CHUNKS)
    def _(r):
        @pl.when(first_plane)
        def _():
            gu_step(r, mb - 1)

        @pl.when(second_plane)
        def _():
            mine, theirs = halves(r, c), halves(r, 1 - c)
            remote(mine, mine, hop.at[0, r], hop.at[1, r], me.sibling).wait_recv()
            remote(mine, mine, hsib.at[0, r], hsib.at[1, r], me.sibling).start()
            remote(theirs, theirs, hsib.at[0, r], hsib.at[1, r], me.sibling).wait_recv()

        project(r)
        attention(r)
        s1[chunk(r), :] = dot(o_v[chunk(r), :], w_out[...]).astype(BF)
        swap(r1, r, e1).start()

        @pl.when(second_plane & (r > 0))
        def _():
            mix_all(r - 1)

    pl.when(second_plane)(lambda: mix_all(CHUNKS - 1))
    @pl.when(second_plane & me.here)
    def _():
        for zs in range(n_t):
            @pl.when(zs != z)
            def _(zs=zs):
                arrived(dmo, zs, c2a_r).wait_recv()
        pltpu.make_async_copy(cot.at[0], dmo.at[block, :], loc.at[4]).wait()
        remote(dmo, dmo, sib.at[0], sib.at[1], me.sibling).start()

    @pl.when(first_plane)
    def _():
        down_steps(mb - 1)
        for j in range(mb):
            wait_slot(GU, j)
            wait_slot(DOWN, j)

        pl.loop(0, CHUNKS)(mix_all)

    finish(CHUNKS - 1)
    for w, n in ((QKV, 1), (OUT, 0), (DOWN, 0), (DOWN, 1)):
        own_wait(w, n)
    for w in range(4):
        for n in range(COUNT[w]):
            k = BASE[w] + n
            for j in range(mb):
                s = c * mb + j

                @pl.when(s != z)
                def _(w=w, n=n, k=k, j=j, s=s):
                    piece = slot_part(w, n, j, x)
                    for d in range(1, nx):
                        remote(piece, piece, x_s.at[k, j, d], x_r.at[k, j, x], me.right).wait_send()
                    forwarded = ((s < z) & (z < n_t - 1)) | ((s > z) & (z > 0))
                    pl.when(forwarded)(remote(piece, piece, z_f.at[k, j], z_r.at[k, j], me.right).wait_send)

    @pl.when(second_plane)
    def _():
        for i in range(mb):
            @pl.when(c * mb + i != z)
            def _(i=i):
                remote(tok.at[i], tok.at[i], a2a_s.at[i], a2a_r.at[z], me.right).wait_send()
                remote(tok.at[i], tok.at[i], c2a_s.at[i], c2a_r.at[z], me.right).wait_send()

        @pl.when(me.here)
        def _():
            for zs in range(n_t):
                @pl.when(zs != z)
                def _(zs=zs):
                    to_first(zs).wait_send()

    @pl.when(me.here)
    def _():
        remote(lens.at[jz], len_v, lsem.at[0], lsem.at[1], me.sibling).wait_send()
        pl.when(first_plane)(remote(x_v, x_v, sib.at[0], sib.at[1], me.sibling).wait_send)
        pl.when(second_plane)(remote(dmo, dmo, sib.at[0], sib.at[1], me.sibling).wait_send)

    @pl.when(second_plane & jnp.logical_not(me.here))
    def _():
        remote(dmo, dmo, sib.at[0], sib.at[1], me.sibling).wait_recv()

    for r in range(CHUNKS):
        swap(r2, r, e2).wait_send()
        pl.when(first_plane)(send_v(r).wait_send)
        mine = halves(r, c)
        pl.when(first_plane)(remote(mine, mine, hop.at[0, r], hop.at[1, r], me.sibling).wait_send)
        pl.when(second_plane)(remote(mine, mine, hsib.at[0, r], hsib.at[1, r], me.sibling).wait_send)


LAG = 2
AHEAD = 3
FF, OUTS, HEADS = range(3)
FF_PIECES = 6
PIECES = [(FF, n) for n in range(FF_PIECES)] + [(OUTS, 0), (HEADS, 0), (HEADS, 1)]
KEY = (0, FF_PIECES, FF_PIECES + 1)


def attend_back_block(i, blk, queries, keys, keys_t, vals, outs, grads, stats, add_dv, add_dk):
    lo, hi = i * blk, (i + 1) * blk
    visible = causal_block(blk)
    queries, grads = queries.astype(F32), grads.astype(F32)
    product = (grads * outs.astype(F32)).T
    parts = []
    for h in range(2):
        qh, qz, gh = head_queries(h, queries, 1.0), head_queries(h, queries, 0.0), head_queries(h, grads, 0.0)
        rows_h = slice(h * HD, (h + 1) * HD)
        delta = jnp.sum(product[rows_h], axis=0, keepdims=True)
        stat = stats(h, lo, hi)

        def side(a, b, diagonal):
            p = jnp.exp(dot_nt(keys(h, a, b), qh) - stat)
            if diagonal:
                p = jnp.where(visible, p, 0.0)
            ds = (p * (dot_nt(vals(a, b), gh) - delta)).astype(BF)
            fresh = i == CHUNKS - 1 and h == 0
            add_dv(a, b, dot(p.astype(BF), gh), fresh)
            add_dk(a, b, dot(ds, qz), fresh)
            return dot(keys_t(rows_h, a, b), ds)

        dq_t = side(lo, hi, True)
        if i:
            dq_t = dq_t + side(0, lo, False)
        parts.append(dq_t)
    return jnp.concatenate(parts, axis=0).T * SCORE_SCALE


def norm_back(values, gain, grad):
    scale = lax.rsqrt(jnp.mean(values * values, axis=-1, keepdims=True) + NORM_EPS)
    unit = values * scale
    inner = grad * gain
    back = scale * (inner - unit * jnp.mean(inner * unit, axis=-1, keepdims=True))
    return back, jnp.sum(grad * unit, axis=0, keepdims=True)


def backward_part(
    me, gains, cos, sin, o_y, o_dx, o_qkv, o_out, o_gu, o_down, o_gain, lx_ff, lx_out, lx_qkv, lz_ff, lz_out, lz_qkv,
    w_qkv, w_out, w_ff, x_v, q_v, ka_v, kb_v, kt_v, vu_v, o_v, lse_v, h_v, b_v, g_v, u_v, m_v,
    dmo, do_v, first, s1, r1, r2, len_v, dk_a, dv_a, st_ff, st_out, st_qkv, g_z, g_x,
    loc, a2a_s, a2a_r, hop, hsib, e1, e2, vsem, x_s, x_r, z_s, z_r, zo_r, f_s, f_r, f_l, stage, gz_s, gz_r, gx_s, gx_r,
    free,
):
    mb, block_rows, dim = o_y.shape
    x, c, z, n_t, nx, jz = me.x, me.c, me.z, me.n_t, me.nx, me.jz
    part = dim // nx
    quarter = part // 2
    cols, ow, half = w_qkv.shape[3], w_out.shape[0] // mb, w_ff.shape[2] // 2
    seq = x_v.shape[0]
    rows = seq // CHUNKS
    pairs = q_v.shape[0]
    slot_pairs = cols // PAIR
    first_plane, second_plane = me.section == 0, me.section == 1
    other_plane = {"section": 1 - me.section}

    def block(n):
        return pl.ds(pl.multiple_of(n * block_rows, 128), block_rows)

    def give_back(t, src, dst):
        @pl.when(me.here)
        def _():
            for d in range(1, n_t):
                to = lax.rem(z + d, n_t)
                remote(src.at[block(to), :], dst.at[jz], a2a_s.at[t, d], a2a_r.at[t, jz], {"tensor": to}).start()
            pltpu.make_async_copy(src.at[block(z), :], dst.at[jz], loc.at[t]).start()

    give_back(0, r2, o_y)

    def chunk(r):
        return pl.ds(pl.multiple_of(r * rows, 128), rows)

    def half_rows(r, core):
        return dmo.at[pl.ds(pl.multiple_of(r * rows + core * (rows // 2), 16), rows // 2), :]

    def swap(buffer, r, sems):
        return remote(s1.at[chunk(r), :], buffer.at[chunk(r), :], sems.at[0, r], sems.at[1, r], me.sibling)

    gain_one, gain_two = gains[0:1, :], gains[1:2, :]
    o_gain[...] = jnp.zeros_like(o_gain)

    def buffers_free(n):
        pl.semaphore_signal(free.at[n], inc=1, device_id=me.sibling, device_id_type=MESH)

    def y_sent():
        @pl.when(me.here)
        def _():
            for d in range(1, n_t):
                there = r2.at[block(0), :]
                remote(there, o_y.at[0], a2a_s.at[0, d], a2a_r.at[0, jz], me.right).wait_send()
            pltpu.make_async_copy(r2.at[block(z), :], o_y.at[jz], loc.at[0]).wait()

    buffers_free(0)
    pl.semaphore_wait(free.at[0], 1)

    def finish_mixed(r):
        at = chunk(r)
        swap(r1, r, e1).wait_recv()
        db = s1[at, :].astype(F32) + r1[at, :].astype(F32)
        back, gain = norm_back(h_v[at, :], gain_two, db)
        o_gain[1:2, :] += gain
        dh = dmo[at, :].astype(F32) + back
        h_v[at, :] = dh
        back_out = dot_nt(dh.astype(BF), w_out[...]).astype(BF)
        for p in range(pairs):
            do_v[p, at, :] = back_out[:, p * PAIR:(p + 1) * PAIR]

    def expand(r):
        at = chunk(r)

        @pl.when(first_plane)
        def _():
            mine, theirs = half_rows(r, c), half_rows(r, 1 - c)
            remote(mine, mine, hop.at[0, r], hop.at[1, r], me.sibling).wait_recv()
            remote(mine, mine, hsib.at[0, r], hsib.at[1, r], me.sibling).start()
            remote(theirs, theirs, hsib.at[0, r], hsib.at[1, r], me.sibling).wait_recv()

        @pl.when(second_plane)
        def _():
            position = (r * rows + lax.broadcasted_iota(jnp.int32, (rows, dim), 0)).astype(F32)
            dmo[at, :] = jnp.where(position < len_v[0:1, 0:1], dmo[at, :].astype(F32), 0.0).astype(BF)

        dy = dmo[at, :]
        total = None
        for j in range(mb):
            dm = dot_nt(dy, w_ff[j, 0])
            gate, up = g_v[j, at, :].astype(F32), u_v[j, at, :].astype(F32)
            sig = 1.0 / (1.0 + jnp.exp(-gate))
            d_gate = (dm * up * (sig * (1.0 + gate * (1.0 - sig)))).astype(BF)
            d_up = (dm * (gate * sig)).astype(BF)
            g_v[j, at, :] = d_gate
            u_v[j, at, :] = d_up
            term = dot(d_gate, w_ff[j, 1]) + dot(d_up, w_ff[j, 2])
            total = term if total is None else total + term
        s1[at, :] = total.astype(BF)
        swap(r1, r, e1).start()

    def ff_grads(t):
        left = (m_v, g_v, u_v)[t]
        right = (dmo, b_v, b_v)[t]

        @pl.loop(0, mb)
        def _(j):
            @pl.loop(0, 2)
            def _(n):
                lanes = pl.ds(pl.multiple_of(n * (dim // 2), 128), dim // 2)
                w_ff[j, t, :, lanes] = dot_tn(left[j], right[:, lanes]).astype(BF)

    def column(p):
        return pl.ds(pl.multiple_of(p * part, 128), part)

    def order(i):
        return jnp.where(c == 0, i, mb - 1 - i)

    def key(kind, n):
        return KEY[kind] + n

    def half_of(n):
        return pl.ds(pl.multiple_of(lax.rem(n, 2) * half, 16), half)

    def grad_part(kind, n, j, p):
        if kind == FF:
            return w_ff.at[j, n // 2, half_of(n), column(p)]
        if kind == OUTS:
            return w_out.at[pl.ds(pl.multiple_of(j * ow, 16), ow), column(p)]
        return w_qkv.at[j, :, pl.ds(pl.multiple_of(p * part + n * quarter, 16), quarter), :]

    def landing(bufs, kind, n, slot):
        if kind == FF:
            return bufs[FF].at[slot, n // 2, half_of(n), :]
        if kind == OUTS:
            return bufs[OUTS].at[slot]
        return bufs[HEADS].at[slot, :, pl.ds(n * quarter, quarter), :]

    def land_x(kind, n, j, d):
        return landing([b.at[d - 1] for b in (lx_ff, lx_out, lx_qkv)], kind, n, j)

    def land_z(kind, n, slot):
        return landing((lz_ff, lz_out, lz_qkv), kind, n, slot)

    def staged(kind, slot):
        return (st_ff, st_out, st_qkv)[kind].at[slot]

    def x_copies(kind, n, j):
        k = key(kind, n)
        for d in range(1, nx):
            to = lax.rem(x + d, nx)
            yield d, remote(
                grad_part(kind, n, j, to), land_x(kind, n, j, d), x_s.at[k, j, d], x_r.at[k, j, d], me.at_x(d)
            )

    def x_start(kind, n, i):
        for _, copy in x_copies(kind, n, order(i)):
            copy.start()

    def reduce_step(kind, n, i):
        k, j = key(kind, n), order(i)
        s = c * mb + j
        mine = grad_part(kind, n, j, x)
        outer = ((s > z) & (z > 0)) | ((s < z) & (z < n_t - 1))
        fetch = [pltpu.make_async_copy(land_x(kind, n, j, d), staged(kind, d - 1), stage.at[d - 1]) for d in range(1, nx)]
        from_z = land_z(kind, n, j)
        fetch_z = pltpu.make_async_copy(from_z, staged(kind, nx - 1), stage.at[nx - 1])
        for d, copy in x_copies(kind, n, j):
            copy.wait_recv()
            fetch[d - 1].start()

        @pl.when(outer)
        def _():
            remote(from_z, from_z, z_s.at[k, j], z_r.at[k, j], me.right).wait_recv()
            fetch_z.start()

        for copy in fetch:
            copy.wait()
        total = mine[...].astype(F32)
        for d in range(1, nx):
            total = total + staged(kind, d - 1)[...].astype(F32)
        mine[...] = total.astype(BF)

        @pl.when(outer)
        def _():
            fetch_z.wait()
            mine[...] = (mine[...].astype(F32) + staged(kind, nx - 1)[...].astype(F32)).astype(BF)

        pl.when(s > z)(remote(mine, land_z(kind, n, j), z_s.at[k, j], z_r.at[k, j], me.right).start)
        pl.when(s < z - 1)(remote(mine, land_z(kind, n, j), z_s.at[k, j], z_r.at[k, j], me.left).start)
        pl.when(s == z - 1)(remote(mine, land_z(kind, n, mb), z_s.at[k, j], zo_r.at[k], me.left).start)

    def final_part(kind, n):
        if kind == FF:
            return o_down.at[half_of(n), :] if n < 2 else o_gu.at[n // 2 - 1, half_of(n), :]
        return o_out if kind == OUTS else o_qkv

    def final_copies(kind, n):
        k, target, mine = key(kind, n), final_part(kind, n), grad_part(kind, n, jz, x)
        cases = []
        for core in range(2):
            if kind == HEADS:
                stays = theirs = mine
            else:
                stays = mine.at[:, core * quarter:(core + 1) * quarter]
                theirs = mine.at[:, (1 - core) * quarter:(2 - core) * quarter]
            if kind != HEADS or core == n:
                cases.append((c == core, pltpu.make_async_copy(stays, target, f_l.at[k]), True))
            if kind != HEADS or core != n:
                cases.append((c == core, remote(theirs, target, f_s.at[k], f_r.at[k], me.sibling), False))
        return cases

    def own_piece(kind, n):
        k = key(kind, n)
        mine = grad_part(kind, n, jz, x)

        @pl.when(me.here)
        def _():
            sides = ((z > 0, land_z(kind, n, jz), z_r.at[k, jz], 0), (z < n_t - 1, land_z(kind, n, mb), zo_r.at[k], nx - 1))
            for there, src, sem, slot in sides:
                @pl.when(there)
                def _(src=src, sem=sem, slot=slot):
                    remote(src, src, f_s.at[k], sem, me.right).wait_recv()
                    pltpu.make_async_copy(src, staged(kind, slot), stage.at[slot]).start()
            for there, src, sem, slot in sides:
                @pl.when(there)
                def _(src=src, slot=slot):
                    pltpu.make_async_copy(src, staged(kind, slot), stage.at[slot]).wait()
                    mine[...] = (mine[...].astype(F32) + staged(kind, slot)[...].astype(F32)).astype(BF)
            for case, copy, _ in final_copies(kind, n):
                pl.when(case)(copy.start)

    n_k = len(PIECES)

    def ahead(index):
        if index + AHEAD < n_k * mb:
            piece, i = divmod(index + AHEAD, mb)
            x_start(*PIECES[piece], i)

    def begin_reduce():
        for index in range(AHEAD):
            x_start(FF, index // mb, index % mb)

    def ff_round(n):
        for i in range(mb):
            n_next, i_next = n + (i + AHEAD) // mb, (i + AHEAD) % mb

            @pl.when(n_next < FF_PIECES)
            def _(n_next=n_next, i_next=i_next):
                x_start(FF, n_next, i_next)
            reduce_step(FF, n, i)

    def send_dv(r):
        return remote(vu_v.at[:, chunk(r), :], first.at[:, chunk(r), :], vsem.at[0, r], vsem.at[1, r], other_plane)

    def attention(r):
        at = chunk(r)
        for i in range(CHUNKS):
            @pl.when(r == i)
            def _(i=i):
                block_rows_i = slice(i * rows, (i + 1) * rows)

                @pl.loop(0, pairs, unroll=2)
                def _(p):
                    lanes = pl.ds(pl.multiple_of(p * PAIR, PAIR), PAIR)

                    def add_to(acc):
                        def add(a, b, value, fresh):
                            if fresh:
                                acc[p, a:b, :] = value
                            else:
                                acc[p, a:b, :] += value
                        return add

                    dq = attend_back_block(
                        i, rows, q_v[p, block_rows_i, :],
                        lambda h, a, b: (ka_v, kb_v)[h][p, a:b, :],
                        lambda rows_h, a, b: kt_v[p, rows_h, a:b],
                        lambda a, b: vu_v[p, a:b, :],
                        o_v[block_rows_i, lanes], do_v[p, block_rows_i, :],
                        lambda h, lo, hi: lse_v[p, h:h + 1, lo:hi],
                        add_to(dv_a), add_to(dk_a),
                    )
                    q_v[p, block_rows_i, :] = rotate_pair(
                        dq, cos[block_rows_i, :], -sin[block_rows_i, :]
                    ).astype(BF)

        pl.when(first_plane)(lambda: send_dv(r).wait_recv())
        for p in range(pairs):
            ka_v[p, at, :] = rotate_pair(dk_a[p, at, :], cos[at, :], -sin[at, :]).astype(BF)

            @pl.when(first_plane)
            def _(p=p):
                vu_v[p, at, :] = (dv_a[p, at, :] + first[p, at, :].astype(F32)).astype(BF)

            @pl.when(second_plane)
            def _(p=p):
                vu_v[p, at, :] = (0.5 * dv_a[p, at, :]).astype(BF)

    def slot_rows(t, j, at):
        source = (q_v, ka_v, vu_v)[t]
        return jnp.concatenate([source[j * slot_pairs + n, at, :] for n in range(slot_pairs)], axis=1)

    def finish_input(r):
        at = chunk(r)
        swap(r2, r, e2).wait_recv()
        da = s1[at, :].astype(F32) + r2[at, :].astype(F32)
        back, gain = norm_back(x_v[at, :].astype(F32), gain_one, da)
        o_gain[0:1, :] += gain
        r2[at, :] = (h_v[at, :] + back).astype(BF)

        @pl.when(second_plane)
        def _():
            mine = pl.ds(pl.multiple_of(r * rows + c * (rows // 2), 16), rows // 2)
            remote(r2.at[mine, :], dmo.at[mine, :], hop.at[0, r], hop.at[1, r], other_plane).start()

    def input_part(r):
        total = None
        for j in range(mb):
            for t in range(3):
                term = dot_nt(slot_rows(t, j, chunk(r)), w_qkv[j, t])
                total = term if total is None else total + term
        swap(r1, r, e1).wait_send()
        s1[chunk(r), :] = total.astype(BF)
        swap(r2, r, e2).start()

    def back(t):
        return CHUNKS - 1 - t

    @pl.when(first_plane)
    def _():
        @pl.loop(0, CHUNKS)
        def _(t):
            expand(back(t))

            @pl.when(t > 0)
            def _():
                finish_mixed(back(t - 1))

        ff_grads(0)
        finish_mixed(0)
        begin_reduce()
        ff_grads(1)
        ff_grads(2)

    @pl.when(second_plane)
    def _():
        expand(CHUNKS - 1)

    @pl.loop(0, pairs)
    def _(p):
        inside, _ = head_views(0, (seq, PAIR))
        kt_v[p] = jnp.where(inside, ka_v[p].astype(F32), kb_v[p].astype(F32)).T.astype(BF)

    y_sent()
    buffers_free(1)
    pl.semaphore_wait(free.at[1], 1)

    @pl.loop(0, CHUNKS)
    def _(t):
        r = back(t)
        pl.when(first_plane)(lambda: ff_round(t))

        @pl.when(second_plane)
        def _():
            pl.when(t < CHUNKS - 1)(lambda: expand(back(t + 1)))
            finish_mixed(r)

        attention(r)
        input_part(r)

        @pl.when(t > 0)
        def _():
            finish_input(back(t - 1))

    finish_input(0)

    @pl.when(second_plane)
    def _():
        for t in range(CHUNKS):
            send_dv(back(t)).start()

    give_back(1, r2, o_dx)
    for d in range(1, n_t):
        remote(o_gain, g_z.at[d], gz_s.at[d], gz_r.at[d], {"tensor": lax.rem(z + d, n_t)}).start()

    @pl.when(second_plane)
    def _():
        for t in range(3):
            ff_grads(t)
        begin_reduce()

    @pl.loop(0, 4)
    def _(n):
        lanes = pl.ds(pl.multiple_of(n * (dim // 4), 128), dim // 4)
        w_out[:, lanes] = dot_tn(o_v[...], h_v[:, lanes].astype(BF)).astype(BF)

    everything = pl.ds(0, seq)

    @pl.loop(0, CHUNKS)
    def _(r):
        b_v[chunk(r), :] = (normalise(x_v[chunk(r), :].astype(F32)) * gain_one).astype(BF)

    @pl.loop(0, mb)
    def _(j):
        for t in range(3):
            w_qkv[j, t] = dot_tn(b_v[...], slot_rows(t, j, everything)).astype(BF)

    @pl.when(second_plane)
    def _():
        @pl.loop(0, pairs)
        def _(p):
            ff_round(p)

    for index in range(FF_PIECES * mb, min(pairs * mb + AHEAD, n_k * mb)):
        x_start(*PIECES[index // mb], index % mb)
    for piece in range(pairs, n_k):
        for i in range(mb):
            ahead(piece * mb + i)
            reduce_step(*PIECES[piece], i)
        for done in range(piece - LAG) if piece == pairs else (piece - LAG,):
            own_piece(*PIECES[done])
        if piece == pairs:
            own_piece(*PIECES[piece - LAG])
    for piece in range(n_k - LAG, n_k):
        own_piece(*PIECES[piece])

    for d in range(1, n_t):
        remote(o_gain, g_z.at[d], gz_s.at[d], gz_r.at[d], me.right).wait()
    g_z[0] = o_gain[...]
    for d in range(1, n_t):
        g_z[0] += g_z[d]
    for d in range(1, nx):
        remote(g_z.at[0], g_x.at[d], gx_s.at[d], gx_r.at[d], me.at_x(d)).start()
    for d in range(1, nx):
        remote(g_z.at[0], g_x.at[d], gx_s.at[d], gx_r.at[d], me.at_x(d)).wait()
    o_gain[...] = g_z[0]
    for d in range(1, nx):
        o_gain[...] += g_x[d]

    @pl.when(jnp.logical_not(me.here))
    def _():
        for kind, n in PIECES:
            k, target = key(kind, n), final_part(kind, n)
            taken = remote(target, target, f_s.at[k], f_r.at[k], me.sibling)
            if kind == HEADS:
                pl.when(c == n)(taken.wait_recv)
            else:
                taken.wait_recv()

    for kind, n in PIECES:
        k = key(kind, n)
        for j in range(mb):
            for _, copy in x_copies(kind, n, j):
                copy.wait_send()
            mine = grad_part(kind, n, j, x)
            pl.when(c * mb + j != z)(remote(mine, mine, z_s.at[k, j], z_r.at[k, j], me.right).wait_send)

    @pl.when(me.here)
    def _():
        for kind, n in PIECES:
            for case, copy, local in final_copies(kind, n):
                pl.when(case)(copy.wait if local else copy.wait_send)
        for d in range(1, n_t):
            there = r2.at[block(0), :]
            remote(there, o_dx.at[0], a2a_s.at[1, d], a2a_r.at[1, jz], me.right).wait_send()
        pltpu.make_async_copy(r2.at[block(z), :], o_dx.at[jz], loc.at[1]).wait()

    for t, dst in enumerate((o_y, o_dx)):
        for i in range(mb):
            @pl.when(c * mb + i != z)
            def _(t=t, i=i, dst=dst):
                remote(dst.at[i], dst.at[i], a2a_s.at[t, 0], a2a_r.at[t, i], me.right).wait_recv()

    for r in range(CHUNKS):
        swap(r2, r, e2).wait_send()
        mine = half_rows(r, c)
        pl.when(second_plane)(remote(mine, mine, hop.at[0, r], hop.at[1, r], me.sibling).wait_send)
        pl.when(first_plane)(remote(mine, mine, hsib.at[0, r], hsib.at[1, r], me.sibling).wait_send)
        pl.when(second_plane)(send_dv(r).wait_send)


def layer_kernel(
    tok, cot, lens, qkv, out, gu, down, gains, cos, sin,
    o_y, o_dx, o_qkv, o_out, o_gu, o_down, o_gain, tok_o, lx_ff, lx_out, lx_qkv, lz_ff, lz_out, lz_qkv,
    w_qkv, w_out, w_ff, x_v, first, q_v, ka_v, kb_v, vt_v, v_v, vu_v, o_v, lse_v, h_v, b_v, g_v, u_v, m_v,
    s1, r1, r2, dmo, len_v, dk_a, dv_a, st_ff, st_out, st_qkv, g_z, g_x,
    *sems,
):
    me = Place(tok.shape[0])
    me.meet()
    forward_part(
        me, tok, cot, lens, qkv, out, gu, down, gains, cos, sin, tok_o,
        w_qkv, w_out, w_ff, x_v, first, q_v, ka_v, kb_v, vt_v, v_v, vu_v, o_v, lse_v, h_v, b_v, g_v, u_v, m_v,
        s1, r1, r2, dmo, len_v, *sems[:20],
    )
    backward_part(
        me, gains, cos, sin, o_y, o_dx, o_qkv, o_out, o_gu, o_down, o_gain,
        lx_ff, lx_out, lx_qkv, lz_ff, lz_out, lz_qkv,
        w_qkv, w_out, w_ff, x_v, q_v, ka_v, kb_v, vt_v, vu_v, o_v, lse_v, h_v, b_v, g_v, u_v, m_v,
        dmo, v_v, first, s1, r1, r2, len_v, dk_a, dv_a, st_ff, st_out, st_qkv, g_z, g_x, *sems[20:],
    )


def layer(tokens, cotangent, lens, qkv, out, gu, down, gains, tables):
    mb, block_rows, dim = tokens.shape
    n_t, n_dp = lax.axis_size("tensor"), lax.axis_size("dp")
    nx = n_dp // 2
    seq = block_rows * n_t
    part, quarter = dim // nx, dim // n_dp
    cols, ow, ff = qkv.shape[3], out.shape[1], down.shape[1]
    pairs = mb * cols // PAIR
    assert pairs == COUNT[GU] == CHUNKS
    dma = pltpu.SemaphoreType.DMA
    wide, heads, turned = (seq, dim), (pairs, seq, PAIR), (pairs, PAIR, seq)
    hidden, block = (mb, seq, ff), (mb, block_rows, dim)
    n_k = len(PIECES)
    shape = lambda s, t=BF: jax.ShapeDtypeStruct(s, t)
    vmem = lambda s, t=BF: pltpu.VMEM(s, t)

    def parts(lead, split):
        return (*lead, 3, ff, split), (*lead, ow, split), (*lead, 3, split, cols)

    return pl.pallas_call(
        layer_kernel,
        out_shape=(
            shape(block), shape(block),
            shape((3, quarter, cols)), shape((ow, quarter)), shape((2, ff, quarter)), shape((ff, quarter)),
            shape((2, dim), F32), shape(wide),
            *(shape(s) for s in parts((nx - 1, mb), part)),
            *(shape(s) for s in parts((mb + 1,), part)),
        ),
        in_specs=[ANY, ANY, VMEM, ANY, ANY, ANY, ANY, VMEM, VMEM, VMEM],
        out_specs=(*(ANY,) * 6, VMEM, *(ANY,) * 7),
        scratch_shapes=[
            vmem((mb, 3, dim, cols)), vmem((mb * ow, dim)), vmem((mb, 3, ff, dim)),
            vmem(wide), *[vmem(heads)] * 4, vmem(turned), *[vmem(heads)] * 2,
            vmem((seq, pairs * PAIR)), vmem((pairs, 2, seq), F32), vmem(wide, F32), vmem(wide), *[vmem(hidden)] * 3,
            *[vmem(wide)] * 4, vmem((8, 128), F32), *[vmem(heads, F32)] * 2,
            vmem((nx, ff // 2, part)), vmem((nx, ow, part)), vmem((nx, 3, quarter, cols)),
            vmem((n_t, 2, dim), F32), vmem((nx, 2, dim), F32),
            dma((5,)), dma((mb,)), dma((n_t,)), dma((mb,)), dma((n_t,)), dma((n_t,)), dma((n_t,)), dma((2,)),
            dma((N_PIECES,)), dma((N_PIECES,)), dma((N_PIECES, mb)), dma((N_PIECES, mb)),
            dma((N_PIECES, mb, nx)), dma((N_PIECES, mb, nx)),
            *[dma((2, CHUNKS))] * 5, dma((2,)),
            dma((2,)), dma((2, n_t)), dma((2, mb)), *[dma((2, CHUNKS))] * 5,
            dma((n_k, mb, nx)), dma((n_k, mb, nx)), dma((n_k, mb)), dma((n_k, mb)), *[dma((n_k,))] * 4,
            dma((nx,)), dma((n_t,)), dma((n_t,)), dma((nx,)), dma((nx,)), pltpu.SemaphoreType.REGULAR((2,)),
        ],
        compiler_params=pltpu.CompilerParams(
            collective_id=0, has_side_effects=True, vmem_limit_bytes=63 << 20
        ),
        name="layer",
    )(tokens, cotangent, lens, qkv, out, gu, down, gains, *tables)


def publish_kernel(*refs):
    count = len(refs) // 3
    sources, targets, held, sems = refs[:count], refs[count:2 * count], refs[2 * count:3 * count], refs[-1]
    copies = [pltpu.make_async_copy(src, dst, sems.at[n]) for n, (src, dst) in enumerate(zip(sources, held))]
    for copy in copies:
        copy.start()
    for copy, dst, src in zip(copies, targets, held):
        copy.wait()
        dst[...] = src[...].astype(dst.dtype)


def publish(*arrays):
    types = (BF,) + (F32,) * (len(arrays) - 1)
    return pl.pallas_call(
        publish_kernel,
        out_shape=tuple(jax.ShapeDtypeStruct(a.shape, t) for a, t in zip(arrays, types)),
        in_specs=[ANY] * len(arrays),
        out_specs=(VMEM,) * len(arrays),
        scratch_shapes=[*(pltpu.VMEM(a.shape, a.dtype) for a in arrays), pltpu.SemaphoreType.DMA((len(arrays),))],
        compiler_params=pltpu.CompilerParams(vmem_limit_bytes=60 << 20),
        name="publish",
    )(*arrays)


def shards(tokens, lengths, qkv_weight, out_weight, gate_up_weight, down_weight, norm_gains, cotangent):
    dp, z = lax.axis_index("dp"), lax.axis_index("tensor")
    mb, rows, dim = tokens.shape
    n_t = lax.axis_size("tensor")
    tables = tuple(jnp.asarray(t) for t in rope_tables(rows * n_t))
    lens = jnp.broadcast_to(lengths.astype(F32)[:, None, None], (mb, 8, 128))
    o_y, o_dx, o_qkv, o_out, o_gu, o_down, gain = layer(
        tokens, cotangent, lens, qkv_weight, out_weight, jnp.swapaxes(gate_up_weight, 2, 3), down_weight,
        norm_gains[0], tables,
    )[:7]
    share = dim // (lax.axis_size("dp") * n_t)
    gain = lax.dynamic_slice_in_dim(gain, (dp * n_t + z) * share, share, 1)
    o_y, o_dx, o_qkv, o_out, o_gu, o_down = publish(o_y, o_dx, o_qkv, o_out, o_gu, o_down)
    return (
        o_y[None], o_dx[None], o_qkv[None], o_out[None], jnp.swapaxes(o_gu, 1, 2)[None], o_down[None],
        gain[None],
    )


def solution(mesh):
    in_specs = (
        P("dp", "tensor", None),
        P("dp"),
        P("section", None, None, "tensor"),
        P("section", "tensor", None),
        P("section", None, None, "tensor"),
        P("section", "tensor", None),
        P("section", None, None),
        P("dp", "tensor", None),
    )
    out_specs = (
        P("section", "dp", "tensor", None),
        P("section", "dp", "tensor", None),
        P("section", None, "dp", "tensor"),
        P("section", "tensor", "dp"),
        P("section", None, "dp", "tensor"),
        P("section", "tensor", "dp"),
        P("section", None, ("dp", "tensor")),
    )
    return jax.shard_map(shards, mesh=mesh, in_specs=in_specs, out_specs=out_specs, check_vma=False)
```

time: 492 us -> 462 us (0.939)
  the two profiles are of different devices: /device:TPU:0 before, /device:TPU:8 now
where the time goes in v4:
time: 462 us; the launch traced here: 454 us
  Pallas kernels  450 us (97%)
    pallas_call x1, Pallas kernels, layer(): pl.pallas_call(layer_kernel, out_shape=(shape(block), shape(block), shape...  445 us

profile of v4, /device:TPU:8, one launch (start us, length us, event | category | flops | bytes accessed | tf_op | source)
XLA Modules:
  0.0 453.6 jit_solution(15175842781974544329)
XLA Ops:
  0.6 0.7 convert_element_type.3
  1.3 0.7 broadcast_in_dim.27.lens
  2.0 445.2 %layer.1 = (bf16[2,256,1024]{2,1,0:T(8,128)(2,1)}, bf16[2,256,1024]{2,1,0:T(8,128)(2,1)}, bf16[3,256,256]{2,1,0:T(8,128)(2,1)}, bf16[256,256]{1,0:T(8,128)(2,1)}...) custom-call(bf16[2,256,1024]{2,1,0:T(8,128)(2,1)} %tok.1, ...), custom_call_target="tpu_custom_call" | custom-call | tf_op jit(solution)/shard_map/layer/pallas_call | solution.py:1118
  447.2 4.7 %publish.1 = (bf16[2,256,1024]{2,1,0:T(8,128)(2,1)}, f32[2,256,1024]{2,1,0:T(8,128)}, f32[3,256,256]{2,1,0:T(8,128)}, f32[256,256]{1,0:T(8,128)}, f32[2,704,256]{2,1,0:T(8,128)}, /*index=5*/f32[704,256]{1,0:T(8,128)}) custom-call(bf16[2,256,1024]{2,1,0:T(8,128)(2,1)} %get-tuple-element.20.refs_0_, bf16[2,256,1024]{2,1,0:T(8,128)(2,1)} %get-tuple-element.21.refs_1_, ...), custom_call_target="tpu_custom_call" | custom-call | tf_op jit(solution)/shard_map/publish/pallas_call | solution.py:1164
  451.9 1.3 dynamic-slice_bitcast_fusion

commit v5 on v4

--- a/solution.py
+++ b/solution.py
@@ -308,11 +308,10 @@
             gu_step(n, i)
         down_steps(i)
 
-    for i in range(mb - 1):
-        ff_steps(i)
     @pl.when(second_plane)
     def _():
-        ff_steps(mb - 1)
+        for i in range(mb):
+            ff_steps(i)
         spread(cot, dmo, c2a_s, c2a_r)
         for i in range(mb):
             @pl.when(c * mb + i == z)
@@ -411,25 +410,27 @@
                         put_out, put_lse,
                     )
 
-    def mix(r):
+    def enter(r):
         at = chunk(r)
         swap(r1, r, e1).wait_recv()
         h = x_v[at, :].astype(F32) + s1[at, :].astype(F32) + r1[at, :].astype(F32)
         h_v[at, :] = h
-        b = (normalise(h) * gain_two).astype(BF)
-        b_v[at, :] = b
-        grown = None
-        for j in range(mb):
-            gate = dot_nt(b, w_ff[j, 1])
-            up = dot_nt(b, w_ff[j, 2])
-            m = (gate / (1.0 + jnp.exp(-gate)) * up).astype(BF)
-            g_v[j, at, :] = gate.astype(BF)
-            u_v[j, at, :] = up.astype(BF)
-            m_v[j, at, :] = m
-            term = dot(m, w_ff[j, 0])
-            grown = term if grown is None else grown + term
+        b_v[at, :] = (normalise(h) * gain_two).astype(BF)
         swap(r1, r, e1).wait_send()
-        s1[at, :] = grown.astype(BF)
+
+    def through_slot(r, j):
+        at = chunk(r)
+        b = b_v[at, :]
+        gate = dot_nt(b, w_ff[j, 1])
+        up = dot_nt(b, w_ff[j, 2])
+        m = (gate / (1.0 + jnp.exp(-gate)) * up).astype(BF)
+        g_v[j, at, :] = gate.astype(BF)
+        u_v[j, at, :] = up.astype(BF)
+        m_v[j, at, :] = m
+        return dot(m, w_ff[j, 0])
+
+    def leave(r, grown):
+        s1[chunk(r), :] = grown.astype(BF)
         swap(r2, r, e2).start()
 
     def finish(r):
@@ -444,12 +445,15 @@
                 r2.at[mine, :], x_v.at[mine, :], hop.at[0, r], hop.at[1, r], other_plane
             ).start()
 
+    def finish_before(r):
+        @pl.when(r > 0)
+        def _():
+            finish(r - 1)
+
     def mix_all(r):
-        mix(r)
-
-        @pl.when(r > 0)
-        def _():
-            finish(r - 1)
+        enter(r)
+        leave(r, sum(through_slot(r, j) for j in range(mb)))
+        finish_before(r)
 
     @pl.when(second_plane)
     def _():
@@ -461,7 +465,7 @@
     def _(r):
         @pl.when(first_plane)
         def _():
-            gu_step(r, mb - 1)
+            gu_step(r, 0)
 
         @pl.when(second_plane)
         def _():
@@ -470,6 +474,15 @@
             remote(mine, mine, hsib.at[0, r], hsib.at[1, r], me.sibling).start()
             remote(theirs, theirs, hsib.at[0, r], hsib.at[1, r], me.sibling).wait_recv()
 
+        @pl.when(second_plane & me.here & (r == CHUNKS - 1))
+        def _():
+            for zs in range(n_t):
+                @pl.when(zs != z)
+                def _(zs=zs):
+                    arrived(dmo, zs, c2a_r).wait_recv()
+            pltpu.make_async_copy(cot.at[0], dmo.at[block, :], loc.at[4]).wait()
+            remote(dmo, dmo, sib.at[0], sib.at[1], me.sibling).start()
+
         project(r)
         attention(r)
         s1[chunk(r), :] = dot(o_v[chunk(r), :], w_out[...]).astype(BF)
@@ -480,23 +493,30 @@
             mix_all(r - 1)
 
     pl.when(second_plane)(lambda: mix_all(CHUNKS - 1))
-    @pl.when(second_plane & me.here)
-    def _():
-        for zs in range(n_t):
-            @pl.when(zs != z)
-            def _(zs=zs):
-                arrived(dmo, zs, c2a_r).wait_recv()
-        pltpu.make_async_copy(cot.at[0], dmo.at[block, :], loc.at[4]).wait()
-        remote(dmo, dmo, sib.at[0], sib.at[1], me.sibling).start()
 
     @pl.when(first_plane)
     def _():
+        down_steps(0)
+        for i in range(1, mb - 1):
+            ff_steps(i)
+        for i in range(mb - 1):
+            wait_slot(GU, order(i))
+            wait_slot(DOWN, order(i))
+
+        @pl.loop(0, CHUNKS)
+        def _(r):
+            gu_step(r, mb - 1)
+            enter(r)
+            s1[chunk(r), :] = sum(through_slot(r, order(i)) for i in range(mb - 1)).astype(BF)
+
         down_steps(mb - 1)
-        for j in range(mb):
-            wait_slot(GU, j)
-            wait_slot(DOWN, j)
-
-        pl.loop(0, CHUNKS)(mix_all)
+        wait_slot(GU, order(mb - 1))
+        wait_slot(DOWN, order(mb - 1))
+
+        @pl.loop(0, CHUNKS)
+        def _(r):
+            leave(r, s1[chunk(r), :].astype(F32) + through_slot(r, order(mb - 1)))
+            finish_before(r)
 
     finish(CHUNKS - 1)
     for w, n in ((QKV, 1), (OUT, 0), (DOWN, 0), (DOWN, 1)):
@@ -552,7 +572,7 @@
 AHEAD = 3
 FF, OUTS, HEADS = range(3)
 FF_PIECES = 6
-PIECES = [(FF, n) for n in range(FF_PIECES)] + [(OUTS, 0), (HEADS, 0), (HEADS, 1)]
+PIECES = [(FF, n) for n in range(FF_PIECES)] + [(OUTS, 0)] + [(HEADS, n) for n in range(4)]
 KEY = (0, FF_PIECES, FF_PIECES + 1)
 
 
@@ -603,7 +623,7 @@
     mb, block_rows, dim = o_y.shape
     x, c, z, n_t, nx, jz = me.x, me.c, me.z, me.n_t, me.nx, me.jz
     part = dim // nx
-    quarter = part // 2
+    quarter, eighth = part // 2, part // 4
     cols, ow, half = w_qkv.shape[3], w_out.shape[0] // mb, w_ff.shape[2] // 2
     seq = x_v.shape[0]
     rows = seq // CHUNKS
@@ -721,14 +741,14 @@
             return w_ff.at[j, n // 2, half_of(n), column(p)]
         if kind == OUTS:
             return w_out.at[pl.ds(pl.multiple_of(j * ow, 16), ow), column(p)]
-        return w_qkv.at[j, :, pl.ds(pl.multiple_of(p * part + n * quarter, 16), quarter), :]
+        return w_qkv.at[j, :, pl.ds(pl.multiple_of(p * part + n * eighth, 16), eighth), :]
 
     def landing(bufs, kind, n, slot):
         if kind == FF:
             return bufs[FF].at[slot, n // 2, half_of(n), :]
         if kind == OUTS:
             return bufs[OUTS].at[slot]
-        return bufs[HEADS].at[slot, :, pl.ds(n * quarter, quarter), :]
+        return bufs[HEADS].at[slot, :, pl.ds(n * eighth, eighth), :]
 
     def land_x(kind, n, j, d):
         return landing([b.at[d - 1] for b in (lx_ff, lx_out, lx_qkv)], kind, n, j)
@@ -787,7 +807,7 @@
     def final_part(kind, n):
         if kind == FF:
             return o_down.at[half_of(n), :] if n < 2 else o_gu.at[n // 2 - 1, half_of(n), :]
-        return o_out if kind == OUTS else o_qkv
+        return o_out if kind == OUTS else o_qkv.at[:, pl.ds(n % 2 * eighth, eighth), :]
 
     def final_copies(kind, n):
         k, target, mine = key(kind, n), final_part(kind, n), grad_part(kind, n, jz, x)
@@ -798,9 +818,9 @@
             else:
                 stays = mine.at[:, core * quarter:(core + 1) * quarter]
                 theirs = mine.at[:, (1 - core) * quarter:(2 - core) * quarter]
-            if kind != HEADS or core == n:
+            if kind != HEADS or core == n // 2:
                 cases.append((c == core, pltpu.make_async_copy(stays, target, f_l.at[k]), True))
-            if kind != HEADS or core != n:
+            if kind != HEADS or core != n // 2:
                 cases.append((c == core, remote(theirs, target, f_s.at[k], f_r.at[k], me.sibling), False))
         return cases
 
@@ -1038,7 +1058,7 @@
             k, target = key(kind, n), final_part(kind, n)
             taken = remote(target, target, f_s.at[k], f_r.at[k], me.sibling)
             if kind == HEADS:
-                pl.when(c == n)(taken.wait_recv)
+                pl.when(c == n // 2)(taken.wait_recv)
             else:
                 taken.wait_recv()
 
@@ -1131,7 +1151,7 @@
             vmem(wide), *[vmem(heads)] * 4, vmem(turned), *[vmem(heads)] * 2,
             vmem((seq, pairs * PAIR)), vmem((pairs, 2, seq), F32), vmem(wide, F32), vmem(wide), *[vmem(hidden)] * 3,
             *[vmem(wide)] * 4, vmem((8, 128), F32), *[vmem(heads, F32)] * 2,
-            vmem((nx, ff // 2, part)), vmem((nx, ow, part)), vmem((nx, 3, quarter, cols)),
+            vmem((nx, ff // 2, part)), vmem((nx, ow, part)), vmem((nx, 3, quarter // 2, cols)),
             vmem((n_t, 2, dim), F32), vmem((nx, 2, dim), F32),
             dma((5,)), dma((mb,)), dma((n_t,)), dma((mb,)), dma((n_t,)), dma((n_t,)), dma((n_t,)), dma((2,)),
             dma((N_PIECES,)), dma((N_PIECES,)), dma((N_PIECES, mb)), dma((N_PIECES, mb)),
@@ -1154,16 +1174,23 @@
     copies = [pltpu.make_async_copy(src, dst, sems.at[n]) for n, (src, dst) in enumerate(zip(sources, held))]
     for copy in copies:
         copy.start()
-    for copy, dst, src in zip(copies, targets, held):
+    for copy, dst, src in zip(copies[:-1], targets, held):
         copy.wait()
         dst[...] = src[...].astype(dst.dtype)
+    copies[-1].wait()
+    dim, share = held[-1].shape[1], targets[-1].shape[1]
+    place = lax.axis_index("dp") * lax.axis_size("tensor") + lax.axis_index("tensor")
+    targets[-1][...] = pltpu.roll(held[-1][...], lax.rem(dim - place * share, dim), 1)[:, :share]
 
 
 def publish(*arrays):
     types = (BF,) + (F32,) * (len(arrays) - 1)
+    gain = arrays[-1]
+    shapes = [a.shape for a in arrays[:-1]]
+    shapes.append((2, gain.shape[1] // (lax.axis_size("dp") * lax.axis_size("tensor"))))
     return pl.pallas_call(
         publish_kernel,
-        out_shape=tuple(jax.ShapeDtypeStruct(a.shape, t) for a, t in zip(arrays, types)),
+        out_shape=tuple(jax.ShapeDtypeStruct(a, t) for a, t in zip(shapes, types)),
         in_specs=[ANY] * len(arrays),
         out_specs=(VMEM,) * len(arrays),
         scratch_shapes=[*(pltpu.VMEM(a.shape, a.dtype) for a in arrays), pltpu.SemaphoreType.DMA((len(arrays),))],
@@ -1173,8 +1200,7 @@
 
 
 def shards(tokens, lengths, qkv_weight, out_weight, gate_up_weight, down_weight, norm_gains, cotangent):
-    dp, z = lax.axis_index("dp"), lax.axis_index("tensor")
-    mb, rows, dim = tokens.shape
+    mb, rows, _ = tokens.shape
     n_t = lax.axis_size("tensor")
     tables = tuple(jnp.asarray(t) for t in rope_tables(rows * n_t))
     lens = jnp.broadcast_to(lengths.astype(F32)[:, None, None], (mb, 8, 128))
@@ -1182,9 +1208,7 @@
         tokens, cotangent, lens, qkv_weight, out_weight, jnp.swapaxes(gate_up_weight, 2, 3), down_weight,
         norm_gains[0], tables,
     )[:7]
-    share = dim // (lax.axis_size("dp") * n_t)
-    gain = lax.dynamic_slice_in_dim(gain, (dp * n_t + z) * share, share, 1)
-    o_y, o_dx, o_qkv, o_out, o_gu, o_down = publish(o_y, o_dx, o_qkv, o_out, o_gu, o_down)
+    o_y, o_dx, o_qkv, o_out, o_gu, o_down, gain = publish(o_y, o_dx, o_qkv, o_out, o_gu, o_down, gain)
     return (
         o_y[None], o_dx[None], o_qkv[None], o_out[None], jnp.swapaxes(o_gu, 1, 2)[None], o_down[None],
         gain[None],

time: 462 us -> 459 us (level)
  the two profiles are of different devices: /device:TPU:8 before, /device:TPU:0 now
where the time goes in v5:
time: 459 us; the launch traced here: 451 us
  Pallas kernels  448 us (98%)
    pallas_call x1, Pallas kernels, layer(): pl.pallas_call(layer_kernel, out_shape=(shape(block), shape(block), shape...  443 us

profile of v5, /device:TPU:0, one launch (start us, length us, event | category | flops | bytes accessed | tf_op | source)
XLA Modules:
  0.0 450.7 jit_solution(16147672046312668457)
XLA Ops:
  0.6 0.7 convert_element_type.3
  1.3 0.7 broadcast_in_dim.27.lens
  2.0 443.5 %layer.1 = (bf16[2,256,1024]{2,1,0:T(8,128)(2,1)}, bf16[2,256,1024]{2,1,0:T(8,128)(2,1)}, bf16[3,256,256]{2,1,0:T(8,128)(2,1)}, bf16[256,256]{1,0:T(8,128)(2,1)}...) custom-call(bf16[2,256,1024]{2,1,0:T(8,128)(2,1)} %tok.1, ...), custom_call_target="tpu_custom_call" | custom-call | tf_op jit(solution)/shard_map/layer/pallas_call | solution.py:1138
  445.4 4.8 %publish.1 = (bf16[2,256,1024]{2,1,0:T(8,128)(2,1)}, f32[2,256,1024]{2,1,0:T(8,128)}, f32[3,256,256]{2,1,0:T(8,128)}, f32[256,256]{1,0:T(8,128)}, f32[2,704,256]...) custom-call(bf16[2,256,1024]{2,1,0:T(8,128)(2,1)} %get-tuple-element.21.refs_0_, ...), custom_call_target="tpu_custom_call" | custom-call | tf_op jit(solution)/shard_map/publish/pallas_call | solution.py:1191

commit v6 on v5

--- a/solution.py
+++ b/solution.py
@@ -568,7 +568,7 @@
         pl.when(second_plane)(remote(mine, mine, hsib.at[0, r], hsib.at[1, r], me.sibling).wait_send)
 
 
-LAG = 2
+LAG = 1
 AHEAD = 3
 FF, OUTS, HEADS = range(3)
 FF_PIECES = 6
@@ -952,8 +952,8 @@
                 finish_mixed(back(t - 1))
 
         ff_grads(0)
+        begin_reduce()
         finish_mixed(0)
-        begin_reduce()
         ff_grads(1)
         ff_grads(2)
 

time: 459 us -> 457 us (level)
  no operation moved by 1% of the time
where the time goes in v6:
time: 457 us; the launch traced here: 448 us
  Pallas kernels  446 us (98%)
    pallas_call x1, Pallas kernels, layer(): pl.pallas_call(layer_kernel, out_shape=(shape(block), shape(block), shape...  441 us

profile of v6, /device:TPU:0, one launch (start us, length us, event | category | flops | bytes accessed | tf_op | source)
XLA Modules:
  0.0 448.1 jit_solution(800060246950957223)
XLA Ops:
  0.6 0.7 convert_element_type.3
  1.3 0.7 broadcast_in_dim.27.lens
  2.0 440.9 %layer.1 = (bf16[2,256,1024]{2,1,0:T(8,128)(2,1)}, bf16[2,256,1024]{2,1,0:T(8,128)(2,1)}, bf16[3,256,256]{2,1,0:T(8,128)(2,1)}, bf16[256,256]{1,0:T(8,128)(2,1)}...) custom-call(bf16[2,256,1024]{2,1,0:T(8,128)(2,1)} %tok.1, ...), custom_call_target="tpu_custom_call" | custom-call | tf_op jit(solution)/shard_map/layer/pallas_call | solution.py:1138
  442.9 4.8 %publish.1 = (bf16[2,256,1024]{2,1,0:T(8,128)(2,1)}, f32[2,256,1024]{2,1,0:T(8,128)}, f32[3,256,256]{2,1,0:T(8,128)}, f32[256,256]{1,0:T(8,128)}, f32[2,704,256]...) custom-call(bf16[2,256,1024]{2,1,0:T(8,128)(2,1)} %get-tuple-element.21.refs_0_, ...), custom_call_target="tpu_custom_call" | custom-call | tf_op jit(solution)/shard_map/publish/pallas_call | solution.py:1191
